TPU v7x, 128 devices: a whole 4x4x4 slice. The times are simulated.
128 devices in a mesh: rep: 16 (over y, z_hi, core), shard: 8 (over x, z_lo).
Axes of the slice: x: 4, y: 4, z: 4 (z_hi: 2, z_lo: 2; z = z_hi * 2 + z_lo), core: 2. Of those that a mesh axis runs over, the one named last changes fastest.
Arguments:
- tokens: bfloat16 [16, 1536, 1280], P('rep', 'shard'), may hold values from -6 to 6
- lengths: int32 [16], P('rep'), may hold values from 1345 to 1500, as said below
- w_query: bfloat16 [1280, 1280], P('shard'), may hold values from -0.25 to 0.25
- w_key: bfloat16 [1280, 1280], P('shard'), may hold values from -0.25 to 0.25
- w_value: bfloat16 [1280, 1280], P('shard'), may hold values from -0.15625 to 0.15625
- w_out: bfloat16 [1280, 1280], P('shard'), may hold values from -0.625 to 0.625
- w_up: bfloat16 [1280, 5120], P('shard'), may hold values from -0.15625 to 0.15625
- w_down: bfloat16 [5120, 1280], P('shard'), may hold values from -0.078125 to 0.078125
- b_query: bfloat16 [1280], P('shard'), may hold values from -3 to 3
- b_value: bfloat16 [1280], P('shard'), may hold values from -3 to 3
- b_out: bfloat16 [1280], P('shard'), may hold values from -3 to 3
- b_up: bfloat16 [5120], P('shard'), may hold values from -3 to 3
- b_down: bfloat16 [1280], P('shard'), may hold values from -3 to 3
- gain_attn: bfloat16 [1280], P('shard'), may hold values from 0.25 to 1.75
- shift_attn: bfloat16 [1280], P('shard'), may hold values from -3 to 3
- gain_ffn: bfloat16 [1280], P('shard'), may hold values from 0.25 to 1.75
- shift_ffn: bfloat16 [1280], P('shard'), may hold values from -3 to 3
- cotangent: bfloat16 [16, 1536, 1280], P('rep', 'shard'), may hold values from -6 to 6
Outputs:
- output: bfloat16 [16, 1536, 1280], P('rep', 'shard')
- input_grad: float32 [16, 1536, 1280], P('rep', 'shard')
- grad_w_query: float32 [1280, 1280], P('shard')
- grad_w_key: float32 [1280, 1280], P('shard')
- grad_w_value: float32 [1280, 1280], P('shard')
- grad_w_out: float32 [1280, 1280], P('shard')
- grad_w_up: float32 [1280, 5120], P('shard')
- grad_w_down: float32 [5120, 1280], P('shard')
- grad_b_query: float32 [1280], P('shard')
- grad_b_value: float32 [1280], P('shard')
- grad_b_out: float32 [1280], P('shard')
- grad_b_up: float32 [5120], P('shard')
- grad_b_down: float32 [1280], P('shard')
- grad_gain_attn: float32 [1280], P('shard')
- grad_shift_attn: float32 [1280], P('shard')
- grad_gain_ffn: float32 [1280], P('shard')
- grad_shift_ffn: float32 [1280], P('shard')
Inputs may be any that keep to these rules, and one draw needn't show every extreme that they name: tokens of each clip, slots from lengths[c] on are padding; the longest clip has exactly 1500 tokens, and every clip, being the only one on its index of rep, has 1345 tokens or more.
All inputs are finite; a program needn't handle non-finite values.
Results may differ from a plain program's by a relative error of at most 0.02.
Values may be sent and summed in bfloat16 or wider, within the bound.
A program may use at most 448 MiB of HBM per device.

v0:
```python
import jax
import jax.numpy as jnp
from jax import lax
from jax.sharding import PartitionSpec as P

H = 16


def as_sent(x):
    return jax.tree.map(lambda a: a.astype(jnp.bfloat16) if a.dtype == jnp.float32 else a, x)


def norm_fwd(values, gain, shift):
    center = values - jnp.mean(values, axis=-1, keepdims=True)
    inverse = lax.rsqrt(jnp.mean(center * center, axis=-1, keepdims=True) + 1e-05)
    normed = center * inverse
    return (normed, inverse, normed * gain + shift)


def norm_back(grad_rows, normed, inverse, gain):
    scaled = grad_rows * gain
    grad_in = inverse * (
        scaled
        - jnp.mean(scaled, axis=-1, keepdims=True)
        - normed * jnp.mean(scaled * normed, axis=-1, keepdims=True)
    )
    return (grad_in, jnp.sum(grad_rows * normed, axis=0), jnp.sum(grad_rows, axis=0))


def gelu_slope(values):
    return (
        0.5 * (1.0 + lax.erf(values * 0.7071067811865476))
        + values * jnp.exp(-0.5 * values * values) * 0.3989422804014327
    )


def clip_scores(queries, keys_all, length):
    head_size = queries.shape[-1]
    raw = jnp.einsum(
        "thd,shd->hts", queries, keys_all, preferred_element_type=jnp.float32
    ) * head_size ** (-0.5)
    valid = jnp.arange(keys_all.shape[0]) < length
    return jnp.where(valid[None, None, :], raw, -1e30)


def forward(tokens, lengths, shards):
    gathered = (
        lax.all_gather(shards[0], "shard", axis=0, tiled=True),
        lax.all_gather(shards[1], "shard", axis=0, tiled=True),
        lax.all_gather(shards[2], "shard", axis=0, tiled=True),
        lax.all_gather(shards[3], "shard", axis=0, tiled=True),
        lax.all_gather(shards[4], "shard", axis=0, tiled=True),
        lax.all_gather(shards[5], "shard", axis=0, tiled=True),
        lax.all_gather(shards[6], "shard", axis=0, tiled=True),
        lax.all_gather(shards[7], "shard", axis=0, tiled=True),
        lax.all_gather(shards[8], "shard", axis=0, tiled=True),
        lax.all_gather(shards[9], "shard", axis=0, tiled=True),
        lax.all_gather(shards[10], "shard", axis=0, tiled=True),
        lax.all_gather(shards[11], "shard", axis=0, tiled=True),
        lax.all_gather(shards[12], "shard", axis=0, tiled=True),
        lax.all_gather(shards[13], "shard", axis=0, tiled=True),
        lax.all_gather(shards[14], "shard", axis=0, tiled=True),
    )
    (
        w_query,
        w_key,
        w_value,
        w_out,
        w_up,
        w_down,
        b_query,
        b_value,
        b_out,
        b_up,
        b_down,
        gain_attn,
        shift_attn,
        gain_ffn,
        shift_ffn,
    ) = gathered
    clip_count, local_len, width = tokens.shape
    head_size = width // H
    flat_rows = tokens.reshape(clip_count * local_len, width).astype(jnp.float32)
    normed_one, inverse_one, pre_one = norm_fwd(
        flat_rows, gain_attn.astype(jnp.float32), shift_attn.astype(jnp.float32)
    )
    first_in = pre_one.astype(jnp.bfloat16)
    queries = (jnp.dot(first_in, w_query, preferred_element_type=jnp.float32) + b_query).astype(
        jnp.bfloat16
    )
    key_rows = jnp.dot(first_in, w_key, preferred_element_type=jnp.float32).astype(jnp.bfloat16)
    value_rows = (jnp.dot(first_in, w_value, preferred_element_type=jnp.float32) + b_value).astype(
        jnp.bfloat16
    )
    keys_full, values_full = (
        lax.all_gather(key_rows.reshape(clip_count, local_len, width), "shard", axis=1, tiled=True),
        lax.all_gather(
            value_rows.reshape(clip_count, local_len, width), "shard", axis=1, tiled=True
        ),
    )
    slot_len = keys_full.shape[1]
    query_heads = queries.reshape(local_len, H, head_size)
    key_heads = keys_full[0].reshape(slot_len, H, head_size)
    value_heads = values_full[0].reshape(slot_len, H, head_size)
    scores = clip_scores(query_heads, key_heads, lengths[0])
    highest = jnp.max(scores, axis=-1, keepdims=True)
    expd = jnp.exp(scores - highest)
    totals = jnp.sum(expd, axis=-1, keepdims=True)
    probs = (expd / totals).astype(jnp.bfloat16)
    logsum_list = [highest + jnp.log(totals)]
    mixed_heads = jnp.einsum("hts,shd->thd", probs, value_heads, preferred_element_type=jnp.float32)
    attended_list = mixed_heads.reshape(local_len, width).astype(jnp.bfloat16)
    middle = flat_rows + jnp.dot(attended_list, w_out, preferred_element_type=jnp.float32) + b_out
    normed_two, inverse_two, pre_two = norm_fwd(
        middle, gain_ffn.astype(jnp.float32), shift_ffn.astype(jnp.float32)
    )
    second_in = pre_two.astype(jnp.bfloat16)
    hidden_pre = jnp.dot(second_in, w_up, preferred_element_type=jnp.float32) + b_up
    activated = jax.nn.gelu(hidden_pre, approximate=False).astype(jnp.bfloat16)
    result = middle + jnp.dot(activated, w_down, preferred_element_type=jnp.float32) + b_down
    return (
        gathered,
        normed_one,
        inverse_one,
        first_in,
        queries,
        keys_full,
        values_full,
        logsum_list,
        attended_list,
        normed_two,
        inverse_two,
        second_in,
        hidden_pre,
        activated,
        result,
    )


def reorder_rows(grad_array, group_size, replica_count):
    block_rows = grad_array.shape[0] // (group_size * replica_count)
    shaped = grad_array.reshape((group_size, replica_count, block_rows) + grad_array.shape[1:])
    return jnp.swapaxes(shaped, 0, 1).reshape(grad_array.shape)


def per_device(
    tokens,
    lengths,
    w_query,
    w_key,
    w_value,
    w_out,
    w_up,
    w_down,
    b_query,
    b_value,
    b_out,
    b_up,
    b_down,
    gain_attn,
    shift_attn,
    gain_ffn,
    shift_ffn,
    cotangent,
):
    shards = (
        w_query,
        w_key,
        w_value,
        w_out,
        w_up,
        w_down,
        b_query,
        b_value,
        b_out,
        b_up,
        b_down,
        gain_attn,
        shift_attn,
        gain_ffn,
        shift_ffn,
    )
    saved = forward(tokens, lengths, shards)
    clip_count, local_len, width = tokens.shape
    output = saved[14].astype(jnp.bfloat16).reshape(clip_count, local_len, width)
    again_tokens, again_shards = lax.optimization_barrier((tokens, shards))
    saved = forward(again_tokens, lengths, again_shards)
    (
        gathered,
        normed_one,
        inverse_one,
        first_in,
        queries,
        keys_full,
        values_full,
        logsum_list,
        attended,
        normed_two,
        inverse_two,
        second_in,
        hidden_pre,
        activated,
        result,
    ) = saved
    (
        full_query,
        full_key,
        full_value,
        full_out,
        full_up,
        full_down,
        full_bq,
        full_bv,
        full_bo,
        full_bu,
        full_bd,
        full_gain_attn,
        full_shift_attn,
        full_gain_ffn,
        full_shift_ffn,
    ) = gathered
    head_size = width // H
    slot_len = keys_full.shape[1]
    first_row = lax.axis_index("shard") * local_len
    position = first_row + jnp.arange(local_len)
    live_rows = (
        (position[None, :] < lengths[:, None])
        .astype(jnp.float32)
        .reshape(clip_count * local_len, 1)
    )
    grad_top = cotangent.reshape(clip_count * local_len, width).astype(jnp.float32) * live_rows
    grad_top_low = grad_top.astype(jnp.bfloat16)
    g_w_down = jnp.einsum("rf,rd->fd", activated, grad_top_low, preferred_element_type=jnp.float32)
    g_b_down = jnp.sum(grad_top, axis=0)
    grad_act = jnp.einsum("rd,fd->rf", grad_top_low, full_down, preferred_element_type=jnp.float32)
    grad_hidden = (grad_act * gelu_slope(hidden_pre)).astype(jnp.bfloat16)
    g_w_up = jnp.einsum("rd,rf->df", second_in, grad_hidden, preferred_element_type=jnp.float32)
    g_b_up = jnp.sum(grad_hidden.astype(jnp.float32), axis=0)
    grad_second = jnp.einsum("rf,df->rd", grad_hidden, full_up, preferred_element_type=jnp.float32)
    grad_mid_ln, g_gain_ffn, g_shift_ffn = norm_back(
        grad_second, normed_two, inverse_two, full_gain_ffn.astype(jnp.float32)
    )
    grad_middle = grad_top + grad_mid_ln
    grad_branch = grad_middle.astype(jnp.bfloat16)
    g_w_out = jnp.einsum("rd,re->de", attended, grad_branch, preferred_element_type=jnp.float32)
    g_b_out = jnp.sum(grad_branch.astype(jnp.float32), axis=0)
    grad_attended = jnp.einsum(
        "re,de->rd", grad_branch, full_out, preferred_element_type=jnp.float32
    ).astype(jnp.bfloat16)
    scale_factor = head_size ** (-0.5)
    query_heads = queries.reshape(local_len, H, head_size)
    key_heads = keys_full[0].reshape(slot_len, H, head_size)
    value_heads = values_full[0].reshape(slot_len, H, head_size)
    grad_heads = grad_attended.reshape(local_len, H, head_size)
    scores = clip_scores(query_heads, key_heads, lengths[0])
    probs = jnp.exp(scores - logsum_list[0])
    probs_low = probs.astype(jnp.bfloat16)
    value_part_list = [
        jnp.einsum(
            "hts,thd->shd", probs_low, grad_heads, preferred_element_type=jnp.float32
        ).reshape(slot_len, width)
    ]
    grad_probs = jnp.einsum(
        "thd,shd->hts", grad_heads, value_heads, preferred_element_type=jnp.float32
    )
    row_total = jnp.sum(probs * grad_probs, axis=-1, keepdims=True)
    grad_scores = (probs * (grad_probs - row_total)).astype(jnp.bfloat16)
    grad_q_heads = (
        jnp.einsum("hts,shd->thd", grad_scores, key_heads, preferred_element_type=jnp.float32)
        * scale_factor
    )
    grad_query_list = grad_q_heads.reshape(local_len, width).astype(jnp.bfloat16)
    key_part_list = [
        (
            jnp.einsum("hts,thd->shd", grad_scores, query_heads, preferred_element_type=jnp.float32)
            * scale_factor
        ).reshape(slot_len, width)
    ]
    key_sums, value_sums = (
        lax.psum_scatter(
            jnp.stack(key_part_list, axis=0).astype(jnp.bfloat16),
            "shard",
            scatter_dimension=1,
            tiled=True,
        ).astype(jnp.float32),
        lax.psum_scatter(
            jnp.stack(value_part_list, axis=0).astype(jnp.bfloat16),
            "shard",
            scatter_dimension=1,
            tiled=True,
        ).astype(jnp.float32),
    )
    grad_keys = key_sums.reshape(clip_count * local_len, width).astype(jnp.bfloat16)
    grad_values = value_sums.reshape(clip_count * local_len, width).astype(jnp.bfloat16)
    g_w_query = jnp.einsum(
        "rd,re->de", first_in, grad_query_list, preferred_element_type=jnp.float32
    )
    g_b_query = jnp.sum(grad_query_list.astype(jnp.float32), axis=0)
    g_w_key = jnp.einsum("rd,re->de", first_in, grad_keys, preferred_element_type=jnp.float32)
    g_w_value = jnp.einsum("rd,re->de", first_in, grad_values, preferred_element_type=jnp.float32)
    g_b_value = jnp.sum(grad_values.astype(jnp.float32), axis=0)
    grad_first = (
        jnp.einsum("re,de->rd", grad_query_list, full_query, preferred_element_type=jnp.float32)
        + jnp.einsum("re,de->rd", grad_keys, full_key, preferred_element_type=jnp.float32)
        + jnp.einsum("re,de->rd", grad_values, full_value, preferred_element_type=jnp.float32)
    )
    grad_in_ln, g_gain_attn, g_shift_attn = norm_back(
        grad_first, normed_one, inverse_one, full_gain_attn.astype(jnp.float32)
    )
    input_grad = (grad_middle + grad_in_ln).reshape(clip_count, local_len, width)
    partial_grads = (
        g_w_query,
        g_w_key,
        g_w_value,
        g_w_out,
        g_w_up,
        g_w_down,
        g_b_query,
        g_b_value,
        g_b_out,
        g_b_up,
        g_b_down,
        g_gain_attn,
        g_shift_attn,
        g_gain_ffn,
        g_shift_ffn,
    )
    group_size = lax.axis_size("shard")
    replica_count = lax.axis_size("rep")
    ordered = tuple((reorder_rows(item, group_size, replica_count) for item in partial_grads))
    owned = lax.psum_scatter(ordered, ("rep", "shard"), scatter_dimension=0, tiled=True)
    summed = jax.tree.map(
        lambda part, own: part.astype(own.dtype),
        lax.all_gather(as_sent(owned), "rep", axis=0, tiled=True),
        owned,
    )
    return (
        output,
        input_grad,
        summed[0],
        summed[1],
        summed[2],
        summed[3],
        summed[4],
        summed[5],
        summed[6],
        summed[7],
        summed[8],
        summed[9],
        summed[10],
        summed[11],
        summed[12],
        summed[13],
        summed[14],
    )


def solution(mesh):
    return jax.shard_map(
        per_device,
        mesh=mesh,
        in_specs=(
            P("rep", "shard", None),
            P("rep"),
            P("shard", None),
            P("shard", None),
            P("shard", None),
            P("shard", None),
            P("shard", None),
            P("shard", None),
            P("shard"),
            P("shard"),
            P("shard"),
            P("shard"),
            P("shard"),
            P("shard"),
            P("shard"),
            P("shard"),
            P("shard"),
            P("rep", "shard", None),
        ),
        out_specs=(
            P("rep", "shard", None),
            P("rep", "shard", None),
            P("shard", None),
            P("shard", None),
            P("shard", None),
            P("shard", None),
            P("shard", None),
            P("shard", None),
            P("shard"),
            P("shard"),
            P("shard"),
            P("shard"),
            P("shard"),
            P("shard"),
            P("shard"),
            P("shard"),
            P("shard"),
        ),
        check_vma=False,
    )
```

profile of v0, /device:TPU:0, one launch (start us, length us, event | category | flops | bytes accessed | tf_op | source)
XLA Modules:
  0.0 3125.3 jit_solution(1894243565604773265)
XLA Ops:
  25.2 36.4 %all-reduce.40 = (bf16[1280]{0:T(1024)(128)(2,1)S(1)}, bf16[1280]{0:T(1024)(128)(2,1)S(1)}, bf16[1280]{0:T(1024)(128)(2,1)S(1)}, bf16[1280]{0:T(1024)(128)(2,1)}...) all-reduce(bf16[1280]{0:T(1024)(128)(2,1)S(1)} %dynamic-update-slic, ...), channel_id=1, replica_groups=mesh['rep'=16,'shard'=8] {'shard'}, use_global_device_ids=true, to_apply=%add.2 | all-reduce | flops 19200 | bytes 76800
  64.1 23.1 all-gather.46.cloned.1.call-done
  91.1 71.6 %all-gather.42.cloned.1.call-done = bf16[1280,1280]{1,0:T(8,128)(2,1)} async-done(((bf16[160,1280]{1,0:T(8,128)(2,1)}), bf16[1280,1280]{1,0:T(8,128)(2,1)}) %all-gather.42.cloned.1.call-update) | async-done | bytes 3276816 | tf_op jit(solution)/shard_map/all_gather | solution.py:50
  169.7 68.3 %all-gather.30.cloned.1.call-done = bf16[1280,1280]{1,0:T(8,128)(2,1)} async-done(((bf16[160,1280]{1,0:T(8,128)(2,1)}), bf16[1280,1280]{1,0:T(8,128)(2,1)}) %all-gather.30.cloned.1.call-update) | async-done | bytes 3276816 | tf_op jit(solution)/shard_map/all_gather | solution.py:50
  242.3 29.9 all-gather.5
  272.2 41.1 %all-gather.44.cloned.1.call-done = bf16[1280,1280]{1,0:T(8,128)(2,1)} async-done(((bf16[160,1280]{1,0:T(8,128)(2,1)}), bf16[1280,1280]{1,0:T(8,128)(2,1)}) %all-gather.44.cloned.1.call-update) | async-done | bytes 3276816 | tf_op jit(solution)/shard_map/all_gather | solution.py:48
  316.4 72.0 %all-gather.34.cloned.1.call-done = bf16[1280,1280]{1,0:T(8,128)(2,1)} async-done(((bf16[160,1280]{1,0:T(8,128)(2,1)}), bf16[1280,1280]{1,0:T(8,128)(2,1)}) %all-gather.34.cloned.1.call-update) | async-done | bytes 3276816 | tf_op jit(solution)/shard_map/all_gather | solution.py:49
  392.2 84.1 %all-gather.62.cloned.1.call-done = bf16[1536,1280]{1,0:T(8,128)(2,1)} async-done(((bf16[192,1280]{1,0:T(8,128)(2,1)}), bf16[1536,1280]{1,0:T(8,128)(2,1)}) %all-gather.62.cloned.1.call-update) | async-done | bytes 3932176 | tf_op jit(solution)/shard_map/all_gather | solution.py:96
  503.2 61.2 %all-gather.60.cloned.1.call-done = bf16[1536,1280]{1,0:T(8,128)(2,1)} async-done(((bf16[192,1280]{1,0:T(8,128)(2,1)}), bf16[1536,1280]{1,0:T(8,128)(2,1)}) %all-gather.60.cloned.1.call-update) | async-done | bytes 3932176 | tf_op jit(solution)/shard_map/all_gather | solution.py:97
  580.3 59.4 %all-gather.48.cloned.1.call-done = bf16[1280,1280]{1,0:T(8,128)(2,1)} async-done(((bf16[160,1280]{1,0:T(8,128)(2,1)}), bf16[1280,1280]{1,0:T(8,128)(2,1)}) %all-gather.48.cloned.1.call-update) | async-done | bytes 3276816 | tf_op jit(solution)/shard_map/all_gather | solution.py:51
  642.8 256.3 %all-gather.52.cloned.1.call-done = bf16[1280,5120]{1,0:T(8,128)(2,1)} async-done(((bf16[160,5120]{1,0:T(8,128)(2,1)}), bf16[1280,5120]{1,0:T(8,128)(2,1)}) %all-gather.52.cloned.1.call-update) | async-done | bytes 13107216 | tf_op jit(solution)/shard_map/all_gather | solution.py:52
  899.1 15.8 fusion.25
  914.9 243.6 %all-gather.50.cloned.1.call-done = bf16[5120,1280]{1,0:T(8,128)(2,1)} async-done(((bf16[640,1280]{1,0:T(8,128)(2,1)}), bf16[5120,1280]{1,0:T(8,128)(2,1)}) %all-gather.50.cloned.1.call-update) | async-done | bytes 13107216 | tf_op jit(solution)/shard_map/all_gather | solution.py:53
  1184.6 14.2 multiply_reduce_fusion
  1198.8 13.1 multiply_convert_fusion
  1244.6 13.0 convolution_bitcast_fusion
  1257.7 19.1 copy.135
  1278.8 28.5 all-gather.4
  1328.4 81.8 %all-gather.58.cloned.1.call-done = bf16[1536,1280]{1,0:T(8,128)(2,1)} async-done(((bf16[192,1280]{1,0:T(8,128)(2,1)}), bf16[1536,1280]{1,0:T(8,128)(2,1)}) %all-gather.58.cloned.1.call-update) | async-done | bytes 3932176 | tf_op jit(solution)/shard_map/all_gather | solution.py:96
  1457.9 31.8 %reshape.327 = f32[8,16,10,5120]{3,2,1,0:T(8,128)} reshape(f32[1280,5120]{1,0:T(8,128)} %fusion.183) | data formatting | bytes 52428800 | tf_op jit(solution)/shard_map/reshape | solution.py:142
  1489.8 29.8 copy.133
  1519.6 34.3 %reshape.328 = f32[1280,5120]{1,0:T(8,128)} reshape(f32[16,8,10,5120]{3,2,1,0:T(8,128)} %copy.133) | data formatting | bytes 52428800 | tf_op jit(solution)/shard_map/reshape | solution.py:143
  1572.2 15.4 reduce-scatter.6.cloned.1.call-done
  1649.0 942.8 %all-reduce.42 = (bf16[1280,1280]{1,0:T(8,128)(2,1)}, bf16[1280,1280]{1,0:T(8,128)(2,1)}, bf16[1280,1280]{1,0:T(8,128)(2,1)}, bf16[1280,1280]{1,0:T(8,128)(2,1)}...) all-reduce(f32[1280,1280]{1,0:T(8,128)} %reshape.323, ...), channel_id=8, replica_groups=mesh['rep'=16,'shard'=8] {'rep','shard'}, use_global_device_ids=true, to_apply=%region_19.20.clone | all-reduce | flops 13122560 | bytes 78735360
  2609.6 76.8 %all-gather.40.cloned.1.call-done = bf16[5120,1280]{1,0:T(8,128)(2,1)} async-done(((bf16[640,1280]{1,0:T(8,128)(2,1)}), bf16[5120,1280]{1,0:T(8,128)(2,1)}) %all-gather.40.cloned.1.call-update) | async-done | bytes 13107216 | tf_op jit(solution)/shard_map/all_gather | solution.py:53
  2686.4 258.5 %all-gather.38.cloned.1.call-done = bf16[1280,5120]{1,0:T(8,128)(2,1)} async-done(((bf16[160,5120]{1,0:T(8,128)(2,1)}), bf16[1280,5120]{1,0:T(8,128)(2,1)}) %all-gather.38.cloned.1.call-update) | async-done | bytes 13107216 | tf_op jit(solution)/shard_map/all_gather | solution.py:52
  2944.9 18.2 fusion.56
  2964.0 26.1 all-gather.6
  2992.0 21.3 all-gather.7
  3015.1 25.3 all-gather.8
  3042.3 21.1 all-gather.9
  3067.1 36.7 %all-reduce.39 = (bf16[160]{0:T(256)(128)(2,1)S(1)}, bf16[160]{0:T(256)(128)(2,1)S(1)}, bf16[160]{0:T(256)(128)(2,1)S(1)}, bf16[640]{0:T(1024)(128)(2,1)S(1)}, b...) all-reduce(bf16[160]{0:T(256)(128)(2,1)S(1)} %dynamic-update-slice., ...), channel_id=1, replica_groups=mesh['rep'=16,'shard'=8] {'rep'}, use_global_device_ids=true, to_apply=%add.15 | all-reduce | flops 1920 | bytes 7680
  (361 shorter events, 336.2 us)
Async XLA Ops:
  7.2 80.1 %all-gather.46.cloned.1.call-start = ((), (), s32[]{:S(2)}) async-start(), calls=%async_computation.11 | async-start | bytes 3686400 | tf_op jit(solution)/shard_map/all_gather | solution.py:49
  7.9 154.7 %all-gather.42.cloned.1.call-start = ((), (), s32[]{:S(2)}) async-start(), calls=%async_computation.9 | async-start | bytes 3686400 | tf_op jit(solution)/shard_map/all_gather | solution.py:50
  8.7 229.2 %all-gather.30.cloned.1.call-start = ((), (), s32[]{:S(2)}) async-start(), calls=%async_computation.3 | async-start | bytes 3686400 | tf_op jit(solution)/shard_map/all_gather | solution.py:50
  9.4 303.9 %all-gather.44.cloned.1.call-start = ((), (), s32[]{:S(2)}) async-start(), calls=%async_computation.10 | async-start | bytes 3686400 | tf_op jit(solution)/shard_map/all_gather | solution.py:48
  10.0 378.3 %all-gather.34.cloned.1.call-start = ((), (), s32[]{:S(2)}) async-start(), calls=%async_computation.5 | async-start | bytes 3686400 | tf_op jit(solution)/shard_map/all_gather | solution.py:49
  10.6 465.7 %all-gather.62.cloned.1.call-start = ((), (), s32[]{:S(2)}) async-start(), calls=%async_computation.22 | async-start | bytes 4423680 | tf_op jit(solution)/shard_map/all_gather | solution.py:96
  61.6 251.7 %copy-start.21 = (f32[1280]{0:T(1024)}, f32[1280]{0:T(1024)S(1)}, u32[]{:S(2)}) copy-start(f32[1280]{0:T(1024)S(1)} %convert_element_type.359) | copy-start | bytes 15364
  61.6 251.7 %copy-start.14 = (f32[1280]{0:T(1024)}, f32[1280]{0:T(1024)S(1)}, u32[]{:S(2)}) copy-start(f32[1280]{0:T(1024)S(1)} %convert_element_type.358) | copy-start | bytes 15364
  62.8 250.5 %copy-start.28 = (f32[192]{0:T(256)}, f32[192]{0:T(256)S(1)}, u32[]{:S(2)}) copy-start(f32[192]{0:T(256)S(1)} %broadcast_multiply_fusion.5) | copy-start | bytes 2308
  64.1 249.2 %copy-start.30 = (f32[192]{0:T(256)}, f32[192]{0:T(256)S(1)}, u32[]{:S(2)}) copy-start(f32[192]{0:T(256)S(1)} %add_rsqrt_fusion.1) | copy-start | bytes 2308
  91.0 473.4 %all-gather.60.cloned.1.call-start = ((), (), s32[]{:S(2)}) async-start(), calls=%async_computation.21 | async-start | bytes 4423680 | tf_op jit(solution)/shard_map/all_gather | solution.py:97
  166.3 473.4 %all-gather.48.cloned.1.call-start = ((), (), s32[]{:S(2)}) async-start(), calls=%async_computation.12 | async-start | bytes 3686400 | tf_op jit(solution)/shard_map/all_gather | solution.py:51
  167.0 732.1 %all-gather.52.cloned.1.call-start = ((), (), s32[]{:S(2)}) async-start(), calls=%async_computation.14 | async-start | bytes 14745600 | tf_op jit(solution)/shard_map/all_gather | solution.py:52
  167.8 990.8 %all-gather.50.cloned.1.call-start = ((), (), s32[]{:S(2)}) async-start(), calls=%async_computation.13 | async-start | bytes 14745600 | tf_op jit(solution)/shard_map/all_gather | solution.py:53
  168.4 1143.3 %all-gather.32.cloned.1.call-start = ((), (), s32[]{:S(2)}) async-start(), calls=%async_computation.4 | async-start | bytes 3686400 | tf_op jit(solution)/shard_map/all_gather | solution.py:48
  169.1 1153.1 %all-gather.56.cloned.1.call-start = ((), (), s32[]{:S(2)}) async-start(), calls=%async_computation.19 | async-start | bytes 4423680 | tf_op jit(solution)/shard_map/all_gather | solution.py:97
  241.5 1168.7 %all-gather.58.cloned.1.call-start = ((), (), s32[]{:S(2)}) async-start(), calls=%async_computation.20 | async-start | bytes 4423680 | tf_op jit(solution)/shard_map/all_gather | solution.py:96
  392.0 1176.8 %reduce-scatter.4.cloned.1.call-start = ((), (), s32[]{:S(2)}) async-start(), calls=%async_computation.15 | async-start | bytes 4423680 | tf_op jit(solution)/shard_map/reduce_scatter | solution.py:280
  580.3 334.7 %copy-start.8 = (bf16[16,80,192]{2,1,0:T(8,128)(2,1)}, bf16[16,80,192]{2,1,0:T(8,128)(2,1)S(1)}, u32[]{:S(2)}) copy-start(bf16[16,80,192]{2,1,0:T(8,128)(2,1)S(1)} %fusion.92) | copy-start | bytes 1474564
  1179.6 249.3 %copy-start.2 = (f32[192,1280]{1,0:T(8,128)}, f32[192,1280]{1,0:T(8,128)S(1)}, u32[]{:S(2)}) copy-start(f32[192,1280]{1,0:T(8,128)S(1)} %get-tuple-element.94) | copy-start | bytes 2949124
  1223.0 364.6 %reduce-scatter.6.cloned.1.call-start = ((), (), s32[]{:S(2)}) async-start(), calls=%async_computation.16 | async-start | bytes 4423680 | tf_op jit(solution)/shard_map/reduce_scatter | solution.py:286
  1239.7 1365.0 %all-gather.36.cloned.1.call-start = ((), (), s32[]{:S(2)}) async-start(), calls=%async_computation.6 | async-start | bytes 3686400 | tf_op jit(solution)/shard_map/all_gather | solution.py:51
  1240.3 1367.6 %reduce-scatter.8.cloned.1.call-start = ((), (), s32[]{:S(2)}) async-start(), calls=%async_computation.17 | async-start | bytes 26419200 | tf_op jit(solution)/shard_map/reduce_scatter | solution.py:331
  1276.8 1409.6 %all-gather.40.cloned.1.call-start = ((), (), s32[]{:S(2)}) async-start(), calls=%async_computation.8 | async-start | bytes 14745600 | tf_op jit(solution)/shard_map/all_gather | solution.py:53
  1277.4 1667.5 %all-gather.38.cloned.1.call-start = ((), (), s32[]{:S(2)}) async-start(), calls=%async_computation.7 | async-start | bytes 14745600 | tf_op jit(solution)/shard_map/all_gather | solution.py:52
  1278.2 1832.2 %all-gather.64.cloned.1.call-start = ((), (), s32[]{:S(2)}) async-start(), calls=%async_computation.23 | async-start | bytes 2785280 | tf_op jit(solution)/shard_map/all_gather | solution.py:334
  1649.0 944.8 %copy-start.56 = (f32[16,192]{1,0:T(8,128)S(1)}, f32[16,192]{1,0:T(8,128)}, u32[]{:S(2)}) copy-start(f32[16,192]{1,0:T(8,128)} %get-tuple-element.97) | copy-start | bytes 36868
  2593.6 521.0 %all-gather.54.cloned.1.call-start = ((), (), s32[]{:S(2)}) async-start(), calls=%async_computation.18 | async-start | bytes 1740800 | tf_op jit(solution)/shard_map/all_gather | solution.py:334
  2604.7 340.2 %copy-start.24 = (f32[8,1,640]{2,1,0:T(1,128)S(1)}, f32[8,1,640]{2,1,0:T(1,128)}, u32[]{:S(2)}) copy-start(f32[8,1,640]{2,1,0:T(1,128)} %convert_element_type.431) | copy-start | bytes 61444
  2604.7 340.2 %copy-start.35 = (f32[1280]{0:T(1024)S(1)}, f32[1280]{0:T(1024)}, u32[]{:S(2)}) copy-start(f32[1280]{0:T(1024)} %convert_element_type.351) | copy-start | bytes 15364
  2604.7 340.2 %copy-start.36 = (f32[1280]{0:T(1024)S(1)}, f32[1280]{0:T(1024)}, u32[]{:S(2)}) copy-start(f32[1280]{0:T(1024)} %convert_element_type.347) | copy-start | bytes 15364
  2604.7 340.2 %copy-start.39 = (f32[1280]{0:T(1024)S(1)}, f32[1280]{0:T(1024)}, u32[]{:S(2)}) copy-start(f32[1280]{0:T(1024)} %convert_element_type.346) | copy-start | bytes 15364
  (46 other events, 2383.2 us)
Sparse Core Ops, SparseCore 0:
  9.7 77.5 all-gather.45
  88.9 73.7 all-gather.41
  164.3 73.5 all-gather.29
  239.4 73.8 all-gather.43
  314.8 73.4 all-gather.33
  390.4 85.8 all-gather.61
  478.5 85.8 all-gather.59
  566.0 73.5 all-gather.47
  641.3 257.7 all-gather.51
  900.6 257.8 all-gather.49
  1160.2 73.5 all-gather.31
  1235.9 86.2 all-gather.55
  1324.4 85.8 all-gather.57
  1412.5 86.3 reduce-scatter.3
  1501.2 86.3 reduce-scatter.5
  1589.0 73.5 all-gather.35
  1664.9 727.8 reduce-scatter.7
  2394.3 292.0 all-gather.39
  2688.0 256.8 all-gather.37
  2947.2 51.9 all-gather.63
  3001.5 46.5 all-gather.53
where the time goes:
time: 3140 us; the launch traced here: 3130 us
  waiting for transfers between devices  1430 us (46%)
  blocking collectives  1170 us (37%)
  local copies, waits for them, and re-layouts  268 us (9%)
  matrix products  201 us (6%)
  other arithmetic  42.5 us (1%)
    unnamed x3, blocking collectives  1020 us
    all_gather x2, waiting for transfers between devices, forward(): lax.all_gather(shards[4], 'shard', axis=0, tiled=True)  515 us
    all_gather x2, waiting for transfers between devices, forward(): lax.all_gather(shards[5], 'shard', axis=0, tiled=True)  320 us
    all_gather x2, waiting for transfers between devices, forward(): lax.all_gather(key_rows.reshape(clip_count, local_len, width), 'shard', a...  166 us
    all_gather x2, waiting for transfers between devices, forward(): lax.all_gather(shards[2], 'shard', axis=0, tiled=True)  140 us
    all_gather x2, waiting for transfers between devices, forward(): lax.all_gather(shards[1], 'shard', axis=0, tiled=True)  95.1 us
    all_gather x4, blocking collectives, per_device(): lax.all_gather(as_sent(owned), 'rep', axis=0, tiled=True)  93.9 us
    transpose x15, local copies, waits for them, and re-layouts, reorder_rows(): return jnp.swapaxes(shaped, 0, 1).reshape(grad_array.shape)  80.7 us
  transfers between devices with their start and end apart: 21, of which 15 were waited for; matrix products, arithmetic and copies ran while one was open for 16% of the time, Pallas kernels for 0%

commit v1 on v0

v1 whole, which is shorter than its diff:
```python
import functools

import jax
import jax.numpy as jnp
from jax import lax
from jax.experimental import pallas as pl
from jax.experimental.pallas import tpu as pltpu
from jax.sharding import PartitionSpec as P

H = 16
HD = 80
EPS = 1e-05
AXES = ("rep", "shard")
F32 = jnp.float32
BF16 = jnp.bfloat16
NT = (((1,), (1,)), ((), ()))
TN = (((0,), (0,)), ((), ()))


def flat_index(y, zh, c, x, zl):
    return ((y % 4) * 4 + (zh % 2) * 2 + c % 2) * 8 + (x % 4) * 2 + zl % 2


def pairs(move):
    found = []
    for y in range(4):
        for zh in range(2):
            for c in range(2):
                for x in range(4):
                    for zl in range(2):
                        here = flat_index(y, zh, c, x, zl)
                        found.append((here, flat_index(*move(y, zh, c, x, zl))))
    return found


def send(value, move):
    return lax.ppermute(value, AXES, pairs(move))


def along_x(value, dx):
    return send(value, lambda y, zh, c, x, zl: (y, zh, c, x + dx, zl))


def along_y(value, dy):
    return send(value, lambda y, zh, c, x, zl: (y + dy, zh, c, x, zl))


def along_z(value, dz):
    def move(y, zh, c, x, zl):
        z = (2 * zh + zl + dz) % 4
        return (y, z // 2, c, x, z % 2)

    return send(value, move)


def to_sibling(value):
    return send(value, lambda y, zh, c, x, zl: (y, zh, c + 1, x, zl))


def cross(value):
    return send(value, lambda y, zh, c, x, zl: (y, zh, zl, x, c))


def gather_group(own):
    near = [own] + [along_x(own, dx) for dx in (1, 2, 3)]
    return [[block, to_sibling(block)] for block in near]


def scatter_group(parts):
    total = None
    for dx in (2, 1, 3, 0):
        both = parts[dx][0].astype(F32) + to_sibling(parts[dx][1]).astype(F32)
        if dx > 0:
            both = along_x(both.astype(BF16), -dx).astype(F32)
        total = both if total is None else total + both
    return total


def sum_four(value, along):
    one, two, three = (along(value, step).astype(F32) for step in (1, 2, 3))
    return (value.astype(F32) + two) + (one + three)


def place(blocks, indices):
    held = jnp.zeros((len(blocks),) + blocks[0].shape, blocks[0].dtype)
    for block, index in zip(blocks, indices):
        held = lax.dynamic_update_index_in_dim(held, block, index, 0)
    return held


def pick(array, index, axis=0):
    return lax.dynamic_index_in_dim(array, index, axis, keepdims=False)


def norm_fwd(values, gain, shift):
    center = values - jnp.mean(values, axis=-1, keepdims=True)
    inverse = lax.rsqrt(jnp.mean(center * center, axis=-1, keepdims=True) + EPS)
    normed = center * inverse
    return (normed, inverse, normed * gain + shift)


def norm_back(grad_rows, normed, inverse, gain):
    scaled = grad_rows * gain
    grad_in = inverse * (
        scaled
        - jnp.mean(scaled, axis=-1, keepdims=True)
        - normed * jnp.mean(scaled * normed, axis=-1, keepdims=True)
    )
    return (grad_in, jnp.sum(grad_rows * normed, axis=0), jnp.sum(grad_rows, axis=0))


def attend_kernel(scale, queries, everything, mask, mixed, probs, keys, values):
    @pl.when(pl.program_id(0) == 0)
    def _():
        for h in range(2):
            keys[h] = everything[:, 160 + h * HD : 160 + (h + 1) * HD]
            values[h] = everything[:, 320 + h * HD : 320 + (h + 1) * HD]

    for h in range(2):
        mine = queries[:, h * HD : (h + 1) * HD]
        scores = lax.dot_general(mine, keys[h], NT, preferred_element_type=F32) * scale
        scores = scores + mask[...]
        top = jnp.max(scores, axis=-1, keepdims=True)
        risen = jnp.exp(scores - top)
        share = 1.0 / jnp.sum(risen, axis=-1, keepdims=True)
        low = (risen * share).astype(BF16)
        probs[h] = low
        mixed[:, h * HD : (h + 1) * HD] = jnp.dot(
            low, values[h], preferred_element_type=F32
        ).astype(BF16)


def attend(qkv, mask, tile):
    rows = qkv.shape[0]
    return pl.pallas_call(
        functools.partial(attend_kernel, HD**-0.5),
        grid=(rows // tile,),
        in_specs=[
            pl.BlockSpec((tile, 480), lambda i: (i, 0)),
            pl.BlockSpec((rows, 480), lambda i: (0, 0)),
            pl.BlockSpec((1, rows), lambda i: (0, 0)),
        ],
        out_specs=[
            pl.BlockSpec((tile, 160), lambda i: (i, 0)),
            pl.BlockSpec((2, tile, rows), lambda i: (0, i, 0)),
        ],
        out_shape=[
            jax.ShapeDtypeStruct((rows, 160), BF16),
            jax.ShapeDtypeStruct((2, rows, rows), BF16),
        ],
        scratch_shapes=[pltpu.VMEM((2, rows, HD), BF16), pltpu.VMEM((2, rows, HD), BF16)],
        compiler_params=pltpu.CompilerParams(vmem_limit_bytes=48 << 20),
        cost_estimate=pl.CostEstimate(
            flops=8 * rows * rows * 256, bytes_accessed=16 << 20, transcendentals=2 * rows * rows
        ),
    )(qkv, qkv, mask)


def attend_back_kernel(
    scale, queries, everything, probs, mixed, grad_mixed, grads, keys, values, sum_k, sum_v
):
    step = pl.program_id(0)
    tile = queries.shape[0]

    @pl.when(step == 0)
    def _():
        for h in range(2):
            keys[h] = everything[:, 160 + h * HD : 160 + (h + 1) * HD]
            values[h] = everything[:, 320 + h * HD : 320 + (h + 1) * HD]
        sum_k[...] = jnp.zeros_like(sum_k)
        sum_v[...] = jnp.zeros_like(sum_v)

    here = pl.ds(pl.multiple_of(step * tile, tile), tile)
    for h in range(2):
        cols = slice(h * HD, (h + 1) * HD)
        mine, back, low = queries[:, cols], grad_mixed[:, cols], probs[h]
        row_total = jnp.sum(
            back.astype(F32) * mixed[:, cols].astype(F32), axis=-1, keepdims=True
        )
        grad_probs = lax.dot_general(back, values[h], NT, preferred_element_type=F32)
        grad_scores = (low.astype(F32) * (grad_probs - row_total)).astype(BF16)
        sum_v[h] += lax.dot_general(low, back, TN, preferred_element_type=F32)
        sum_k[h] += lax.dot_general(grad_scores, mine, TN, preferred_element_type=F32)
        grad_q = jnp.dot(grad_scores, keys[h], preferred_element_type=F32) * scale
        grads[here, cols] = grad_q.astype(BF16)

    @pl.when(step == pl.num_programs(0) - 1)
    def _():
        for h in range(2):
            grads[:, 160 + h * HD : 160 + (h + 1) * HD] = (sum_k[h] * scale).astype(BF16)
            grads[:, 320 + h * HD : 320 + (h + 1) * HD] = sum_v[h].astype(BF16)


def attend_back(qkv, probs, mixed, grad_mixed, tile):
    rows = qkv.shape[0]
    return pl.pallas_call(
        functools.partial(attend_back_kernel, HD**-0.5),
        grid=(rows // tile,),
        in_specs=[
            pl.BlockSpec((tile, 480), lambda i: (i, 0)),
            pl.BlockSpec((rows, 480), lambda i: (0, 0)),
            pl.BlockSpec((2, tile, rows), lambda i: (0, i, 0)),
            pl.BlockSpec((tile, 160), lambda i: (i, 0)),
            pl.BlockSpec((tile, 160), lambda i: (i, 0)),
        ],
        out_specs=pl.BlockSpec((rows, 480), lambda i: (0, 0)),
        out_shape=jax.ShapeDtypeStruct((rows, 480), BF16),
        scratch_shapes=[
            pltpu.VMEM((2, rows, HD), BF16),
            pltpu.VMEM((2, rows, HD), BF16),
            pltpu.VMEM((2, rows, HD), F32),
            pltpu.VMEM((2, rows, HD), F32),
        ],
        compiler_params=pltpu.CompilerParams(vmem_limit_bytes=48 << 20),
        cost_estimate=pl.CostEstimate(
            flops=16 * rows * rows * 256, bytes_accessed=16 << 20, transcendentals=0
        ),
    )(qkv, qkv, probs, mixed, grad_mixed)


def dot(a, b):
    return jnp.dot(a, b, preferred_element_type=F32)


def dot_nt(a, b):
    return lax.dot_general(a, b, NT, preferred_element_type=F32)


def dot_tn(a, b):
    return lax.dot_general(a, b, TN, preferred_element_type=F32)


def rejoin_rows(part, y, c, zl):
    pieces = part.astype(BF16).reshape((4, part.shape[0] // 4) + part.shape[1:])
    total = pick(pieces, y).astype(F32)
    for dy in (2, 1, 3):
        total = total + along_y(pick(pieces, (y + dy) % 4), dy).astype(F32)
    total = sum_four(total.astype(BF16), along_z).astype(BF16)
    other = to_sibling(total)
    total = jnp.where(c == zl, total, other)
    blocks = [total] + [along_y(total, dy) for dy in (1, 2, 3)]
    held = place(blocks, [(y - dy) % 4 for dy in range(4)])
    return held.reshape((-1,) + held.shape[2:]).astype(F32)


def rejoin_columns(part, y, c, x, zl):
    depth = part.shape[0] // 32
    pieces = part.astype(BF16).reshape(8, 4, depth, part.shape[1])
    total = pick(pieces, y, 1).astype(F32)
    for dy in (2, 1, 3):
        total = total + along_y(pick(pieces, (y + dy) % 4, 1), dy).astype(F32)
    total = sum_four(total.astype(BF16), along_z).astype(BF16)
    near = [pick(total, 2 * x + zl)]
    near += [along_x(pick(total, 2 * ((x + dx) % 4) + zl), dx) for dx in (1, 2, 3)]
    near = jnp.stack(near)
    far = to_sibling(near)
    blocks, indices = [], []
    for dx in range(4):
        for dc, source in enumerate((near, far)):
            blocks.append(source[dx])
            indices.append(2 * ((x - dx) % 4) + (c ^ dc))
    whole = place(blocks, indices)
    blocks = [whole] + [along_y(whole, dy) for dy in (1, 2, 3)]
    return place(blocks, [(y - dy) % 4 for dy in range(4)])


def per_device(
    tokens,
    lengths,
    w_query,
    w_key,
    w_value,
    w_out,
    w_up,
    w_down,
    b_query,
    b_value,
    b_out,
    b_up,
    b_down,
    gain_attn,
    shift_attn,
    gain_ffn,
    shift_ffn,
    cotangent,
):
    rep, shard = lax.axis_index("rep"), lax.axis_index("shard")
    y, c, x, zl = rep // 4, rep % 2, shard // 2, shard % 2
    rows, width = tokens.shape[1:]

    own = cross(tokens[0])
    length = jnp.where(c == zl, lengths, to_sibling(lengths))[0]

    small = jnp.concatenate(
        [b_query, b_value, b_out, b_down, gain_attn, shift_attn, gain_ffn, shift_ffn, b_up]
    ).reshape(4, 480)
    cut = jnp.stack([w_query, w_key, w_value]).reshape(3, 160, 8, 160)
    cut = cut.transpose(2, 1, 0, 3).reshape(8, 160, 480)

    def spread(get):
        blocks, indices = [], []
        for dx in range(4):
            for dz in range(2):
                block = get(2 * ((x + dx) % 4) + c)
                if dx or dz:
                    block = send(
                        block,
                        lambda y, zh, c, x, zl, dx=dx, dz=dz: (y, zh, c, x + dx, zl + dz),
                    )
                blocks.append(block)
                indices.append(2 * ((x - dx) % 4) + (zl ^ dz))
        return place(blocks, indices)

    held = spread(lambda index: jnp.concatenate([pick(cut, index), small]))
    w_qkv = held[:, :160].reshape(width, 480)
    small = held[:, 160:].reshape(8, 1920)
    full = small[:, :1280].reshape(8, 8, 160).transpose(1, 0, 2).reshape(8, width).astype(F32)
    bias_out, bias_down, gain_one, shift_one, gain_two, shift_two = (full[k] for k in range(2, 8))
    me = 2 * x + c
    mine_small = pick(small, me).astype(F32)
    bias_qkv = jnp.concatenate([mine_small[:160], jnp.zeros((160,), F32), mine_small[160:320]])
    bias_up = mine_small[1280:]

    token_blocks = gather_group(own)

    def first_norm(block):
        return norm_fwd(block.astype(F32), gain_one, shift_one)

    first_in, qkv = [], []
    for dx in range(4):
        normed = first_norm(jnp.concatenate(token_blocks[dx]))[2].astype(BF16)
        first_in.append(normed)
        qkv.append((dot(normed, w_qkv) + bias_qkv).astype(BF16))
    first_in, qkv = jnp.concatenate(first_in), jnp.concatenate(qkv)

    starts = jnp.stack([2 * ((x - dx) % 4) + (c ^ dc) for dx in range(4) for dc in range(2)])
    position = (starts[:, None] * rows + jnp.arange(rows)[None, :]).reshape(1, 8 * rows)
    mask = jnp.where(position < length, 0.0, -1e30).astype(F32)
    live = (position < length).astype(F32).reshape(4, 2 * rows, 1)

    out_blocks = gather_group(cross(w_out))
    out_full = jnp.concatenate([block for both in out_blocks for block in both])
    up_mine = spread(
        lambda index: lax.dynamic_slice_in_dim(w_up, index * 640, 640, axis=1)
    ).reshape(width, 640)
    down_mine = cross(w_down)
    grad_blocks = gather_group(cross(cotangent[0]))
    grad_top = [
        (jnp.concatenate(grad_blocks[dx]).astype(F32) * live[dx]).astype(BF16) for dx in range(4)
    ]

    mixed, probs = attend(qkv, mask, 384)

    def exchange(blocks):
        got = [[None, None] for _ in range(4)]
        for dx in range(4):
            for dc in range(2):
                block = blocks[dx][dc]
                if dx or dc:
                    block = send(
                        block,
                        lambda y, zh, c, x, zl, dx=dx, dc=dc: (y, zh, c + dc, x - dx, zl),
                    )
                got[-dx % 4][dc] = block
        return got

    split = mixed.reshape(4, 2, rows, 160)
    attended = exchange([[split[dx, dc] for dc in range(2)] for dx in range(4)])
    attended = jnp.concatenate([block for both in attended for block in both], axis=1)
    middle = own.astype(F32) + dot(attended, out_full) + bias_out
    normed_two, inverse_two, second_own = norm_fwd(middle, gain_two, shift_two)
    second_blocks = gather_group(second_own.astype(BF16))

    second_in, active, grad_hidden, out_parts, second_parts = [], [], [], [], []
    for dx in range(4):
        block = jnp.concatenate(second_blocks[dx])
        hidden = dot(block, up_mine) + bias_up
        bell = 0.5 * (1.0 + lax.erf(hidden * 0.7071067811865476))
        act = (hidden * bell).astype(BF16)
        slope = bell + hidden * jnp.exp(-0.5 * hidden * hidden) * 0.3989422804014327
        grad_z = (dot_nt(grad_top[dx], down_mine) * slope).astype(BF16)
        second_in.append(block)
        active.append(act)
        grad_hidden.append(grad_z)
        second_parts.append(dot_nt(grad_z, up_mine).astype(BF16).reshape(2, rows, width))
        out_parts.append(dot(act, down_mine).astype(BF16).reshape(2, rows, width))
    grad_second = scatter_group(second_parts)
    result = scatter_group(out_parts)
    output = cross((middle + result + bias_down).astype(BF16))

    grad_hidden = jnp.concatenate(grad_hidden)
    g_w_up = dot_tn(jnp.concatenate(second_in), grad_hidden)
    g_w_down = dot_tn(jnp.concatenate(active), jnp.concatenate(grad_top))
    g_b_up = jnp.sum(grad_hidden.astype(F32), axis=0)

    top_own = grad_top[0][:rows].astype(F32)
    grad_ln, g_gain_ffn, g_shift_ffn = norm_back(grad_second, normed_two, inverse_two, gain_two)
    grad_middle = top_own + grad_ln
    branch = grad_middle.astype(BF16)
    grad_attended = dot_nt(branch, out_full).astype(BF16)
    back = exchange(
        [
            [grad_attended[:, (2 * dx + dc) * 160 : (2 * dx + dc + 1) * 160] for dc in range(2)]
            for dx in range(4)
        ]
    )
    grad_mixed = jnp.concatenate([block for both in back for block in both])
    grad_qkv = attend_back(qkv, probs, mixed, grad_mixed, 384)

    branch_blocks = gather_group(branch)
    branch_all = jnp.concatenate([block for both in branch_blocks for block in both])
    g_w_out = dot_tn(mixed, branch_all)

    first_parts = []
    for dx in range(4):
        part = dot_nt(grad_qkv[2 * rows * dx : 2 * rows * (dx + 1)], w_qkv)
        first_parts.append(part.astype(BF16).reshape(2, rows, width))
    grad_first = scatter_group(first_parts)
    g_w_qkv = dot_tn(first_in, grad_qkv)
    sums = jnp.sum(grad_qkv.astype(F32), axis=0)
    normed_one, inverse_one, _ = first_norm(own)
    grad_ln, g_gain_attn, g_shift_attn = norm_back(grad_first, normed_one, inverse_one, gain_one)
    input_grad = cross(grad_middle + grad_ln)

    grad_down = rejoin_rows(g_w_down, y, c, zl)
    grad_out = rejoin_rows(g_w_out, y, c, zl)
    grad_up = rejoin_columns(g_w_up, y, c, x, zl)
    grad_up = grad_up.transpose(0, 2, 1, 3).reshape(160, 5120).astype(F32)
    three = rejoin_columns(g_w_qkv, y, c, x, zl).reshape(4, 8, 40, 3, 160)
    three = three.transpose(3, 0, 2, 1, 4).reshape(3, 160, width).astype(F32)

    vectors = jnp.stack(
        [
            jnp.sum(branch.astype(F32), axis=0),
            jnp.sum(top_own, axis=0),
            g_gain_attn,
            g_shift_attn,
            g_gain_ffn,
            g_shift_ffn,
        ]
    )
    vectors = vectors + to_sibling(vectors)
    vectors = sum_four(vectors, along_x)
    sliced = jnp.concatenate([sums[:160], sums[320:], g_b_up])
    packed = jnp.concatenate([vectors.reshape(-1), sliced])
    packed = sum_four(packed, along_y)
    packed = sum_four(packed, along_z)
    sliced = packed[6 * width :]
    sliced = jnp.where(c == zl, sliced, to_sibling(sliced))
    vectors = lax.dynamic_slice_in_dim(packed[: 6 * width].reshape(6, width), shard * 160, 160, 1)
    return (
        output[None],
        input_grad[None],
        three[0],
        three[1],
        three[2],
        grad_out,
        grad_up,
        grad_down,
        sliced[:160],
        sliced[160:320],
        vectors[0],
        sliced[320:],
        vectors[1],
        vectors[2],
        vectors[3],
        vectors[4],
        vectors[5],
    )


def solution(mesh):
    by_clip, matrix, vector = P("rep", "shard", None), P("shard", None), P("shard")
    return jax.shard_map(
        per_device,
        mesh=mesh,
        in_specs=(by_clip, P("rep")) + (matrix,) * 6 + (vector,) * 9 + (by_clip,),
        out_specs=(by_clip, by_clip) + (matrix,) * 6 + (vector,) * 9,
        check_vma=False,
    )
```

time: 3140 us -> 705 us (0.22)
  waiting for transfers between devices: 1430 us -> 252 us
  blocking collectives: 1170 us -> 0 us
  starting transfers between devices: 1.29 us -> 197 us
  matrix products: 201 us -> 49.5 us
  local copies, waits for them, and re-layouts: 268 us -> 119 us
    all_gather x18 -> x0, waiting for transfers between devices: 1400 us -> none  [the longest x2 515 us: forward(): lax.all_gather(shards[4], 'shard', axis=0, tiled=True)]
    unnamed x3 -> x0, blocking collectives: 1020 us -> none
    ppermute x0 -> x148, waiting for transfers between devices: none -> 252 us  [send(): return lax.ppermute(value, AXES, pairs(move))]
    ppermute x0 -> x148, starting transfers between devices: none -> 197 us  [send(): return lax.ppermute(value, AXES, pairs(move))]
    all_gather x6 -> x0, blocking collectives: 152 us -> none  [the longest x4 93.9 us: per_device(): lax.all_gather(as_sent(owned), 'rep', axis=0, tiled=True)]
    dot_general x29 -> x30, matrix products: 189 us -> 49.5 us  [the longest x13 19.7 us: dot_nt(): return lax.dot_general(a, b, NT, preferred_element_type=F32)]
    reshape x24 -> x4, local copies, waits for them, and re-layouts: 107 us -> 0.21 us  [the longest x1 0.11 us: per_device(): small = held[:, 160:].reshape(8, 1920)]
    transpose x15 -> x0, local copies, waits for them, and re-layouts: 80.7 us -> none  [reorder_rows(): return jnp.swapaxes(shaped, 0, 1).reshape(grad_array.shape)]
  transfers between devices with their start and end apart: 21 -> 148, of which waited for: 15 -> 45; matrix products, arithmetic and copies ran while one was open for 16% -> 26% of each run, Pallas kernels for 0% -> 4%
where the time goes in v1:
time: 705 us; the launch traced here: 693 us
  waiting for transfers between devices  252 us (36%)
  starting transfers between devices  197 us (28%)
  local copies, waits for them, and re-layouts  119 us (17%)
  matrix products  49.5 us (7%)
  other arithmetic  39.7 us (6%)
  Pallas kernels  30.3 us (4%)
    ppermute x148, waiting for transfers between devices, send(): return lax.ppermute(value, AXES, pairs(move))  252 us
    ppermute x148, starting transfers between devices, send(): return lax.ppermute(value, AXES, pairs(move))  197 us
    dynamic_update_slice x44, local copies, waits for them, and re-layouts, place(): held = lax.dynamic_update_index_in_dim(held, block, index, 0)  39.7 us
    dot_general x13, matrix products, dot_nt(): return lax.dot_general(a, b, NT, preferred_element_type=F32)  19.7 us
    dot_general x13, matrix products, dot(): return jnp.dot(a, b, preferred_element_type=F32)  19.2 us
    unnamed x175, local copies, waits for them, and re-layouts  18.3 us
    pallas_call x1, Pallas kernels, attend_back(): pl.pallas_call(functools.partial(attend_back_kernel, HD ** (-0.5)), grid=...  16 us
    pallas_call x1, Pallas kernels, attend(): pl.pallas_call(functools.partial(attend_kernel, HD ** (-0.5)), grid=(rows...  14.3 us
  transfers between devices with their start and end apart: 148, of which 45 were waited for; matrix products, arithmetic and copies ran while one was open for 26% of the time, Pallas kernels for 4%

profile of v1, /device:TPU:0, one launch (start us, length us, event | category | flops | bytes accessed | tf_op | source)
XLA Modules:
  0.0 692.6 jit_solution(7245423426637500332)
XLA Ops:
  0.8 6.1 concatenate.98
  25.6 7.4 %collective-permute-done.2 = bf16[164,480]{1,0:T(8,128)(2,1)S(1)} collective-permute-done((bf16[164,480]{1,0:T(8,128)(2,1)}, bf16[164,480]{1,0:T(8,128)(2,1)S(1)}, u32[]{:S(2)}, u32[]{:S(2)}) %collective-permute-start.2) | collective-permute-done | bytes 157472 | tf_op jit(solution)/shard_map/ppermute | solution.py:37
  68.8 8.5 %collective-permute-start.24 = (bf16[160,1280]{1,0:T(8,128)(2,1)S(1)}, bf16[160,1280]{1,0:T(8,128)(2,1)S(1)}, u32[]{:S(2)}, u32[]{:S(2)}) collective-permute-start(bf16[160,1280]{1,0:T(8,128)(2,1)S(1)} %collective-permute-done.23), channel_id=1, source_target_pairs={{0,8},{1,9},{2,10},{3,11},{4,12},{5,13},{6,14},{7,15},{8,0},{9,1},... | collective-permute-start | bytes 1228808 | tf_op jit(solution)/shard_map/ppermute | solution.py:37
  84.4 5.4 collective-permute-done.25
  100.7 10.4 %collective-permute-done.9 = bf16[192,1280]{1,0:T(8,128)(2,1)S(1)} collective-permute-done((bf16[192,1280]{1,0:T(8,128)(2,1)S(1)}, bf16[192,1280]{1,0:T(8,128)(2,1)S(1)}, u32[]{:S(2)}, u32[]{:S(2)}) %collective-permute-start.9) | collective-permute-done | bytes 491552 | tf_op jit(solution)/shard_map/ppermute | solution.py:37
  116.0 5.8 collective-permute-done.11
  124.1 8.1 %collective-permute-done.64 = bf16[192,1280]{1,0:T(8,128)(2,1)S(1)} collective-permute-done((bf16[192,1280]{1,0:T(8,128)(2,1)S(1)}, bf16[192,1280]{1,0:T(8,128)(2,1)S(1)}, u32[]{:S(2)}, u32[]{:S(2)}) %collective-permute-start.64) | collective-permute-done | bytes 491552 | tf_op jit(solution)/shard_map/ppermute | solution.py:37
  140.7 14.3 %shard_map.305 = (bf16[1536,160]{1,0:T(8,128)(2,1)S(1)}, bf16[2,1536,1536]{2,1,0:T(8,128)(2,1)}) custom-call(bf16[1536,480]{1,0:T(8,128)(2,1)S(1)} %pad_maximum_fusion.2.queries.everything, bf16[1536,480]{1,0:T(8,128)(2,1)S(1)} %pad_maximum_fusion.2.queries.everything, f32[1,1536]{1,0:T(1,128)S(1)} %select_n.470.mask), custom_call_target="tpu_custom_call" | custom-call | flops 4831838208 | bytes 16777216 | tf_op jit(solution)/shard_map/pallas_call | solution.py:135
  165.4 13.9 %collective-permute-start.40 = (bf16[640,1280]{1,0:T(8,128)(2,1)}, bf16[640,1280]{1,0:T(8,128)(2,1)}, u32[]{:S(2)}, u32[]{:S(2)}) collective-permute-start(bf16[640,1280]{1,0:T(8,128)(2,1)} %param.25), channel_id=1, source_target_pairs={{0,0},{1,8},{2,2},{3,10},{4,4},{5,12},{6,6},{7,14},{8,1},{9,9},{10... | collective-permute-start | bytes 4915208 | tf_op jit(solution)/shard_map/ppermute | solution.py:37
  192.9 7.8 %collective-permute-done.47 = bf16[192,1280]{1,0:T(8,128)(2,1)S(1)} collective-permute-done((bf16[192,1280]{1,0:T(8,128)(2,1)S(1)}, bf16[192,1280]{1,0:T(8,128)(2,1)S(1)}, u32[]{:S(2)}, u32[]{:S(2)}) %collective-permute-start.47) | collective-permute-done | bytes 491552 | tf_op jit(solution)/shard_map/ppermute | solution.py:37
  209.8 6.2 collective-permute-done.43
  255.0 15.0 %collective-permute-done.115 = bf16[8,40,640]{2,1,0:T(8,128)(2,1)S(1)} collective-permute-done((bf16[8,40,640]{2,1,0:T(8,128)(2,1)S(1)}, bf16[8,40,640]{2,1,0:T(8,128)(2,1)S(1)}, u32[]{:S(2)}, u32[]{:S(2)}) %collective-permute-start.115) | collective-permute-done | bytes 409632 | tf_op jit(solution)/shard_map/ppermute | solution.py:37
  271.0 15.4 %collective-permute-done.128 = bf16[160,1280]{1,0:T(8,128)(2,1)S(1)} collective-permute-done((bf16[160,1280]{1,0:T(8,128)(2,1)S(1)}, bf16[160,1280]{1,0:T(8,128)(2,1)S(1)}, u32[]{:S(2)}, u32[]{:S(2)}) %collective-permute-start.128) | collective-permute-done | bytes 409632 | tf_op jit(solution)/shard_map/ppermute | solution.py:37
  298.0 11.4 %collective-permute-done.119 = bf16[8,40,640]{2,1,0:T(8,128)(2,1)S(1)} collective-permute-done((bf16[8,40,640]{2,1,0:T(8,128)(2,1)S(1)}, bf16[8,40,640]{2,1,0:T(8,128)(2,1)S(1)}, u32[]{:S(2)}, u32[]{:S(2)}) %collective-permute-start.119) | collective-permute-done | bytes 409632 | tf_op jit(solution)/shard_map/ppermute | solution.py:37
  315.7 5.3 collective-permute-start.121
  326.7 5.7 collective-permute-start.67
  332.4 7.5 %collective-permute-start.59 = (bf16[192,1280]{1,0:T(8,128)(2,1)}, bf16[192,1280]{1,0:T(8,128)(2,1)}, u32[]{:S(2)}, u32[]{:S(2)}) collective-permute-start(bf16[192,1280]{1,0:T(8,128)(2,1)} %add_convert_fusion.5), channel_id=1, source_target_pairs={{0,4},{1,5},{2,6},{3,7},{4,0},{5,1},{6,2},{7,3},{8,12},{9,13},{10,... | collective-permute-start | bytes 1474568 | tf_op jit(solution)/shard_map/ppermute | solution.py:37
  344.8 14.7 %collective-permute-done.122 = bf16[40,640]{1,0:T(8,128)(2,1)} collective-permute-done((bf16[40,640]{1,0:T(8,128)(2,1)}, bf16[40,640]{1,0:T(8,128)(2,1)}, u32[]{:S(2)}, u32[]{:S(2)}) %collective-permute-start.122) | collective-permute-done | bytes 51232 | tf_op jit(solution)/shard_map/ppermute | solution.py:37
  369.3 18.4 %collective-permute-done.50 = bf16[192,1280]{1,0:T(8,128)(2,1)S(1)} collective-permute-done((bf16[192,1280]{1,0:T(8,128)(2,1)}, bf16[192,1280]{1,0:T(8,128)(2,1)S(1)}, u32[]{:S(2)}, u32[]{:S(2)}) %collective-permute-start.50) | collective-permute-done | bytes 491552 | tf_op jit(solution)/shard_map/ppermute | solution.py:37
  394.5 5.3 collective-permute-start.53
  402.5 5.0 collective-permute-done.70
  407.5 5.4 collective-permute-done.71
  412.8 6.1 collective-permute-done.72
  419.0 5.5 collective-permute-done.73
  433.6 16.0 %shard_map.306 = bf16[1536,480]{1,0:T(8,128)(2,1)S(1)} custom-call(bf16[1536,480]{1,0:T(8,128)(2,1)S(1)} %pad_maximum_fusion.2.queries.everything, bf16[1536,480]{1,0:T(8,128)(2,1)S(1)} %pad_maximum_fusion.2.queries.everything, bf16[2,1536,1536]{2,1,0:T(8,128)(2,1)} %get-tuple-element.20.probs, bf16[1536,160]{1,0:T(8,128)(2,1)S(1)} %get-tuple-element.19.mixed, ...), custom_call_target="tpu_custom_call" | custom-call | flops 9663676416 | bytes 16777216 | tf_op jit(solution)/shard_map/pallas_call | solution.py:196
  498.6 5.2 collective-permute-done.84
  512.5 14.5 %collective-permute-done.124 = bf16[8,40,640]{2,0,1:T(8,128)(2,1)S(1)} collective-permute-done((bf16[8,40,640]{2,0,1:T(8,128)(2,1)S(1)}, bf16[8,40,640]{2,0,1:T(8,128)(2,1)S(1)}, u32[]{:S(2)}, u32[]{:S(2)}) %collective-permute-start.124) | collective-permute-done | bytes 409632 | tf_op jit(solution)/shard_map/ppermute | solution.py:37
  527.3 7.8 %collective-permute-done.126 = bf16[8,40,640]{2,0,1:T(8,128)(2,1)S(1)} collective-permute-done((bf16[8,40,640]{2,0,1:T(8,128)(2,1)S(1)}, bf16[8,40,640]{2,0,1:T(8,128)(2,1)S(1)}, u32[]{:S(2)}, u32[]{:S(2)}) %collective-permute-start.126) | collective-permute-done | bytes 409632 | tf_op jit(solution)/shard_map/ppermute | solution.py:37
  544.0 6.2 collective-permute-done.134
  586.8 13.6 %collective-permute-done.81 = bf16[192,1280]{1,0:T(8,128)(2,1)S(1)} collective-permute-done((bf16[192,1280]{1,0:T(8,128)(2,1)S(1)}, bf16[192,1280]{1,0:T(8,128)(2,1)S(1)}, u32[]{:S(2)}, u32[]{:S(2)}) %collective-permute-start.81) | collective-permute-done | bytes 491552 | tf_op jit(solution)/shard_map/ppermute | solution.py:37
  637.2 8.9 %collective-permute-start.83 = (f32[192,1280]{1,0:T(8,128)}, f32[192,1280]{1,0:T(8,128)}, u32[]{:S(2)}, u32[]{:S(2)}) collective-permute-start(f32[192,1280]{1,0:T(8,128)} %fusion.70), channel_id=1, source_target_pairs={{0,0},{1,8},{2,2},{3,10},{4,4},{5,12},{6,6},{7,14},{8,1},{9,9},{10... | collective-permute-start | bytes 2949128 | tf_op jit(solution)/shard_map/ppermute | solution.py:37
  655.2 11.1 %fusion.127 = (f32[1,4,40,8,160]{4,0,2,3,1:T(1,128)S(1)}, f32[1,4,40,8,160]{4,0,2,3,1:T(1,128)}, f32[1,4,40,8,160]{4,0,2,3,1:T(1,128)S(1)}) fusion(f32[3,4,40,8,160]{4,0,2,3,1:T(4,128)} %bitcast.245), kind=kLoop, calls=%fused_computation.371 | loop fusion | bytes 4915200 | tf_op jit(solution)/shard_map/slice | solution.py:456
  (689 shorter events, 389.6 us)
Async XLA Ops:
  65.0 27.1 %collective-permute-start.54 = (bf16[192,1280]{1,0:T(8,128)(2,1)}, bf16[192,1280]{1,0:T(8,128)(2,1)S(1)}, u32[]{:S(2)}, u32[]{:S(2)}) collective-permute-start(bf16[192,1280]{1,0:T(8,128)(2,1)} %bitcast.52), channel_id=1, source_target_pairs={{0,0},{1,8},{2,2},{3,10},{4,4},{5,12},{6,6},{7,14},{8,1},{9,9},{10... | collective-permute-start | bytes 1474568 | tf_op jit(solution)/shard_map/ppermute | solution.py:37
  83.4 31.2 %collective-permute-start.29 = (bf16[160,1280]{1,0:T(8,128)(2,1)S(1)}, bf16[160,1280]{1,0:T(8,128)(2,1)S(1)}, u32[]{:S(2)}, u32[]{:S(2)}) collective-permute-start(bf16[160,1280]{1,0:T(8,128)(2,1)S(1)} %collective-permute-done.23), channel_id=1, source_target_pairs={{0,6},{1,7},{2,0},{3,1},{4,2},{5,3},{6,4},{7,5},{8,14},{9,15},{10,... | collective-permute-start | bytes 1228808 | tf_op jit(solution)/shard_map/ppermute | solution.py:37
  92.1 29.6 %collective-permute-start.11 = (bf16[192,1280]{1,0:T(8,128)(2,1)S(1)}, bf16[192,1280]{1,0:T(8,128)(2,1)S(1)}, u32[]{:S(2)}, u32[]{:S(2)}) collective-permute-start(bf16[192,1280]{1,0:T(8,128)(2,1)S(1)} %collective-permute-done), channel_id=1, source_target_pairs={{0,4},{1,5},{2,6},{3,7},{4,0},{5,1},{6,2},{7,3},{8,12},{9,13},{10,... | collective-permute-start | bytes 1474568 | tf_op jit(solution)/shard_map/ppermute | solution.py:37
  114.6 42.7 %collective-permute-start.60 = (bf16[192,1280]{1,0:T(8,128)(2,1)S(1)}, bf16[192,1280]{1,0:T(8,128)(2,1)}, u32[]{:S(2)}, u32[]{:S(2)}) collective-permute-start(bf16[192,1280]{1,0:T(8,128)(2,1)S(1)} %collective-permute-done.54), channel_id=1, source_target_pairs={{0,2},{1,3},{2,4},{3,5},{4,6},{5,7},{6,0},{7,1},{8,10},{9,11},{10,... | collective-permute-start | bytes 1474568 | tf_op jit(solution)/shard_map/ppermute | solution.py:37
  122.5 35.2 %collective-permute-start.56 = (bf16[192,1280]{1,0:T(8,128)(2,1)S(1)}, bf16[192,1280]{1,0:T(8,128)(2,1)}, u32[]{:S(2)}, u32[]{:S(2)}) collective-permute-start(bf16[192,1280]{1,0:T(8,128)(2,1)S(1)} %collective-permute-done.54), channel_id=1, source_target_pairs={{0,4},{1,5},{2,6},{3,7},{4,0},{5,1},{6,2},{7,3},{8,12},{9,13},{10,... | collective-permute-start | bytes 1474568 | tf_op jit(solution)/shard_map/ppermute | solution.py:37
  123.8 31.7 %collective-permute-start.30 = (bf16[160,1280]{1,0:T(8,128)(2,1)S(1)}, bf16[160,1280]{1,0:T(8,128)(2,1)S(1)}, u32[]{:S(2)}, u32[]{:S(2)}) collective-permute-start(bf16[160,1280]{1,0:T(8,128)(2,1)S(1)} %collective-permute-done.29), channel_id=1, source_target_pairs={{0,8},{1,9},{2,10},{3,11},{4,12},{5,13},{6,14},{7,15},{8,0},{9,1},... | collective-permute-start | bytes 1228808 | tf_op jit(solution)/shard_map/ppermute | solution.py:37
  132.1 28.5 %collective-permute-start.65 = (bf16[192,1280]{1,0:T(8,128)(2,1)S(1)}, bf16[192,1280]{1,0:T(8,128)(2,1)S(1)}, u32[]{:S(2)}, u32[]{:S(2)}) collective-permute-start(bf16[192,1280]{1,0:T(8,128)(2,1)S(1)} %collective-permute-done.64), channel_id=1, source_target_pairs={{0,8},{1,9},{2,10},{3,11},{4,12},{5,13},{6,14},{7,15},{8,0},{9,1},... | collective-permute-start | bytes 1474568 | tf_op jit(solution)/shard_map/ppermute | solution.py:37
  165.4 36.4 %collective-permute-start.40 = (bf16[640,1280]{1,0:T(8,128)(2,1)}, bf16[640,1280]{1,0:T(8,128)(2,1)}, u32[]{:S(2)}, u32[]{:S(2)}) collective-permute-start(bf16[640,1280]{1,0:T(8,128)(2,1)} %param.25), channel_id=1, source_target_pairs={{0,0},{1,8},{2,2},{3,10},{4,4},{5,12},{6,6},{7,14},{8,1},{9,9},{10... | collective-permute-start | bytes 4915208 | tf_op jit(solution)/shard_map/ppermute | solution.py:37
  251.1 35.2 %collective-permute-start.128 = (bf16[160,1280]{1,0:T(8,128)(2,1)S(1)}, bf16[160,1280]{1,0:T(8,128)(2,1)S(1)}, u32[]{:S(2)}, u32[]{:S(2)}) collective-permute-start(bf16[160,1280]{1,0:T(8,128)(2,1)S(1)} %get-tuple-element.63), channel_id=1, source_target_pairs={{0,32},{1,33},{2,34},{3,35},{4,36},{5,37},{6,38},{7,39},{8,40},{9,... | collective-permute-start | bytes 1228808 | tf_op jit(solution)/shard_map/ppermute | solution.py:37
  252.1 34.3 %collective-permute-start.127 = (bf16[160,1280]{1,0:T(8,128)(2,1)S(1)}, bf16[160,1280]{1,0:T(8,128)(2,1)S(1)}, u32[]{:S(2)}, u32[]{:S(2)}) collective-permute-start(bf16[160,1280]{1,0:T(8,128)(2,1)S(1)} %get-tuple-element.61), channel_id=1, source_target_pairs={{0,64},{1,65},{2,66},{3,67},{4,68},{5,69},{6,70},{7,71},{8,72},{9,... | collective-permute-start | bytes 1228808 | tf_op jit(solution)/shard_map/ppermute | solution.py:37
  287.1 33.9 %collective-permute-start.41 = (bf16[192,1280]{1,0:T(8,128)(2,1)S(1)}, bf16[192,1280]{1,0:T(8,128)(2,1)S(1)}, u32[]{:S(2)}, u32[]{:S(2)}) collective-permute-start(bf16[192,1280]{1,0:T(8,128)(2,1)S(1)} %slice.409), channel_id=1, source_target_pairs={{0,8},{1,9},{2,10},{3,11},{4,12},{5,13},{6,14},{7,15},{8,0},{9,1},... | collective-permute-start | bytes 1474568 | tf_op jit(solution)/shard_map/ppermute | solution.py:37
  296.5 30.2 %collective-permute-start.132 = (bf16[160,1280]{1,0:T(8,128)(2,1)S(1)}, bf16[160,1280]{1,0:T(8,128)(2,1)S(1)}, u32[]{:S(2)}, u32[]{:S(2)}) collective-permute-start(bf16[160,1280]{1,0:T(8,128)(2,1)S(1)} %fusion.103), channel_id=1, source_target_pairs={{0,17},{1,0},{2,19},{3,2},{4,21},{5,4},{6,23},{7,6},{8,25},{9,8},{... | collective-permute-start | bytes 1228808 | tf_op jit(solution)/shard_map/ppermute | solution.py:37
  326.7 35.4 %collective-permute-start.68 = (bf16[192,1280]{1,0:T(8,128)(2,1)}, bf16[192,1280]{1,0:T(8,128)(2,1)}, u32[]{:S(2)}, u32[]{:S(2)}) collective-permute-start(bf16[192,1280]{1,0:T(8,128)(2,1)} %slice.429), channel_id=1, source_target_pairs={{0,8},{1,9},{2,10},{3,11},{4,12},{5,13},{6,14},{7,15},{8,0},{9,1},... | collective-permute-start | bytes 1474568 | tf_op jit(solution)/shard_map/ppermute | solution.py:37
  326.7 37.2 %collective-permute-start.67 = (bf16[192,1280]{1,0:T(8,128)(2,1)}, bf16[192,1280]{1,0:T(8,128)(2,1)}, u32[]{:S(2)}, u32[]{:S(2)}) collective-permute-start(bf16[192,1280]{1,0:T(8,128)(2,1)} %add_convert_fusion.3), channel_id=1, source_target_pairs={{0,2},{1,3},{2,4},{3,5},{4,6},{5,7},{6,0},{7,1},{8,10},{9,11},{10,... | collective-permute-start | bytes 1474568 | tf_op jit(solution)/shard_map/ppermute | solution.py:37
  332.4 33.0 %collective-permute-start.63 = (bf16[192,1280]{1,0:T(8,128)(2,1)}, bf16[192,1280]{1,0:T(8,128)(2,1)}, u32[]{:S(2)}, u32[]{:S(2)}) collective-permute-start(bf16[192,1280]{1,0:T(8,128)(2,1)} %add_convert_fusion.4), channel_id=1, source_target_pairs={{0,6},{1,7},{2,0},{3,1},{4,2},{5,3},{6,4},{7,5},{8,14},{9,15},{10,... | collective-permute-start | bytes 1474568 | tf_op jit(solution)/shard_map/ppermute | solution.py:37
  332.4 33.6 %collective-permute-start.59 = (bf16[192,1280]{1,0:T(8,128)(2,1)}, bf16[192,1280]{1,0:T(8,128)(2,1)}, u32[]{:S(2)}, u32[]{:S(2)}) collective-permute-start(bf16[192,1280]{1,0:T(8,128)(2,1)} %add_convert_fusion.5), channel_id=1, source_target_pairs={{0,4},{1,5},{2,6},{3,7},{4,0},{5,1},{6,2},{7,3},{8,12},{9,13},{10,... | collective-permute-start | bytes 1474568 | tf_op jit(solution)/shard_map/ppermute | solution.py:37
  366.0 127.8 %collective-permute-start.133 = (bf16[160,1280]{1,0:T(8,128)(2,1)}, bf16[160,1280]{1,0:T(8,128)(2,1)}, u32[]{:S(2)}, u32[]{:S(2)}) collective-permute-start(bf16[160,1280]{1,0:T(8,128)(2,1)} %add_convert_fusion.11), channel_id=1, source_target_pairs={{0,8},{1,9},{2,10},{3,11},{4,12},{5,13},{6,14},{7,15},{8,0},{9,1},... | collective-permute-start | bytes 1228808 | tf_op jit(solution)/shard_map/ppermute | solution.py:37
  368.8 95.6 %collective-permute-start.123 = (bf16[4,40,640]{2,1,0:T(8,128)(2,1)}, bf16[4,40,640]{2,1,0:T(8,128)(2,1)}, u32[]{:S(2)}, u32[]{:S(2)}) collective-permute-start(bf16[4,40,640]{2,1,0:T(8,128)(2,1)} %pad_maximum_fusion.12), channel_id=1, source_target_pairs={{0,8},{1,9},{2,10},{3,11},{4,12},{5,13},{6,14},{7,15},{8,0},{9,1},... | collective-permute-start | bytes 614408 | tf_op jit(solution)/shard_map/ppermute | solution.py:37
  394.1 111.6 %collective-permute-start.97 = (bf16[192,1280]{1,0:T(8,128)(2,1)S(1)}, bf16[192,1280]{1,0:T(8,128)(2,1)}, u32[]{:S(2)}, u32[]{:S(2)}) collective-permute-start(bf16[192,1280]{1,0:T(8,128)(2,1)S(1)} %get-tuple-element.40), channel_id=1, source_target_pairs={{0,8},{1,9},{2,10},{3,11},{4,12},{5,13},{6,14},{7,15},{8,0},{9,1},... | collective-permute-start | bytes 1474568 | tf_op jit(solution)/shard_map/ppermute | solution.py:37
  394.5 110.4 %collective-permute-start.53 = (bf16[192,1280]{1,0:T(8,128)(2,1)}, bf16[192,1280]{1,0:T(8,128)(2,1)}, u32[]{:S(2)}, u32[]{:S(2)}) collective-permute-start(bf16[192,1280]{1,0:T(8,128)(2,1)} %get-tuple-element.74), channel_id=1, source_target_pairs={{0,0},{1,8},{2,2},{3,10},{4,4},{5,12},{6,6},{7,14},{8,1},{9,9},{10... | collective-permute-start | bytes 1474568 | tf_op jit(solution)/shard_map/ppermute | solution.py:37
  463.7 30.5 %collective-permute-start.86 = (bf16[8,40,480]{2,1,0:T(8,128)(2,1)}, bf16[8,40,480]{2,1,0:T(8,128)(2,1)}, u32[]{:S(2)}, u32[]{:S(2)}) collective-permute-start(bf16[8,40,480]{2,1,0:T(8,128)(2,1)} %get-tuple-element.71), channel_id=1, source_target_pairs={{0,96},{1,97},{2,98},{3,99},{4,100},{5,101},{6,102},{7,103},{8,104... | collective-permute-start | bytes 921608 | tf_op jit(solution)/shard_map/ppermute | solution.py:37
  464.3 30.9 %collective-permute-start.85 = (bf16[8,40,480]{2,1,0:T(8,128)(2,1)}, bf16[8,40,480]{2,1,0:T(8,128)(2,1)}, u32[]{:S(2)}, u32[]{:S(2)}) collective-permute-start(bf16[8,40,480]{2,1,0:T(8,128)(2,1)} %get-tuple-element.72), channel_id=1, source_target_pairs={{0,32},{1,33},{2,34},{3,35},{4,36},{5,37},{6,38},{7,39},{8,40},{9,... | collective-permute-start | bytes 921608 | tf_op jit(solution)/shard_map/ppermute | solution.py:37
  495.2 73.5 %collective-permute-start.100 = (bf16[192,1280]{1,0:T(8,128)(2,1)S(1)}, bf16[192,1280]{1,0:T(8,128)(2,1)S(1)}, u32[]{:S(2)}, u32[]{:S(2)}) collective-permute-start(bf16[192,1280]{1,0:T(8,128)(2,1)S(1)} %get-tuple-element.40), channel_id=1, source_target_pairs={{0,4},{1,5},{2,6},{3,7},{4,0},{5,1},{6,2},{7,3},{8,12},{9,13},{10,... | collective-permute-start | bytes 1474568 | tf_op jit(solution)/shard_map/ppermute | solution.py:37
  503.7 34.0 %collective-permute-start.80 = (bf16[192,1280]{1,0:T(8,128)(2,1)S(1)}, bf16[192,1280]{1,0:T(8,128)(2,1)S(1)}, u32[]{:S(2)}, u32[]{:S(2)}) collective-permute-start(bf16[192,1280]{1,0:T(8,128)(2,1)S(1)} %copy-done.35), channel_id=1, source_target_pairs={{0,8},{1,9},{2,10},{3,11},{4,12},{5,13},{6,14},{7,15},{8,0},{9,1},... | collective-permute-start | bytes 1474568 | tf_op jit(solution)/shard_map/ppermute | solution.py:37
  505.0 35.4 %collective-permute-start.78 = (bf16[192,1280]{1,0:T(8,128)(2,1)S(1)}, bf16[192,1280]{1,0:T(8,128)(2,1)S(1)}, u32[]{:S(2)}, u32[]{:S(2)}) collective-permute-start(bf16[192,1280]{1,0:T(8,128)(2,1)S(1)} %copy-done.34), channel_id=1, source_target_pairs={{0,8},{1,9},{2,10},{3,11},{4,12},{5,13},{6,14},{7,15},{8,0},{9,1},... | collective-permute-start | bytes 1474568 | tf_op jit(solution)/shard_map/ppermute | solution.py:37
  540.4 26.8 %collective-permute-start.136 = (bf16[160,1280]{1,0:T(8,128)(2,1)S(1)}, bf16[160,1280]{1,0:T(8,128)(2,1)S(1)}, u32[]{:S(2)}, u32[]{:S(2)}) collective-permute-start(bf16[160,1280]{1,0:T(8,128)(2,1)S(1)} %get-tuple-element.43), channel_id=1, source_target_pairs={{0,96},{1,97},{2,98},{3,99},{4,100},{5,101},{6,102},{7,103},{8,104... | collective-permute-start | bytes 1228808 | tf_op jit(solution)/shard_map/ppermute | solution.py:37
  584.5 61.6 %collective-permute-start.94 = (bf16[8,40,480]{2,1,0:T(8,128)(2,1)}, bf16[8,40,480]{2,1,0:T(8,128)(2,1)S(1)}, u32[]{:S(2)}, u32[]{:S(2)}) collective-permute-start(bf16[8,40,480]{2,1,0:T(8,128)(2,1)} %slice_dynamic-update-slice_fusion.1), channel_id=1, source_target_pairs={{0,32},{1,33},{2,34},{3,35},{4,36},{5,37},{6,38},{7,39},{8,40},{9,... | collective-permute-start | bytes 921608 | tf_op jit(solution)/shard_map/ppermute | solution.py:37
  585.7 62.6 %collective-permute-start.95 = (bf16[8,40,480]{2,1,0:T(8,128)(2,1)}, bf16[8,40,480]{2,1,0:T(8,128)(2,1)S(1)}, u32[]{:S(2)}, u32[]{:S(2)}) collective-permute-start(bf16[8,40,480]{2,1,0:T(8,128)(2,1)} %slice_dynamic-update-slice_fusion.1), channel_id=1, source_target_pairs={{0,64},{1,65},{2,66},{3,67},{4,68},{5,69},{6,70},{7,71},{8,72},{9,... | collective-permute-start | bytes 921608 | tf_op jit(solution)/shard_map/ppermute | solution.py:37
  637.2 50.9 %collective-permute-start.83 = (f32[192,1280]{1,0:T(8,128)}, f32[192,1280]{1,0:T(8,128)}, u32[]{:S(2)}, u32[]{:S(2)}) collective-permute-start(f32[192,1280]{1,0:T(8,128)} %fusion.70), channel_id=1, source_target_pairs={{0,0},{1,8},{2,2},{3,10},{4,4},{5,12},{6,6},{7,14},{8,1},{9,9},{10... | collective-permute-start | bytes 2949128 | tf_op jit(solution)/shard_map/ppermute | solution.py:37
  646.1 27.9 %collective-permute-start.109 = (bf16[40,1280]{1,0:T(8,128)(2,1)S(1)}, bf16[40,1280]{1,0:T(8,128)(2,1)S(1)}, u32[]{:S(2)}, u32[]{:S(2)}) collective-permute-start(bf16[40,1280]{1,0:T(8,128)(2,1)S(1)} %fusion.116), channel_id=1, source_target_pairs={{0,17},{1,0},{2,19},{3,2},{4,21},{5,4},{6,23},{7,6},{8,25},{9,8},{... | collective-permute-start | bytes 307208 | tf_op jit(solution)/shard_map/ppermute | solution.py:37
  646.1 27.8 %collective-permute-start.108 = (bf16[40,1280]{1,0:T(8,128)(2,1)S(1)}, bf16[40,1280]{1,0:T(8,128)(2,1)}, u32[]{:S(2)}, u32[]{:S(2)}) collective-permute-start(bf16[40,1280]{1,0:T(8,128)(2,1)S(1)} %fusion.116), channel_id=1, source_target_pairs={{0,1},{1,16},{2,3},{3,18},{4,5},{5,20},{6,7},{7,22},{8,9},{9,24},{... | collective-permute-start | bytes 307208 | tf_op jit(solution)/shard_map/ppermute | solution.py:37
  648.3 25.7 %collective-permute-start.107 = (bf16[40,1280]{1,0:T(8,128)(2,1)S(1)}, bf16[40,1280]{1,0:T(8,128)(2,1)S(1)}, u32[]{:S(2)}, u32[]{:S(2)}) collective-permute-start(bf16[40,1280]{1,0:T(8,128)(2,1)S(1)} %fusion.116), channel_id=1, source_target_pairs={{0,16},{1,17},{2,18},{3,19},{4,20},{5,21},{6,22},{7,23},{8,24},{9,... | collective-permute-start | bytes 307208 | tf_op jit(solution)/shard_map/ppermute | solution.py:37
  (190 other events, 2566.3 us)

commit v2 on v1

v2 whole, which is shorter than its diff:
```python
import functools

import jax
import jax.numpy as jnp
from jax import lax
from jax.experimental import pallas as pl
from jax.experimental.pallas import tpu as pltpu
from jax.sharding import PartitionSpec as P

H = 16
HD = 80
EPS = 1e-05
AXES = ("rep", "shard")
F32 = jnp.float32
BF16 = jnp.bfloat16
NT = (((1,), (1,)), ((), ()))
TN = (((0,), (0,)), ((), ()))


def flat_index(y, zh, c, x, zl):
    return ((y % 4) * 4 + (zh % 2) * 2 + c % 2) * 8 + (x % 4) * 2 + zl % 2


def pairs(move):
    found = []
    for y in range(4):
        for zh in range(2):
            for c in range(2):
                for x in range(4):
                    for zl in range(2):
                        here = flat_index(y, zh, c, x, zl)
                        found.append((here, flat_index(*move(y, zh, c, x, zl))))
    return found


def send(value, move):
    return lax.ppermute(value, AXES, pairs(move))


def along_x(value, dx):
    return send(value, lambda y, zh, c, x, zl: (y, zh, c, x + dx, zl))


def along_y(value, dy):
    return send(value, lambda y, zh, c, x, zl: (y + dy, zh, c, x, zl))


def along_z(value, dz):
    def move(y, zh, c, x, zl):
        z = (2 * zh + zl + dz) % 4
        return (y, z // 2, c, x, z % 2)

    return send(value, move)


def to_sibling(value):
    return send(value, lambda y, zh, c, x, zl: (y, zh, c + 1, x, zl))


def cross(value):
    return send(value, lambda y, zh, c, x, zl: (y, zh, zl, x, c))


def gather_group(own):
    near = [own] + [along_x(own, dx) for dx in (1, 2, 3)]
    return [[block, to_sibling(block)] for block in near]


def scatter_group(parts):
    total = None
    for dx in (2, 1, 3, 0):
        both = parts[dx][0].astype(F32) + to_sibling(parts[dx][1]).astype(F32)
        if dx > 0:
            both = along_x(both.astype(BF16), -dx).astype(F32)
        total = both if total is None else total + both
    return total


def sum_four(value, along):
    one, two, three = (along(value, step).astype(F32) for step in (1, 2, 3))
    return (value.astype(F32) + two) + (one + three)


def place(blocks, indices):
    held = jnp.zeros((len(blocks),) + blocks[0].shape, blocks[0].dtype)
    for block, index in zip(blocks, indices):
        held = lax.dynamic_update_index_in_dim(held, block, index, 0)
    return held


def pick(array, index, axis=0):
    return lax.dynamic_index_in_dim(array, index, axis, keepdims=False)


def norm_fwd(values, gain, shift):
    center = values - jnp.mean(values, axis=-1, keepdims=True)
    inverse = lax.rsqrt(jnp.mean(center * center, axis=-1, keepdims=True) + EPS)
    normed = center * inverse
    return (normed, inverse, normed * gain + shift)


def norm_back(grad_rows, normed, inverse, gain):
    scaled = grad_rows * gain
    grad_in = inverse * (
        scaled
        - jnp.mean(scaled, axis=-1, keepdims=True)
        - normed * jnp.mean(scaled * normed, axis=-1, keepdims=True)
    )
    return (grad_in, jnp.sum(grad_rows * normed, axis=0), jnp.sum(grad_rows, axis=0))


MESH = pl.DeviceIdType.MESH
VMEM = pl.BlockSpec(memory_space=pltpu.VMEM)
HBM = pl.BlockSpec(memory_space=pl.ANY)


class Net:
    def __init__(self, sent, got, still):
        rep, shard = lax.axis_index("rep"), lax.axis_index("shard")
        self.y, self.zh, self.c = rep // 4, rep // 2 % 2, rep % 2
        self.x, self.zl = shard // 2, shard % 2
        self.me, self.shard = 2 * self.x + self.c, shard
        self.sent, self.got, self.still, self.used, self.started = sent, got, still, 0, []

    def device(self, dx=0, dc=0, dz=0, dy=0):
        z = (2 * self.zh + self.zl + dz) % 4
        return (
            (self.y + dy) % 4 * 4 + z // 2 * 2 + (self.c + dc) % 2,
            (self.x + dx) % 4 * 2 + z % 2,
        )

    def in_pair(self, dx, dz):
        return (
            self.y * 4 + self.zh * 2 + self.c,
            (self.x + dx) % 4 * 2 + (self.zl + dz) % 2,
        )

    def partner(self):
        return (self.y * 4 + self.zh * 2 + self.zl, 2 * self.x + self.c)

    def greet(self, devices):
        barrier = pltpu.get_barrier_semaphore()
        for device in devices:
            pl.semaphore_signal(barrier, inc=1, device_id=device, device_id_type=MESH)
        return lambda: pl.semaphore_wait(barrier, len(devices))

    def reserve(self, count):
        first = self.used
        self.used += count
        return first

    def copy(self, index, source, target, device):
        return pltpu.make_async_remote_copy(
            src_ref=source,
            dst_ref=target,
            send_sem=self.sent.at[index],
            recv_sem=self.got.at[index],
            device_id=device,
            device_id_type=MESH,
        )

    def go(self, source, target, device):
        copy = self.copy(self.reserve(1), source, target, device)
        copy.start()
        self.started.append(copy)
        return copy

    def cross(self, source, target):
        index = self.reserve(1)
        copy = self.copy(index, source, target, self.partner())
        local = pltpu.make_async_copy(source, target, self.still.at[index])

        @pl.when(self.c != self.zl)
        def _():
            copy.start()

        @pl.when(self.c == self.zl)
        def _():
            local.start()

        def arrived():
            @pl.when(self.c != self.zl)
            def _():
                copy.wait_recv()

            @pl.when(self.c == self.zl)
            def _():
                local.wait()

        def left():
            @pl.when(self.c != self.zl)
            def _():
                copy.wait_send()

        return arrived, left

    def all_sent(self):
        for copy in self.started:
            copy.wait_send()


def order(k):
    return 1 + 2 * k - 3 * (k // 2)


def aligned(index, size):
    return pl.ds(pl.multiple_of(index * size, size), size)


def scratch_for(copies):
    return [pltpu.SemaphoreType.DMA((copies,)) for _ in range(3)]


def begin_kernel(
    tokens,
    w_query,
    w_key,
    w_value,
    small,
    w_out,
    w_up,
    w_down,
    cotangent,
    length,
    h1,
    heads,
    probs,
    mixed,
    attended,
    w_qkv,
    smalls,
    own,
    clip,
    out_full,
    up_mine,
    down_mine,
    top,
    gathered,
    cut,
    lens,
    vectors,
    sent,
    got,
    still,
):
    net = Net(sent, got, still)
    x, c, zl, me, shard = net.x, net.c, net.zl, net.me, net.shard
    rows, width = tokens.shape
    plane = [net.device(dx, dc) for dx in range(4) for dc in range(2) if dx or dc]
    across = [net.in_pair(dx, 1) for dx in range(4)]
    everyone = plane + across + [(net.y * 4 + net.zh * 2 + 1 - c, 2 * x + 1 - zl)]
    wait = net.greet(everyone)
    for block in range(8):
        cols = slice(160 * block, 160 * block + 160)
        cut[block, :, :160] = w_query[:, cols]
        cut[block, :, 160:320] = w_key[:, cols]
        cut[block, :, 320:] = w_value[:, cols]
    wait()

    token_arrived, token_left = net.cross(tokens, gathered.at[2 * x + zl])
    base = net.reserve(4)

    def token_send(k, source):
        dx = order(k)
        return net.copy(base + dx, source, gathered.at[me], net.device(dx))

    @pl.when(c == zl)
    def _():
        for k in range(3):
            token_send(k, tokens).start()

    @pl.when(c == 0)
    def _():
        lens[0] = length[...]

    @pl.when(c == 1)
    def _():
        lens[1] = length[...]

    lens_copy = net.go(length, lens.at[c], net.device(0, 1))
    arriving = []
    for dx in (0, 1, 3, 2):
        for dz in range(2):
            if dx or dz:
                device = net.in_pair(dx, dz)
                arriving.append(net.go(small, smalls.at[shard], device))
                target = 2 * ((x + dx) % 4) + c
                arriving.append(net.go(cut.at[target], w_qkv.at[aligned(shard, 160)], device))
    smalls[shard] = small[...]
    w_qkv[aligned(shard, 160)] = cut[me]
    token_arrived()

    @pl.when(c != zl)
    def _():
        for k in range(3):
            token_send(k, gathered.at[me]).start()

    sibling = net.device(0, 1)
    own_over = net.go(gathered.at[me], gathered.at[me], sibling)
    out_arrived, out_left = net.cross(w_out, out_full.at[2 * x + zl])
    top_arrived, top_left = net.cross(cotangent, top.at[2 * x + zl])
    down_arrived, down_left = net.cross(w_down, down_mine)
    own[...] = gathered[me]

    for copy in arriving:
        copy.wait_recv()
    for block in range(8):
        vectors[:, 160 * block : 160 * block + 160] = smalls[block, :8, :160].astype(F32)
    gain, shift = vectors[4:5, :], vectors[5:6, :]
    bias_q = smalls[me, 0:1, :160].astype(F32)
    bias_v = smalls[me, 1:2, :160].astype(F32)

    def project(slot):
        values = gathered[slot].astype(F32)
        center = values - jnp.mean(values, axis=-1, keepdims=True)
        inverse = lax.rsqrt(jnp.mean(center * center, axis=-1, keepdims=True) + EPS)
        normed = (center * inverse * gain + shift).astype(BF16)
        h1[slot] = normed
        made = jnp.dot(normed, w_qkv[...], preferred_element_type=F32)
        here = aligned(slot, rows)
        for h in range(2):
            cols = slice(h * HD, (h + 1) * HD)
            heads[h, here, :] = (made[:, cols] + bias_q[:, cols]).astype(BF16)
            heads[2 + h, here, :] = made[:, 160 + h * HD : 240 + h * HD].astype(BF16)
            heads[4 + h, here, :] = (
                made[:, 320 + h * HD : 400 + h * HD] + bias_v[:, cols]
            ).astype(BF16)

    project(me)
    own_over.wait_recv()
    project(2 * x + 1 - c)
    over = net.reserve(4)

    def passed(dx, slot):
        return net.copy(over + dx, gathered.at[slot], gathered.at[slot], sibling)

    @pl.loop(0, 3)
    def _(k):
        dx = order(k)
        from_x = (x - dx + 4) % 4
        token_send(k, gathered.at[me]).wait_recv()
        passed(dx, 2 * from_x + c).start()
        project(2 * from_x + c)
        passed(dx, 2 * from_x + c).wait_recv()
        project(2 * from_x + 1 - c)

    later = []
    top_arrived()
    for dx in (1, 3, 2):
        later.append((net.go(top.at[me], top.at[me], net.device(dx)), top, dx))
    out_arrived()
    for dx in (1, 3, 2):
        later.append((net.go(out_full.at[me], out_full.at[me], net.device(dx)), out_full, dx))
    last = [
        net.go(top.at[me], top.at[me], sibling),
        net.go(out_full.at[me], out_full.at[me], sibling),
    ]
    for dx in (0, 1, 3, 2):
        for dz in range(2):
            if dx or dz:
                target = 2 * ((x + dx) % 4) + c
                source = w_up.at[:, pl.ds(pl.multiple_of(target * 640, 128), 640)]
                last.append(net.go(source, up_mine.at[shard], net.in_pair(dx, dz)))
    mine_up = pltpu.make_async_copy(
        w_up.at[:, pl.ds(pl.multiple_of(me * 640, 128), 640)],
        up_mine.at[shard],
        still.at[net.reserve(1)],
    )
    mine_up.start()

    lens_copy.wait_recv()
    clip[...] = lens[zl]
    clip_length = clip[0:1, 0:1]
    position = lax.broadcasted_iota(jnp.int32, (1, 8 * rows), 1).astype(F32)
    mask = jnp.where(position < clip_length, 0.0, -1e30)

    def attend_rows(to_x):
        here = aligned(to_x, 2 * rows)
        for h in range(2):
            cols = slice(h * HD, (h + 1) * HD)
            scores = lax.dot_general(heads[h, here, :], heads[2 + h], NT, preferred_element_type=F32)
            scores = scores * HD**-0.5 + mask
            risen = jnp.exp(scores - jnp.max(scores, axis=-1, keepdims=True))
            share = 1.0 / jnp.sum(risen, axis=-1, keepdims=True)
            low = (risen * share).astype(BF16)
            probs[h, here, :] = low
            made = jnp.dot(low, heads[4 + h], preferred_element_type=F32).astype(BF16)
            mixed[2 * to_x, :, cols] = made[:rows]
            mixed[2 * to_x + 1, :, cols] = made[rows:]

    mixed_base = net.reserve(8)

    def mixed_send(dx, dc):
        slot = 2 * ((x + dx) % 4) + (c + dc) % 2
        return net.copy(
            mixed_base + 2 * dx + dc, mixed.at[slot], attended.at[me], net.device(dx, dc)
        )

    @pl.loop(1, 5)
    def _(step):
        dx = step % 4
        attend_rows((x + dx) % 4)
        mixed_send(dx, 1).start()

        @pl.when(dx != 0)
        def _():
            mixed_send(dx, 0).start()

    attended[me] = mixed[me]
    for copy, array, dx in later:
        copy.wait_recv()
        slot = 2 * ((x - dx + 4) % 4) + c
        last.append(net.go(array.at[slot], array.at[slot], sibling))

    for dx in range(4):
        for dc in range(2):
            if dx or dc:
                mixed_send(dx, dc).wait()
    for copy in last:
        copy.wait_recv()
    mine_up.wait()
    down_arrived()
    for left in (token_left, out_left, top_left, down_left):
        left()
    for k in range(3):
        token_send(k, gathered.at[me]).wait_send()
        dx = order(k)
        passed(dx, me).wait_send()
    net.all_sent()


def begin(tokens, w_query, w_key, w_value, small, w_out, w_up, w_down, cotangent, length):
    rows, width = tokens.shape

    def shape(*dims):
        return jax.ShapeDtypeStruct(dims, BF16)

    return pl.pallas_call(
        begin_kernel,
        in_specs=[VMEM] * 5 + [HBM] * 4 + [VMEM],
        out_specs=[VMEM] * 9 + [HBM] * 4,
        out_shape=[
            shape(8, rows, width),
            shape(6, 8 * rows, HD),
            shape(2, 8 * rows, 8 * rows),
            shape(8, rows, 160),
            shape(8, rows, 160),
            shape(width, 480),
            shape(8, 16, 640),
            shape(rows, width),
            jax.ShapeDtypeStruct((8, 128), F32),
            shape(8, 160, width),
            shape(8, 160, 640),
            shape(640, width),
            shape(8, rows, width),
        ],
        scratch_shapes=[
            pltpu.VMEM((8, rows, width), BF16),
            pltpu.VMEM((8, 160, 480), BF16),
            pltpu.VMEM((2, 8, 128), F32),
            pltpu.VMEM((8, width), F32),
        ]
        + scratch_for(80),
        compiler_params=pltpu.CompilerParams(
            collective_id=0, has_side_effects=True, vmem_limit_bytes=58 << 20
        ),
    )(tokens, w_query, w_key, w_value, small, w_out, w_up, w_down, cotangent, length)


def middle_kernel(
    attended,
    own,
    smalls,
    clip,
    out_full,
    up_mine,
    down_mine,
    top,
    middle,
    grad_middle,
    branch,
    out_parts,
    g_up,
    g_down,
    g_up_bias,
    g_vectors,
    grad_mixed,
    vectors,
    second,
    masked,
    active,
    hidden,
    parts,
    over,
    sums,
    arrived,
    joined,
    by_head,
    sent,
    got,
    still,
):
    net = Net(sent, got, still)
    x, c, me = net.x, net.c, net.me
    rows, width = own.shape
    wait = net.greet([net.device(dx, dc) for dx in range(4) for dc in range(2) if dx or dc])
    for block in range(8):
        vectors[:, 160 * block : 160 * block + 160] = smalls[block, :8, :160].astype(F32)
    bias_up = smalls[me, 8:9, :].astype(F32)
    mine = aligned(me, rows)
    for block in range(8):
        joined[:, 160 * block : 160 * block + 160] = attended[block]
    made = jnp.dot(joined[...], out_full[...], preferred_element_type=F32)
    middle[...] = own[...].astype(F32) + made + vectors[2:3, :]

    def normalised():
        values = middle[...]
        center = values - jnp.mean(values, axis=-1, keepdims=True)
        inverse = lax.rsqrt(jnp.mean(center * center, axis=-1, keepdims=True) + EPS)
        return center * inverse, inverse

    second[mine, :] = (normalised()[0] * vectors[6:7, :] + vectors[7:8, :]).astype(BF16)
    wait()

    near, pass_on, swap, add = (net.reserve(4) for _ in range(4))

    def near_copy(dx):
        return net.copy(near + dx, second.at[mine], second.at[mine], net.device(dx))

    def pass_copy(dx, slot):
        here = second.at[aligned(slot, rows)]
        return net.copy(pass_on + dx, here, here, net.device(0, 1))

    def swap_copy(dx, to_x):
        source = parts.at[aligned(2 * to_x + 1 - c, rows)]
        return net.copy(swap + dx, source, over.at[to_x], net.device(0, 1))

    def add_copy(dx, to_x):
        return net.copy(add + dx, sums.at[to_x], arrived.at[dx], net.device(4 - dx))

    for dx in (1, 3, 2):
        near_copy(dx).start()

    @pl.loop(0, 4)
    def _(k):
        dx = k ^ (k >> 1)
        to_x = (x - dx + 4) % 4

        @pl.when(dx != 0)
        def _():
            near_copy(dx).wait_recv()

        pass_copy(dx, 2 * to_x + c).start()
        here = aligned(to_x, 2 * rows)
        position = lax.broadcasted_iota(jnp.int32, (2 * rows, 1), 0) + to_x * 2 * rows
        live = position.astype(F32) < clip[0:1, 0:1]
        low_top = jnp.where(live, top[here, :].astype(F32), 0.0).astype(BF16)
        masked[here, :] = low_top
        grad_act = lax.dot_general(low_top, down_mine[...], NT, preferred_element_type=F32)
        pass_copy(dx, 2 * to_x + c).wait_recv()
        z = jnp.dot(second[here, :], up_mine[...], preferred_element_type=F32) + bias_up
        bell = 0.5 * (1.0 + lax.erf(z * 0.7071067811865476))
        active[here, :] = (z * bell).astype(BF16)
        slope = bell + z * jnp.exp(-0.5 * z * z) * 0.3989422804014327
        grad_z = (grad_act * slope).astype(BF16)
        hidden[here, :] = grad_z
        parts[here, :] = lax.dot_general(
            grad_z, up_mine[...], NT, preferred_element_type=F32
        ).astype(BF16)
        swap_copy(dx, to_x).start()
        out_parts[here, :] = jnp.dot(
            active[here, :], down_mine[...], preferred_element_type=F32
        ).astype(BF16)
        swap_copy(dx, to_x).wait_recv()

        @pl.when(dx != 0)
        def _():
            kept = parts[aligned(2 * to_x + c, rows), :].astype(F32)
            sums[to_x] = (kept + over[to_x].astype(F32)).astype(BF16)
            add_copy(dx, to_x).start()

    @pl.loop(0, 5)
    def _(i):
        cols = pl.ds(pl.multiple_of(i * 256, 256), 256)
        g_up[cols, :] = lax.dot_general(
            second[:, cols], hidden[...], TN, preferred_element_type=F32
        ).astype(BF16)
        cols = pl.ds(pl.multiple_of(i * 128, 128), 128)
        g_down[cols, :] = lax.dot_general(
            active[:, cols], masked[...], TN, preferred_element_type=F32
        ).astype(BF16)

    g_up_bias[...] = jnp.sum(hidden[...].astype(F32), axis=0, keepdims=True)
    grad_second = parts[mine, :].astype(F32) + over[x].astype(F32)
    for dx in (1, 3, 2):
        add_copy(dx, (x - dx + 4) % 4).wait_recv()
        grad_second = grad_second + arrived[dx].astype(F32)
    normed, inverse = normalised()
    scaled = grad_second * vectors[6:7, :]
    back = inverse * (
        scaled
        - jnp.mean(scaled, axis=-1, keepdims=True)
        - normed * jnp.mean(scaled * normed, axis=-1, keepdims=True)
    )
    top_own = masked[mine, :].astype(F32)
    total = top_own + back
    grad_middle[...] = total
    low = total.astype(BF16)
    branch[...] = low
    grad_attended = lax.dot_general(low, out_full[...], NT, preferred_element_type=F32)
    grad_attended = grad_attended.astype(BF16)
    for block in range(8):
        by_head[block] = grad_attended[:, 160 * block : 160 * block + 160]
    mixing = []
    for dx in (2, 1, 3, 0):
        for dc in (1, 0):
            if dx or dc:
                slot = 2 * ((x + dx) % 4) + (c + dc) % 2
                mixing.append(net.go(by_head.at[slot], grad_mixed.at[me], net.device(dx, dc)))
    grad_mixed[me] = by_head[me]
    g_vectors[0:1, :] = jnp.sum(low.astype(F32), axis=0, keepdims=True)
    g_vectors[1:2, :] = jnp.sum(top_own, axis=0, keepdims=True)
    g_vectors[2:3, :] = jnp.sum(grad_second * normed, axis=0, keepdims=True)
    g_vectors[3:4, :] = jnp.sum(grad_second, axis=0, keepdims=True)
    for copy in mixing:
        copy.wait_recv()
    for dx in range(4):
        to_x = (x - dx + 4) % 4
        pass_copy(dx, 2 * to_x + c).wait_send()
        swap_copy(dx, to_x).wait_send()
        if dx:
            near_copy(dx).wait_send()
            add_copy(dx, to_x).wait_send()
    net.all_sent()


def middle_part(attended, own, smalls, clip, out_full, up_mine, down_mine, top):
    rows, width = own.shape

    def shape(*dims, dtype=BF16):
        return jax.ShapeDtypeStruct(dims, dtype)

    def buffer(*dims, dtype=BF16):
        return pltpu.VMEM(dims, dtype)

    return pl.pallas_call(
        middle_kernel,
        in_specs=[VMEM] * 8,
        out_specs=[VMEM] * 9,
        out_shape=[
            shape(rows, width, dtype=F32),
            shape(rows, width, dtype=F32),
            shape(rows, width),
            shape(8 * rows, width),
            shape(width, 640),
            shape(640, width),
            shape(1, 640, dtype=F32),
            shape(4, width, dtype=F32),
            shape(8, rows, 160),
        ],
        scratch_shapes=[
            buffer(8, width, dtype=F32),
            buffer(8 * rows, width),
            buffer(8 * rows, width),
            buffer(8 * rows, 640),
            buffer(8 * rows, 640),
            buffer(8 * rows, width),
            buffer(4, rows, width),
            buffer(4, rows, width),
            buffer(4, rows, width),
            buffer(rows, width),
            buffer(8, rows, 160),
        ]
        + scratch_for(24),
        compiler_params=pltpu.CompilerParams(
            collective_id=1, has_side_effects=True, vmem_limit_bytes=60 << 20
        ),
    )(attended, own, smalls, clip, out_full, up_mine, down_mine, top)


def attend_back_kernel(scale, queries, keys, values, probs, mixed, grad_mixed, grads, sum_k, sum_v):
    step = pl.program_id(0)
    tile = queries.shape[1]

    @pl.when(step == 0)
    def _():
        sum_k[...] = jnp.zeros_like(sum_k)
        sum_v[...] = jnp.zeros_like(sum_v)

    here = pl.ds(pl.multiple_of(step * tile, tile), tile)
    for h in range(2):
        cols = slice(h * HD, (h + 1) * HD)
        mine, back, low = queries[h], grad_mixed[:, cols], probs[h]
        row_total = jnp.sum(
            back.astype(F32) * mixed[:, cols].astype(F32), axis=-1, keepdims=True
        )
        grad_probs = lax.dot_general(back, values[h], NT, preferred_element_type=F32)
        grad_scores = (low.astype(F32) * (grad_probs - row_total)).astype(BF16)
        sum_v[h] += lax.dot_general(low, back, TN, preferred_element_type=F32)
        sum_k[h] += lax.dot_general(grad_scores, mine, TN, preferred_element_type=F32)
        grad_q = jnp.dot(grad_scores, keys[h], preferred_element_type=F32) * scale
        grads[here, cols] = grad_q.astype(BF16)

    @pl.when(step == pl.num_programs(0) - 1)
    def _():
        for h in range(2):
            grads[:, 160 + h * HD : 160 + (h + 1) * HD] = (sum_k[h] * scale).astype(BF16)
            grads[:, 320 + h * HD : 320 + (h + 1) * HD] = sum_v[h].astype(BF16)


def attend_back(heads, probs, mixed, grad_mixed, tile):
    rows = heads.shape[1]
    return pl.pallas_call(
        functools.partial(attend_back_kernel, HD**-0.5),
        grid=(rows // tile,),
        in_specs=[
            pl.BlockSpec((2, tile, HD), lambda i: (0, i, 0)),
            pl.BlockSpec((2, rows, HD), lambda i: (1, 0, 0)),
            pl.BlockSpec((2, rows, HD), lambda i: (2, 0, 0)),
            pl.BlockSpec((2, tile, rows), lambda i: (0, i, 0)),
            pl.BlockSpec((tile, 160), lambda i: (i, 0)),
            pl.BlockSpec((tile, 160), lambda i: (i, 0)),
        ],
        out_specs=pl.BlockSpec((rows, 480), lambda i: (0, 0)),
        out_shape=jax.ShapeDtypeStruct((rows, 480), BF16),
        scratch_shapes=[
            pltpu.VMEM((2, rows, HD), F32),
            pltpu.VMEM((2, rows, HD), F32),
        ],
        compiler_params=pltpu.CompilerParams(vmem_limit_bytes=48 << 20),
        cost_estimate=pl.CostEstimate(
            flops=16 * rows * rows * 256, bytes_accessed=16 << 20, transcendentals=0
        ),
    )(heads, heads, heads, probs, mixed, grad_mixed)


def dot(a, b):
    return jnp.dot(a, b, preferred_element_type=F32)


def dot_nt(a, b):
    return lax.dot_general(a, b, NT, preferred_element_type=F32)


def dot_tn(a, b):
    return lax.dot_general(a, b, TN, preferred_element_type=F32)


def rejoin_rows(part, y, c, zl):
    pieces = part.astype(BF16).reshape((4, part.shape[0] // 4) + part.shape[1:])
    total = pick(pieces, y).astype(F32)
    for dy in (2, 1, 3):
        total = total + along_y(pick(pieces, (y + dy) % 4), dy).astype(F32)
    total = sum_four(total.astype(BF16), along_z).astype(BF16)
    other = to_sibling(total)
    total = jnp.where(c == zl, total, other)
    blocks = [total] + [along_y(total, dy) for dy in (1, 2, 3)]
    held = place(blocks, [(y - dy) % 4 for dy in range(4)])
    return held.reshape((-1,) + held.shape[2:]).astype(F32)


def rejoin_columns(part, y, c, x, zl):
    depth = part.shape[0] // 32
    pieces = part.astype(BF16).reshape(8, 4, depth, part.shape[1])
    total = pick(pieces, y, 1).astype(F32)
    for dy in (2, 1, 3):
        total = total + along_y(pick(pieces, (y + dy) % 4, 1), dy).astype(F32)
    total = sum_four(total.astype(BF16), along_z).astype(BF16)
    near = [pick(total, 2 * x + zl)]
    near += [along_x(pick(total, 2 * ((x + dx) % 4) + zl), dx) for dx in (1, 2, 3)]
    near = jnp.stack(near)
    far = to_sibling(near)
    blocks, indices = [], []
    for dx in range(4):
        for dc, source in enumerate((near, far)):
            blocks.append(source[dx])
            indices.append(2 * ((x - dx) % 4) + (c ^ dc))
    whole = place(blocks, indices)
    blocks = [whole] + [along_y(whole, dy) for dy in (1, 2, 3)]
    return place(blocks, [(y - dy) % 4 for dy in range(4)])


def per_device(
    tokens,
    lengths,
    w_query,
    w_key,
    w_value,
    w_out,
    w_up,
    w_down,
    b_query,
    b_value,
    b_out,
    b_up,
    b_down,
    gain_attn,
    shift_attn,
    gain_ffn,
    shift_ffn,
    cotangent,
):
    rep, shard = lax.axis_index("rep"), lax.axis_index("shard")
    y, c, x, zl = rep // 4, rep % 2, shard // 2, shard % 2
    rows, width = tokens.shape[1:]

    eight = [b_query, b_value, b_out, b_down, gain_attn, shift_attn, gain_ffn, shift_ffn]
    small = jnp.zeros((16, 640), BF16)
    small = small.at[:8, :160].set(jnp.stack(eight)).at[8].set(b_up)
    known = jnp.full((8, 128), lengths[0], F32)
    (
        h1,
        heads,
        probs,
        mixed,
        attended,
        w_qkv,
        smalls,
        own,
        clip,
        out_full,
        up_mine,
        down_mine,
        top,
    ) = begin(
        tokens[0], w_query, w_key, w_value, small, w_out, w_up, w_down, cotangent[0], known
    )

    (
        middle,
        grad_middle,
        branch,
        out_parts,
        g_w_up,
        g_w_down,
        g_b_up,
        g_vectors,
        grad_mixed,
    ) = middle_part(
        attended,
        own,
        smalls,
        clip,
        out_full.reshape(width, width),
        up_mine.reshape(width, 640),
        down_mine,
        top.reshape(8 * rows, width),
    )
    g_b_up = g_b_up[0]

    def relative(blocks):
        blocks = blocks.reshape(8, rows, width)
        return [
            [pick(blocks, 2 * ((x - dx) % 4) + (c ^ dc)) for dc in range(2)] for dx in range(4)
        ]

    full = smalls[:, :8, :160].transpose(1, 0, 2).reshape(8, width).astype(F32)
    bias_down, gain_one, shift_one = full[3], full[4], full[5]
    mixed = mixed.reshape(8 * rows, 160)
    grad_qkv = attend_back(heads, probs, mixed, grad_mixed.reshape(8 * rows, 160), 384)
    result = scatter_group(relative(out_parts))
    output = cross((middle + result + bias_down).astype(BF16))
    branch_blocks = gather_group(branch)
    branch_all = place(
        [block for both in branch_blocks for block in both],
        [2 * ((x - dx) % 4) + (c ^ dc) for dx in range(4) for dc in range(2)],
    ).reshape(8 * rows, width)
    g_w_out = dot_tn(mixed, branch_all)

    grad_first = scatter_group(relative(dot_nt(grad_qkv, w_qkv).astype(BF16)))
    g_w_qkv = dot_tn(h1.reshape(8 * rows, width), grad_qkv)
    sums = jnp.sum(grad_qkv.astype(F32), axis=0)
    normed_one, inverse_one, _ = norm_fwd(own.astype(F32), gain_one, shift_one)
    grad_ln, g_gain_attn, g_shift_attn = norm_back(grad_first, normed_one, inverse_one, gain_one)
    input_grad = cross(grad_middle + grad_ln)

    grad_down = rejoin_rows(g_w_down, y, c, zl)
    grad_out = rejoin_rows(g_w_out, y, c, zl)
    grad_up = rejoin_columns(g_w_up, y, c, x, zl)
    grad_up = grad_up.transpose(0, 2, 1, 3).reshape(160, 5120).astype(F32)
    three = rejoin_columns(g_w_qkv, y, c, x, zl).reshape(4, 8, 40, 3, 160)
    three = three.transpose(3, 0, 2, 1, 4).reshape(3, 160, width).astype(F32)

    vectors = jnp.stack(
        [g_vectors[0], g_vectors[1], g_gain_attn, g_shift_attn, g_vectors[2], g_vectors[3]]
    )
    vectors = vectors + to_sibling(vectors)
    vectors = sum_four(vectors, along_x)
    sliced = jnp.concatenate([sums[:160], sums[320:], g_b_up])
    packed = jnp.concatenate([vectors.reshape(-1), sliced])
    packed = sum_four(packed, along_y)
    packed = sum_four(packed, along_z)
    sliced = packed[6 * width :]
    sliced = jnp.where(c == zl, sliced, to_sibling(sliced))
    vectors = lax.dynamic_slice_in_dim(packed[: 6 * width].reshape(6, width), shard * 160, 160, 1)
    return (
        output[None],
        input_grad[None],
        three[0],
        three[1],
        three[2],
        grad_out,
        grad_up,
        grad_down,
        sliced[:160],
        sliced[160:320],
        vectors[0],
        sliced[320:],
        vectors[1],
        vectors[2],
        vectors[3],
        vectors[4],
        vectors[5],
    )


def solution(mesh):
    by_clip, matrix, vector = P("rep", "shard", None), P("shard", None), P("shard")
    return jax.shard_map(
        per_device,
        mesh=mesh,
        in_specs=(by_clip, P("rep")) + (matrix,) * 6 + (vector,) * 9 + (by_clip,),
        out_specs=(by_clip, by_clip) + (matrix,) * 6 + (vector,) * 9,
        check_vma=False,
    )
```

time: 705 us -> 609 us (0.86)
  Pallas kernels: 30.3 us -> 215 us
  waiting for transfers between devices: 252 us -> 119 us
  starting transfers between devices: 197 us -> 116 us
  matrix products: 49.5 us -> 10.4 us
  other arithmetic: 39.7 us -> 25.3 us
  local copies, waits for them, and re-layouts: 119 us -> 110 us
    pallas_call x1 -> x2, Pallas kernels: 14.3 us -> 199 us  [the longest x1 131 us: begin(): pl.pallas_call(begin_kernel, in_specs=[VMEM] * 5 + [HBM] * 4 + [VMEM], ou...]
    ppermute x148 -> x80, waiting for transfers between devices: 252 us -> 119 us  [send(): return lax.ppermute(value, AXES, pairs(move))]
    ppermute x148 -> x80, starting transfers between devices: 197 us -> 116 us  [send(): return lax.ppermute(value, AXES, pairs(move))]
    dot_general x13 -> x0, matrix products: 19.2 us -> none  [dot(): return jnp.dot(a, b, preferred_element_type=F32)]
    dot_general x13 -> x1, matrix products: 19.7 us -> 4.2 us  [dot_nt(): return lax.dot_general(a, b, NT, preferred_element_type=F32)]
    unnamed x175 -> x87, local copies, waits for them, and re-layouts: 18.3 us -> 9.72 us
    concatenate x6 -> x0, local copies, waits for them, and re-layouts: 8.33 us -> none  [the longest x1 6.14 us: per_device(): jnp.concatenate([b_query, b_value, b_out, b_down, gain_attn, shift_attn,...]
    squeeze x6 -> x8, local copies, waits for them, and re-layouts: 2.51 us -> 10.7 us  [pick(): return lax.dynamic_index_in_dim(array, index, axis, keepdims=False)]
  transfers between devices with their start and end apart: 148 -> 80, of which waited for: 45 -> 26; matrix products, arithmetic and copies ran while one was open for 26% -> 21% of each run, Pallas kernels for 4% -> 0%
where the time goes in v2:
time: 609 us; the launch traced here: 598 us
  Pallas kernels  215 us (35%)
  waiting for transfers between devices  119 us (20%)
  starting transfers between devices  116 us (19%)
  local copies, waits for them, and re-layouts  110 us (18%)
  other arithmetic  25.3 us (4%)
  matrix products  10.4 us (2%)
    pallas_call x1, Pallas kernels, begin(): pl.pallas_call(begin_kernel, in_specs=[VMEM] * 5 + [HBM] * 4 + [VMEM], ou...  131 us
    ppermute x80, waiting for transfers between devices, send(): return lax.ppermute(value, AXES, pairs(move))  119 us
    ppermute x80, starting transfers between devices, send(): return lax.ppermute(value, AXES, pairs(move))  116 us
    pallas_call x1, Pallas kernels, middle_part(): pl.pallas_call(middle_kernel, in_specs=[VMEM] * 8, out_specs=[VMEM] * 9,...  68.3 us
    dynamic_update_slice x37, local copies, waits for them, and re-layouts, place(): held = lax.dynamic_update_index_in_dim(held, block, index, 0)  35.1 us
    pallas_call x1, Pallas kernels, attend_back(): pl.pallas_call(functools.partial(attend_back_kernel, HD ** (-0.5)), grid=...  15.2 us
    slice x2, local copies, waits for them, and re-layouts, per_device(): three[2]  14.4 us
  transfers between devices with their start and end apart: 80, of which 26 were waited for; matrix products, arithmetic and copies ran while one was open for 21% of the time, Pallas kernels for 0%

profile of v2, /device:TPU:0, one launch (start us, length us, event | category | flops | bytes accessed | tf_op | source)
XLA Modules:
  0.0 597.8 jit_solution(13924854716946311380)
XLA Ops:
  8.0 131.1 %shard_map.305 = (bf16[8,192,1280]{2,1,0:T(8,128)(2,1)}, bf16[6,1536,80]{2,1,0:T(8,128)(2,1)}, bf16[2,1536,1536]{2,1,0:T(8,128)(2,1)}, bf16[8,192,160]{2,1,0:T(8...) custom-call(bf16[192,1280]{1,0:T(8,128)(2,1)} %bitcast.221, ...), custom_call_target="tpu_custom_call" | custom-call | tf_op jit(solution)/shard_map/pallas_call | solution.py:438
  139.2 68.3 %shard_map.306 = (f32[192,1280]{1,0:T(8,128)}, f32[192,1280]{1,0:T(8,128)}, bf16[192,1280]{1,0:T(8,128)(2,1)}, bf16[1536,1280]{1,0:T(8,128)(2,1)}, bf16[1280,640...) custom-call(bf16[8,192,160]{2,1,0:T(8,128)(2,1)} %get-tuple-element., ...), custom_call_target="tpu_custom_call" | custom-call | tf_op jit(solution)/shard_map/pallas_call | solution.py:646
  210.3 15.2 %shard_map.307 = bf16[1536,480]{1,0:T(8,128)(2,1)S(1)} custom-call(bf16[6,1536,80]{2,1,0:T(8,128)(2,1)S(1)} %copy-done, bf16[6,1536,80]{2,1,0:T(8,128)(2,1)S(1)} %copy-done, bf16[6,1536,80]{2,1,0:T(8,128)(2,1)S(1)} %copy-done, bf16[2,1536,1536]{2,1,0:T(8,128)(2,1)} %get-tuple-element.75.probs, bf16[1536,160]{1,0:T(8,128)(2,1)S(1)} %bitcast.200, ...), custom_call_target="tpu_custom_call" | custom-call | flops 9663676416 | bytes 16777216 | tf_op jit(solution)/shard_map/pallas_call | solution.py:713
  225.5 3.2 convolution_convert_fusion.1
  243.9 4.2 convolution_convert_fusion
  268.9 5.8 collective-permute-done.46
  278.3 4.7 collective-permute-done.61
  283.5 4.6 collective-permute-done.59
  292.8 6.3 %collective-permute-start.21 = (bf16[8,40,480]{2,1,0:T(8,128)(2,1)S(1)}, bf16[8,40,480]{2,1,0:T(8,128)(2,1)S(1)}, u32[]{:S(2)}, u32[]{:S(2)}) collective-permute-start(bf16[8,40,480]{2,1,0:T(8,128)(2,1)S(1)} %fusion.31), channel_id=1, source_target_pairs={{0,17},{1,0},{2,19},{3,2},{4,21},{5,4},{6,23},{7,6},{8,25},{9,8},{... | collective-permute-start | bytes 921608 | tf_op jit(solution)/shard_map/ppermute | solution.py:37
  303.3 10.3 %collective-permute-done.21 = bf16[8,40,480]{2,1,0:T(8,128)(2,1)S(1)} collective-permute-done((bf16[8,40,480]{2,1,0:T(8,128)(2,1)S(1)}, bf16[8,40,480]{2,1,0:T(8,128)(2,1)S(1)}, u32[]{:S(2)}, u32[]{:S(2)}) %collective-permute-start.21) | collective-permute-done | bytes 307232 | tf_op jit(solution)/shard_map/ppermute | solution.py:37
  313.6 3.7 collective-permute-start.51
  318.9 4.0 collective-permute-start.24
  324.8 3.6 collective-permute-done.23
  336.7 3.1 collective-permute-start.62
  339.8 7.3 %collective-permute-done.50 = bf16[8,40,640]{2,1,0:T(8,128)(2,1)S(1)} collective-permute-done((bf16[8,40,640]{2,1,0:T(8,128)(2,1)S(1)}, bf16[8,40,640]{2,1,0:T(8,128)(2,1)S(1)}, u32[]{:S(2)}, u32[]{:S(2)}) %collective-permute-start.50) | collective-permute-done | bytes 409632 | tf_op jit(solution)/shard_map/ppermute | solution.py:37
  355.6 6.8 %collective-permute-done.63 = bf16[160,1280]{1,0:T(8,128)(2,1)S(1)} collective-permute-done((bf16[160,1280]{1,0:T(8,128)(2,1)S(1)}, bf16[160,1280]{1,0:T(8,128)(2,1)S(1)}, u32[]{:S(2)}, u32[]{:S(2)}) %collective-permute-start.63) | collective-permute-done | bytes 409632 | tf_op jit(solution)/shard_map/ppermute | solution.py:37
  373.9 18.3 %collective-permute-done.54 = bf16[40,640]{1,0:T(8,128)(2,1)} collective-permute-done((bf16[40,640]{1,0:T(8,128)(2,1)}, bf16[40,640]{1,0:T(8,128)(2,1)}, u32[]{:S(2)}, u32[]{:S(2)}) %collective-permute-start.54) | collective-permute-done | bytes 51232 | tf_op jit(solution)/shard_map/ppermute | solution.py:37
  394.7 3.7 collective-permute-start.34
  408.0 3.0 collective-permute-done.34
  417.8 3.9 collective-permute-done.3
  429.3 6.3 %collective-permute-start.71 = (f32[6,1280]{1,0:T(8,128)S(1)}, f32[6,1280]{1,0:T(8,128)S(1)}, u32[]{:S(2)}, u32[]{:S(2)}) collective-permute-start(f32[6,1280]{1,0:T(8,128)S(1)} %fusion.35), channel_id=1, source_target_pairs={{0,2},{1,3},{2,4},{3,5},{4,6},{5,7},{6,0},{7,1},{8,10},{9,11},{10,... | collective-permute-start | bytes 92168 | tf_op jit(solution)/shard_map/ppermute | solution.py:37
  440.6 3.4 collective-permute-done.70
  471.1 3.1 collective-permute-start.28
  474.6 5.2 collective-permute-start.7
  482.6 3.2 collective-permute-start.78
  488.5 6.8 %reshape.234 = f32[4,8,40,3,160]{4,3,2,1,0:T(4,128)} reshape(bf16[4,8,40,480]{3,2,1,0:T(8,128)(2,1)} %bitcast_dynamic-update-slice_fusion.16) | data formatting | bytes 3686400 | tf_op jit(solution)/shard_map/convert_element_type | solution.py:882
  495.3 11.6 %fusion.37 = (f32[1,4,40,8,160]{4,0,2,3,1:T(1,128)}, f32[1,4,40,8,160]{4,0,2,3,1:T(1,128)}, f32[1,4,40,8,160]{4,0,2,3,1:T(1,128)S(1)}) fusion(f32[3,4,40,8,160]{4,0,2,3,1:T(4,128)} %bitcast.202), kind=kLoop, calls=%fused_computation.138 | loop fusion | bytes 4915200 | tf_op jit(solution)/shard_map/slice | solution.py:901
  525.6 3.5 collective-permute-start.39
  538.5 16.5 %collective-permute-done.43 = bf16[40,1280]{1,0:T(8,128)(2,1)S(1)} collective-permute-done((bf16[40,1280]{1,0:T(8,128)(2,1)S(1)}, bf16[40,1280]{1,0:T(8,128)(2,1)S(1)}, u32[]{:S(2)}, u32[]{:S(2)}) %collective-permute-start.43) | collective-permute-done | bytes 102432 | tf_op jit(solution)/shard_map/ppermute | solution.py:37
  555.8 5.4 collective-permute-done.44
  565.9 3.2 collective-permute-start.58
  573.5 14.3 %collective-permute-done.58 = bf16[8,40,640]{2,0,1:T(8,128)(2,1)S(1)} collective-permute-done((bf16[8,40,640]{2,0,1:T(8,128)(2,1)S(1)}, bf16[8,40,640]{2,0,1:T(8,128)(2,1)S(1)}, u32[]{:S(2)}, u32[]{:S(2)}) %collective-permute-start.58) | collective-permute-done | bytes 409632 | tf_op jit(solution)/shard_map/ppermute | solution.py:37
  (353 shorter events, 201.4 us)
Async XLA Ops:
  233.4 27.1 %collective-permute-start.18 = (bf16[8,40,480]{2,1,0:T(8,128)(2,1)}, bf16[8,40,480]{2,1,0:T(8,128)(2,1)}, u32[]{:S(2)}, u32[]{:S(2)}) collective-permute-start(bf16[8,40,480]{2,1,0:T(8,128)(2,1)} %get-tuple-element.122), channel_id=1, source_target_pairs={{0,96},{1,97},{2,98},{3,99},{4,100},{5,101},{6,102},{7,103},{8,104... | collective-permute-start | bytes 921608 | tf_op jit(solution)/shard_map/ppermute | solution.py:37
  236.4 26.8 %collective-permute-start.17 = (bf16[8,40,480]{2,1,0:T(8,128)(2,1)}, bf16[8,40,480]{2,1,0:T(8,128)(2,1)}, u32[]{:S(2)}, u32[]{:S(2)}) collective-permute-start(bf16[8,40,480]{2,1,0:T(8,128)(2,1)} %get-tuple-element.123), channel_id=1, source_target_pairs={{0,32},{1,33},{2,34},{3,35},{4,36},{5,37},{6,38},{7,39},{8,40},{9,... | collective-permute-start | bytes 921608 | tf_op jit(solution)/shard_map/ppermute | solution.py:37
  236.4 29.3 %collective-permute-start.16 = (bf16[8,40,480]{2,1,0:T(8,128)(2,1)}, bf16[8,40,480]{2,1,0:T(8,128)(2,1)}, u32[]{:S(2)}, u32[]{:S(2)}) collective-permute-start(bf16[8,40,480]{2,1,0:T(8,128)(2,1)} %get-tuple-element.121), channel_id=1, source_target_pairs={{0,64},{1,65},{2,66},{3,67},{4,68},{5,69},{6,70},{7,71},{8,72},{9,... | collective-permute-start | bytes 921608 | tf_op jit(solution)/shard_map/ppermute | solution.py:37
  239.7 26.0 %collective-permute-start.48 = (bf16[8,40,640]{2,1,0:T(8,128)(2,1)}, bf16[8,40,640]{2,1,0:T(8,128)(2,1)}, u32[]{:S(2)}, u32[]{:S(2)}) collective-permute-start(bf16[8,40,640]{2,1,0:T(8,128)(2,1)} %get-tuple-element.119), channel_id=1, source_target_pairs={{0,96},{1,97},{2,98},{3,99},{4,100},{5,101},{6,102},{7,103},{8,104... | collective-permute-start | bytes 1228808 | tf_op jit(solution)/shard_map/ppermute | solution.py:37
  240.7 28.0 %collective-permute-start.47 = (bf16[8,40,640]{2,1,0:T(8,128)(2,1)}, bf16[8,40,640]{2,1,0:T(8,128)(2,1)}, u32[]{:S(2)}, u32[]{:S(2)}) collective-permute-start(bf16[8,40,640]{2,1,0:T(8,128)(2,1)} %get-tuple-element.120), channel_id=1, source_target_pairs={{0,32},{1,33},{2,34},{3,35},{4,36},{5,37},{6,38},{7,39},{8,40},{9,... | collective-permute-start | bytes 1228808 | tf_op jit(solution)/shard_map/ppermute | solution.py:37
  265.7 22.5 %collective-permute-start.59 = (bf16[160,1280]{1,0:T(8,128)(2,1)}, bf16[160,1280]{1,0:T(8,128)(2,1)S(1)}, u32[]{:S(2)}, u32[]{:S(2)}) collective-permute-start(bf16[160,1280]{1,0:T(8,128)(2,1)} %get-tuple-element.115), channel_id=1, source_target_pairs={{0,64},{1,65},{2,66},{3,67},{4,68},{5,69},{6,70},{7,71},{8,72},{9,... | collective-permute-start | bytes 1228808 | tf_op jit(solution)/shard_map/ppermute | solution.py:37
  268.8 54.8 %collective-permute-start.29 = (bf16[192,1280]{1,0:T(8,128)(2,1)S(1)}, bf16[192,1280]{1,0:T(8,128)(2,1)S(1)}, u32[]{:S(2)}, u32[]{:S(2)}) collective-permute-start(bf16[192,1280]{1,0:T(8,128)(2,1)S(1)} %copy-done.10), channel_id=1, source_target_pairs={{0,8},{1,9},{2,10},{3,11},{4,12},{5,13},{6,14},{7,15},{8,0},{9,1},... | collective-permute-start | bytes 1474568 | tf_op jit(solution)/shard_map/ppermute | solution.py:37
  274.6 54.8 %collective-permute-start.30 = (bf16[192,1280]{1,0:T(8,128)(2,1)S(1)}, bf16[192,1280]{1,0:T(8,128)(2,1)S(1)}, u32[]{:S(2)}, u32[]{:S(2)}) collective-permute-start(bf16[192,1280]{1,0:T(8,128)(2,1)S(1)} %copy-done.10), channel_id=1, source_target_pairs={{0,2},{1,3},{2,4},{3,5},{4,6},{5,7},{6,0},{7,1},{8,10},{9,11},{10,... | collective-permute-start | bytes 1474568 | tf_op jit(solution)/shard_map/ppermute | solution.py:37
  292.8 20.8 %collective-permute-start.21 = (bf16[8,40,480]{2,1,0:T(8,128)(2,1)S(1)}, bf16[8,40,480]{2,1,0:T(8,128)(2,1)S(1)}, u32[]{:S(2)}, u32[]{:S(2)}) collective-permute-start(bf16[8,40,480]{2,1,0:T(8,128)(2,1)S(1)} %fusion.31), channel_id=1, source_target_pairs={{0,17},{1,0},{2,19},{3,2},{4,21},{5,4},{6,23},{7,6},{8,25},{9,8},{... | collective-permute-start | bytes 921608 | tf_op jit(solution)/shard_map/ppermute | solution.py:37
  313.6 23.1 %collective-permute-start.51 = (bf16[8,40,640]{2,1,0:T(8,128)(2,1)S(1)}, bf16[8,40,640]{2,1,0:T(8,128)(2,1)S(1)}, u32[]{:S(2)}, u32[]{:S(2)}) collective-permute-start(bf16[8,40,640]{2,1,0:T(8,128)(2,1)S(1)} %fusion.28), channel_id=1, source_target_pairs={{0,17},{1,0},{2,19},{3,2},{4,21},{5,4},{6,23},{7,6},{8,25},{9,8},{... | collective-permute-start | bytes 1228808 | tf_op jit(solution)/shard_map/ppermute | solution.py:37
  324.6 22.5 %collective-permute-start.50 = (bf16[8,40,640]{2,1,0:T(8,128)(2,1)S(1)}, bf16[8,40,640]{2,1,0:T(8,128)(2,1)S(1)}, u32[]{:S(2)}, u32[]{:S(2)}) collective-permute-start(bf16[8,40,640]{2,1,0:T(8,128)(2,1)S(1)} %fusion.28), channel_id=1, source_target_pairs={{0,1},{1,16},{2,3},{3,18},{4,5},{5,20},{6,7},{7,22},{8,9},{9,24},{... | collective-permute-start | bytes 1228808 | tf_op jit(solution)/shard_map/ppermute | solution.py:37
  328.8 26.7 %collective-permute-start.64 = (bf16[160,1280]{1,0:T(8,128)(2,1)S(1)}, bf16[160,1280]{1,0:T(8,128)(2,1)S(1)}, u32[]{:S(2)}, u32[]{:S(2)}) collective-permute-start(bf16[160,1280]{1,0:T(8,128)(2,1)S(1)} %fusion.25), channel_id=1, source_target_pairs={{0,17},{1,0},{2,19},{3,2},{4,21},{5,4},{6,23},{7,6},{8,25},{9,8},{... | collective-permute-start | bytes 1228808 | tf_op jit(solution)/shard_map/ppermute | solution.py:37
  330.9 31.5 %collective-permute-start.63 = (bf16[160,1280]{1,0:T(8,128)(2,1)S(1)}, bf16[160,1280]{1,0:T(8,128)(2,1)S(1)}, u32[]{:S(2)}, u32[]{:S(2)}) collective-permute-start(bf16[160,1280]{1,0:T(8,128)(2,1)S(1)} %fusion.25), channel_id=1, source_target_pairs={{0,1},{1,16},{2,3},{3,18},{4,5},{5,20},{6,7},{7,22},{8,9},{9,24},{... | collective-permute-start | bytes 1228808 | tf_op jit(solution)/shard_map/ppermute | solution.py:37
  336.7 28.1 %collective-permute-start.62 = (bf16[160,1280]{1,0:T(8,128)(2,1)S(1)}, bf16[160,1280]{1,0:T(8,128)(2,1)S(1)}, u32[]{:S(2)}, u32[]{:S(2)}) collective-permute-start(bf16[160,1280]{1,0:T(8,128)(2,1)S(1)} %fusion.25), channel_id=1, source_target_pairs={{0,16},{1,17},{2,18},{3,19},{4,20},{5,21},{6,22},{7,23},{8,24},{9,... | collective-permute-start | bytes 1228808 | tf_op jit(solution)/shard_map/ppermute | solution.py:37
  355.5 39.2 %collective-permute-start.14 = (bf16[192,1280]{1,0:T(8,128)(2,1)S(1)}, bf16[192,1280]{1,0:T(8,128)(2,1)}, u32[]{:S(2)}, u32[]{:S(2)}) collective-permute-start(bf16[192,1280]{1,0:T(8,128)(2,1)S(1)} %copy-done.14), channel_id=1, source_target_pairs={{0,8},{1,9},{2,10},{3,11},{4,12},{5,13},{6,14},{7,15},{8,0},{9,1},... | collective-permute-start | bytes 1474568 | tf_op jit(solution)/shard_map/ppermute | solution.py:37
  362.4 36.0 %collective-permute-start.13 = (bf16[192,1280]{1,0:T(8,128)(2,1)}, bf16[192,1280]{1,0:T(8,128)(2,1)}, u32[]{:S(2)}, u32[]{:S(2)}) collective-permute-start(bf16[192,1280]{1,0:T(8,128)(2,1)} %get-tuple-element.102), channel_id=1, source_target_pairs={{0,2},{1,3},{2,4},{3,5},{4,6},{5,7},{6,0},{7,1},{8,10},{9,11},{10,... | collective-permute-start | bytes 1474568 | tf_op jit(solution)/shard_map/ppermute | solution.py:37
  364.8 33.6 %collective-permute-start.11 = (bf16[192,1280]{1,0:T(8,128)(2,1)}, bf16[192,1280]{1,0:T(8,128)(2,1)}, u32[]{:S(2)}, u32[]{:S(2)}) collective-permute-start(bf16[192,1280]{1,0:T(8,128)(2,1)} %get-tuple-element.103), channel_id=1, source_target_pairs={{0,6},{1,7},{2,0},{3,1},{4,2},{5,3},{6,4},{7,5},{8,14},{9,15},{10,... | collective-permute-start | bytes 1474568 | tf_op jit(solution)/shard_map/ppermute | solution.py:37
  365.8 33.7 %collective-permute-start.9 = (bf16[192,1280]{1,0:T(8,128)(2,1)}, bf16[192,1280]{1,0:T(8,128)(2,1)}, u32[]{:S(2)}, u32[]{:S(2)}) collective-permute-start(bf16[192,1280]{1,0:T(8,128)(2,1)} %get-tuple-element.101), channel_id=1, source_target_pairs={{0,4},{1,5},{2,6},{3,7},{4,0},{5,1},{6,2},{7,3},{8,12},{9,13},{10,... | collective-permute-start | bytes 1474568 | tf_op jit(solution)/shard_map/ppermute | solution.py:37
  367.4 24.9 %collective-permute-start.54 = (bf16[40,640]{1,0:T(8,128)(2,1)}, bf16[40,640]{1,0:T(8,128)(2,1)}, u32[]{:S(2)}, u32[]{:S(2)}) collective-permute-start(bf16[40,640]{1,0:T(8,128)(2,1)} %get-tuple-element.125), channel_id=1, source_target_pairs={{0,6},{1,7},{2,0},{3,1},{4,2},{5,3},{6,4},{7,5},{8,14},{9,15},{10,... | collective-permute-start | bytes 153608 | tf_op jit(solution)/shard_map/ppermute | solution.py:37
  413.0 67.8 %collective-permute-start.26 = (bf16[8,40,480]{2,1,0:T(8,128)(2,1)}, bf16[8,40,480]{2,1,0:T(8,128)(2,1)}, u32[]{:S(2)}, u32[]{:S(2)}) collective-permute-start(bf16[8,40,480]{2,1,0:T(8,128)(2,1)} %slice_dynamic-update-slice_fusion), channel_id=1, source_target_pairs={{0,32},{1,33},{2,34},{3,35},{4,36},{5,37},{6,38},{7,39},{8,40},{9,... | collective-permute-start | bytes 921608 | tf_op jit(solution)/shard_map/ppermute | solution.py:37
  415.7 67.0 %collective-permute-start.27 = (bf16[8,40,480]{2,1,0:T(8,128)(2,1)}, bf16[8,40,480]{2,1,0:T(8,128)(2,1)}, u32[]{:S(2)}, u32[]{:S(2)}) collective-permute-start(bf16[8,40,480]{2,1,0:T(8,128)(2,1)} %slice_dynamic-update-slice_fusion), channel_id=1, source_target_pairs={{0,64},{1,65},{2,66},{3,67},{4,68},{5,69},{6,70},{7,71},{8,72},{9,... | collective-permute-start | bytes 921608 | tf_op jit(solution)/shard_map/ppermute | solution.py:37
  446.5 21.1 %collective-permute-start.75 = (f32[8640]{0:T(1024)}, f32[8640]{0:T(1024)}, u32[]{:S(2)}, u32[]{:S(2)}) collective-permute-start(f32[8640]{0:T(1024)} %concatenate.7), channel_id=1, source_target_pairs={{0,96},{1,97},{2,98},{3,99},{4,100},{5,101},{6,102},{7,103},{8,104... | collective-permute-start | bytes 103688 | tf_op jit(solution)/shard_map/ppermute | solution.py:37
  474.6 62.6 %collective-permute-start.65 = (bf16[160,1280]{1,0:T(8,128)(2,1)S(1)}, bf16[160,1280]{1,0:T(8,128)(2,1)S(1)}, u32[]{:S(2)}, u32[]{:S(2)}) collective-permute-start(bf16[160,1280]{1,0:T(8,128)(2,1)S(1)} %copy-done.7), channel_id=1, source_target_pairs={{0,8},{1,9},{2,10},{3,11},{4,12},{5,13},{6,14},{7,15},{8,0},{9,1},... | collective-permute-start | bytes 1228808 | tf_op jit(solution)/shard_map/ppermute | solution.py:37
  474.6 95.5 %collective-permute-start.7 = (bf16[192,1280]{1,0:T(8,128)(2,1)}, bf16[192,1280]{1,0:T(8,128)(2,1)}, u32[]{:S(2)}, u32[]{:S(2)}) collective-permute-start(bf16[192,1280]{1,0:T(8,128)(2,1)} %fusion.19), channel_id=1, source_target_pairs={{0,0},{1,8},{2,2},{3,10},{4,4},{5,12},{6,6},{7,14},{8,1},{9,9},{10... | collective-permute-start | bytes 1474568 | tf_op jit(solution)/shard_map/ppermute | solution.py:37
  480.8 41.5 %collective-permute-start.77 = (f32[8640]{0:T(1024)S(1)}, f32[8640]{0:T(1024)S(1)}, u32[]{:S(2)}, u32[]{:S(2)}) collective-permute-start(f32[8640]{0:T(1024)S(1)} %add_add_fusion.2), channel_id=1, source_target_pairs={{0,1},{1,16},{2,3},{3,18},{4,5},{5,20},{6,7},{7,22},{8,9},{9,24},{... | collective-permute-start | bytes 103688 | tf_op jit(solution)/shard_map/ppermute | solution.py:37
  482.6 41.1 %collective-permute-start.78 = (f32[8640]{0:T(1024)S(1)}, f32[8640]{0:T(1024)S(1)}, u32[]{:S(2)}, u32[]{:S(2)}) collective-permute-start(f32[8640]{0:T(1024)S(1)} %add_add_fusion.2), channel_id=1, source_target_pairs={{0,17},{1,0},{2,19},{3,2},{4,21},{5,4},{6,23},{7,6},{8,25},{9,8},{... | collective-permute-start | bytes 103688 | tf_op jit(solution)/shard_map/ppermute | solution.py:37
  487.6 36.8 %collective-permute-start.76 = (f32[8640]{0:T(1024)S(1)}, f32[8640]{0:T(1024)S(1)}, u32[]{:S(2)}, u32[]{:S(2)}) collective-permute-start(f32[8640]{0:T(1024)S(1)} %add_add_fusion.2), channel_id=1, source_target_pairs={{0,16},{1,17},{2,18},{3,19},{4,20},{5,21},{6,22},{7,23},{8,24},{9,... | collective-permute-start | bytes 103688 | tf_op jit(solution)/shard_map/ppermute | solution.py:37
  529.1 65.6 %collective-permute-start.15 = (f32[192,1280]{1,0:T(8,128)}, f32[192,1280]{1,0:T(8,128)S(1)}, u32[]{:S(2)}, u32[]{:S(2)}) collective-permute-start(f32[192,1280]{1,0:T(8,128)} %fusion.9), channel_id=1, source_target_pairs={{0,0},{1,8},{2,2},{3,10},{4,4},{5,12},{6,6},{7,14},{8,1},{9,9},{10... | collective-permute-start | bytes 2949128 | tf_op jit(solution)/shard_map/ppermute | solution.py:37
  531.0 39.1 %collective-permute-start.56 = (bf16[8,40,640]{2,0,1:T(8,128)(2,1)S(1)}, bf16[8,40,640]{2,0,1:T(8,128)(2,1)S(1)}, u32[]{:S(2)}, u32[]{:S(2)}) collective-permute-start(bf16[8,40,640]{2,0,1:T(8,128)(2,1)S(1)} %dynamic_update_slice.158), channel_id=1, source_target_pairs={{0,32},{1,33},{2,34},{3,35},{4,36},{5,37},{6,38},{7,39},{8,40},{9,... | collective-permute-start | bytes 1228808 | tf_op jit(solution)/shard_map/ppermute | solution.py:37
  534.1 37.5 %collective-permute-start.57 = (bf16[8,40,640]{2,0,1:T(8,128)(2,1)S(1)}, bf16[8,40,640]{2,0,1:T(8,128)(2,1)S(1)}, u32[]{:S(2)}, u32[]{:S(2)}) collective-permute-start(bf16[8,40,640]{2,0,1:T(8,128)(2,1)S(1)} %dynamic_update_slice.158), channel_id=1, source_target_pairs={{0,64},{1,65},{2,66},{3,67},{4,68},{5,69},{6,70},{7,71},{8,72},{9,... | collective-permute-start | bytes 1228808 | tf_op jit(solution)/shard_map/ppermute | solution.py:37
  565.9 21.9 %collective-permute-start.58 = (bf16[8,40,640]{2,0,1:T(8,128)(2,1)S(1)}, bf16[8,40,640]{2,0,1:T(8,128)(2,1)S(1)}, u32[]{:S(2)}, u32[]{:S(2)}) collective-permute-start(bf16[8,40,640]{2,0,1:T(8,128)(2,1)S(1)} %dynamic_update_slice.158), channel_id=1, source_target_pairs={{0,96},{1,97},{2,98},{3,99},{4,100},{5,101},{6,102},{7,103},{8,104... | collective-permute-start | bytes 1228808 | tf_op jit(solution)/shard_map/ppermute | solution.py:37
  571.6 21.1 %collective-permute-start.68 = (bf16[160,1280]{1,0:T(8,128)(2,1)S(1)}, bf16[160,1280]{1,0:T(8,128)(2,1)S(1)}, u32[]{:S(2)}, u32[]{:S(2)}) collective-permute-start(bf16[160,1280]{1,0:T(8,128)(2,1)S(1)} %get-tuple-element.92), channel_id=1, source_target_pairs={{0,96},{1,97},{2,98},{3,99},{4,100},{5,101},{6,102},{7,103},{8,104... | collective-permute-start | bytes 1228808 | tf_op jit(solution)/shard_map/ppermute | solution.py:37
  (90 other events, 1112.2 us)

commit v3 on v2

--- a/solution.py
+++ b/solution.py
@@ -476,16 +476,17 @@
     up_mine,
     down_mine,
     top,
-    middle,
+    result,
     grad_middle,
     branch,
-    out_parts,
+    out_sums,
     g_up,
     g_down,
     g_up_bias,
     g_vectors,
     grad_mixed,
     vectors,
+    middle,
     second,
     masked,
     active,
@@ -494,6 +495,8 @@
     over,
     sums,
     arrived,
+    out_parts,
+    out_over,
     joined,
     by_head,
     sent,
@@ -522,7 +525,11 @@
     second[mine, :] = (normalised()[0] * vectors[6:7, :] + vectors[7:8, :]).astype(BF16)
     wait()
 
-    near, pass_on, swap, add = (net.reserve(4) for _ in range(4))
+    near, pass_on, swap, add, out_swap = (net.reserve(4) for _ in range(5))
+
+    def out_copy(dx, to_x):
+        source = out_parts.at[aligned(2 * to_x + 1 - c, rows)]
+        return net.copy(out_swap + dx, source, out_over.at[to_x], net.device(0, 1))
 
     def near_copy(dx):
         return net.copy(near + dx, second.at[mine], second.at[mine], net.device(dx))
@@ -571,6 +578,7 @@
         out_parts[here, :] = jnp.dot(
             active[here, :], down_mine[...], preferred_element_type=F32
         ).astype(BF16)
+        out_copy(dx, to_x).start()
         swap_copy(dx, to_x).wait_recv()
 
         @pl.when(dx != 0)
@@ -590,6 +598,14 @@
             active[:, cols], masked[...], TN, preferred_element_type=F32
         ).astype(BF16)
 
+    for dx in range(4):
+        to_x = (x - dx + 4) % 4
+        out_copy(dx, to_x).wait_recv()
+        kept = out_parts[aligned(2 * to_x + c, rows), :].astype(F32) + out_over[to_x].astype(F32)
+        if dx:
+            out_sums[to_x] = kept.astype(BF16)
+        else:
+            result[...] = middle[...] + kept + vectors[3:4, :]
     g_up_bias[...] = jnp.sum(hidden[...].astype(F32), axis=0, keepdims=True)
     grad_second = parts[mine, :].astype(F32) + over[x].astype(F32)
     for dx in (1, 3, 2):
@@ -628,6 +644,7 @@
         to_x = (x - dx + 4) % 4
         pass_copy(dx, 2 * to_x + c).wait_send()
         swap_copy(dx, to_x).wait_send()
+        out_copy(dx, to_x).wait_send()
         if dx:
             near_copy(dx).wait_send()
             add_copy(dx, to_x).wait_send()
@@ -651,7 +668,7 @@
             shape(rows, width, dtype=F32),
             shape(rows, width, dtype=F32),
             shape(rows, width),
-            shape(8 * rows, width),
+            shape(4, rows, width),
             shape(width, 640),
             shape(640, width),
             shape(1, 640, dtype=F32),
@@ -660,6 +677,7 @@
         ],
         scratch_shapes=[
             buffer(8, width, dtype=F32),
+            buffer(rows, width, dtype=F32),
             buffer(8 * rows, width),
             buffer(8 * rows, width),
             buffer(8 * rows, 640),
@@ -668,116 +686,767 @@
             buffer(4, rows, width),
             buffer(4, rows, width),
             buffer(4, rows, width),
+            buffer(8 * rows, width),
+            buffer(4, rows, width),
             buffer(rows, width),
             buffer(8, rows, 160),
         ]
-        + scratch_for(24),
+        + scratch_for(32),
         compiler_params=pltpu.CompilerParams(
             collective_id=1, has_side_effects=True, vmem_limit_bytes=60 << 20
         ),
     )(attended, own, smalls, clip, out_full, up_mine, down_mine, top)
 
 
-def attend_back_kernel(scale, queries, keys, values, probs, mixed, grad_mixed, grads, sum_k, sum_v):
-    step = pl.program_id(0)
-    tile = queries.shape[1]
-
-    @pl.when(step == 0)
+def piece_start(index):
+    return pl.multiple_of(48 * index - 32 * (index // 3), 16)
+
+
+def column_flow(net, source, r1, s1, r2, s2, planes, landed, place_of):
+    y, z, x, c = net.y, 2 * net.zh + net.zl, net.x, net.c
+    b1, b2, b3, b4, b5 = (net.reserve(4) for _ in range(5))
+    sibling = net.device(0, 1)
+
+    def copy_1(d):
+        rows = pl.ds(piece_start((y + d) % 4), 48)
+        return net.copy(b1 + d, source.at[:, rows, :], r1.at[d], net.device(dy=d))
+
+    mine = pltpu.make_async_copy(
+        source.at[:, pl.ds(piece_start(y), 48), :], r1.at[0], net.still.at[b1]
+    )
+
+    def copy_2(d):
+        part = s1.at[pl.ds(2 * ((z + d) % 4), 2)]
+        return net.copy(b2 + d, part, r2.at[d], net.device(dz=d))
+
+    def copy_3(d):
+        return net.copy(b3 + d, s2.at[(z + d) % 2], planes.at[z], net.device(dz=d))
+
+    def copy_4(d):
+        target = place_of(landed, 2 * x + c)
+        return net.copy(b4 + d, planes.at[(x + d) % 4], target, net.device(d))
+
+    def copy_5(d):
+        here = place_of(landed, 2 * ((x - d + 4) % 4) + c)
+        return net.copy(b5 + d, here, here, sibling)
+
+    def first():
+        mine.start()
+        for d in (2, 1, 3):
+            copy_1(d).start()
+
+    def second():
+        mine.wait()
+        for d in (1, 2, 3):
+            copy_1(d).wait_recv()
+        total = r1[0].astype(F32)
+        for d in (1, 2, 3):
+            total = total + r1[d].astype(F32)
+        s1[...] = total.astype(BF16)
+        for d in (2, 1, 3):
+            copy_2(d).start()
+
+    def third():
+        total = s1[pl.ds(2 * z, 2)].astype(F32)
+        for d in (1, 2, 3):
+            copy_2(d).wait_recv()
+            total = total + r2[d].astype(F32)
+        s2[...] = total.astype(BF16)
+        for d in (2, 1, 3):
+            copy_3(d).start()
+        planes[z] = s2[z % 2]
+
+    def fourth():
+        for d in (1, 2, 3):
+            copy_3(d).wait_recv()
+        for d in (2, 1, 3):
+            copy_4(d).start()
+        place_of(landed, 2 * x + c)[...] = planes[x]
+        copy_5(0).start()
+
+    def fifth():
+        for d in (1, 3, 2):
+            copy_4(d).wait_recv()
+            copy_5(d).start()
+        for d in range(4):
+            copy_5(d).wait_recv()
+
+    def sent():
+        for d in range(4):
+            copy_5(d).wait_send()
+        for d in (1, 2, 3):
+            for copy in (copy_1, copy_2, copy_3, copy_4):
+                copy(d).wait_send()
+
+    return first, second, third, fourth, fifth, sent
+
+
+def share_over_y(net, whole, final, half_of):
+    y = net.y
+    near, over = net.reserve(4), net.reserve(4)
+    own = pltpu.make_async_copy(whole, final.at[y], net.still.at[near])
+
+    def copy(d):
+        return net.copy(near + d, half_of(whole), half_of(final.at[y]), net.device(dy=d))
+
+    def forward(d):
+        here = half_of(final.at[(y - d + 4) % 4])
+        return net.copy(over + d, here, here, net.device(0, 1))
+
+    def first():
+        own.start()
+        for d in (2, 1, 3):
+            copy(d).start()
+
+    def second():
+        for d in (1, 3, 2):
+            copy(d).wait_recv()
+            forward(d).start()
+
+    def third():
+        own.wait()
+        for d in (1, 2, 3):
+            forward(d).wait_recv()
+            forward(d).wait_send()
+            copy(d).wait_send()
+
+    return first, second, third
+
+
+def four_way(net, base, held, position, device_of):
+    def copy(d):
+        return net.copy(base + d, held.at[position], held.at[position], device_of(d))
+
+    def go():
+        for d in (2, 1, 3):
+            copy(d).start()
+
+    def total():
+        for d in (1, 2, 3):
+            copy(d).wait_recv()
+        return (held[0].astype(F32) + held[1].astype(F32)) + (
+            held[2].astype(F32) + held[3].astype(F32)
+        )
+
+    def sent():
+        for d in (1, 2, 3):
+            copy(d).wait_send()
+
+    return go, total, sent
+
+
+def finish_kernel(
+    heads,
+    mixed,
+    grad_mixed,
+    w_qkv,
+    own,
+    smalls,
+    result,
+    grad_middle,
+    branch,
+    out_sums,
+    g_up_bias,
+    g_vectors,
+    probs,
+    h1,
+    g_up,
+    g_down,
+    hb_out,
+    vec_out,
+    output,
+    input_grad,
+    fin_up,
+    fin_qkv,
+    fin_down,
+    fin_out,
+    branch_all,
+    tall,
+    prob_buf,
+    grads,
+    sum_k,
+    sum_v,
+    give,
+    over,
+    sums,
+    arrived,
+    out_arrived,
+    final_rows,
+    final_grad,
+    up_r1,
+    up_s1,
+    up_r2,
+    up_s2,
+    up_planes,
+    up_landed,
+    g_qkv,
+    qkv_r1,
+    qkv_s1,
+    qkv_r2,
+    qkv_s2,
+    qkv_planes,
+    qkv_landed,
+    qkv_rows,
+    down_r1,
+    down_s1,
+    down_r2,
+    down_l3,
+    down_p,
+    g_out,
+    out_r1,
+    out_z,
+    out_t,
+    head_y,
+    head_z,
+    head_sib,
+    vec_cut,
+    vec_1,
+    vec_1s,
+    vec_2,
+    vec_3,
+    vectors,
+    sent,
+    got,
+    still,
+):
+    net = Net(sent, got, still)
+    x, y, c, zl, me = net.x, net.y, net.c, net.zl, net.me
+    z = 2 * net.zh + zl
+    rows, width = own.shape
+    sibling = net.device(0, 1)
+    wait = net.greet(
+        [net.device(dx, dc) for dx in range(4) for dc in range(2) if dx or dc]
+        + [net.device(dy=d) for d in (1, 2, 3)]
+        + [net.device(dz=d) for d in (1, 2, 3)]
+        + [(y * 4 + net.zh * 2 + 1 - c, 2 * x + 1 - zl)]
+    )
+
+    tile = 2 * rows
+    slots = net.reserve(2)
+
+    def load_probs(i):
+        slot = i % 2
+        return pltpu.make_async_copy(
+            probs.at[:, aligned(i, tile), :], prob_buf.at[slot], still.at[slots + slot]
+        )
+
+    load_probs(0).start()
+    load_h1 = pltpu.make_async_copy(h1, tall, still.at[net.reserve(1)])
+    load_h1.start()
+    own_branch = pltpu.make_async_copy(
+        branch, branch_all.at[aligned(me, rows)], still.at[net.reserve(1)]
+    )
+    own_branch.start()
+    for block in range(8):
+        vectors[:, 160 * block : 160 * block + 160] = smalls[block, :8, :160].astype(F32)
+    sum_k[...] = jnp.zeros_like(sum_k)
+    sum_v[...] = jnp.zeros_like(sum_v)
+
+    up = column_flow(
+        net,
+        g_up,
+        up_r1,
+        up_s1,
+        up_r2,
+        up_s2,
+        up_planes,
+        up_landed,
+        lambda ref, hb: ref.at[:, pl.ds(pl.multiple_of(hb * 640, 128), 640)],
+    )
+    three = column_flow(
+        net,
+        g_qkv,
+        qkv_r1,
+        qkv_s1,
+        qkv_r2,
+        qkv_s2,
+        qkv_planes,
+        qkv_landed,
+        lambda ref, hb: ref.at[hb],
+    )
+    up_share = share_over_y(
+        net,
+        up_landed,
+        fin_up,
+        lambda ref: ref.at[:, pl.ds(pl.multiple_of(c * 2560, 128), 2560)],
+    )
+    three_share = share_over_y(
+        net,
+        qkv_rows,
+        fin_qkv,
+        lambda ref: ref.at[:, :, pl.ds(pl.multiple_of(c * 640, 128), 640)],
+    )
+
+    d1, d2, d4, d5 = (net.reserve(4) for _ in range(4))
+    d3_go, _, d3_sent = four_way(net, d3 := net.reserve(4), down_l3, y, lambda d: net.device(dy=d))
+    down_mine = pltpu.make_async_copy(
+        g_down.at[aligned(z, 160)], down_r1.at[0], still.at[d1]
+    )
+
+    def down_1(d):
+        return net.copy(d1 + d, g_down.at[aligned((z + d) % 4, 160)], down_r1.at[d], net.device(dz=d))
+
+    def down_2(d):
+        part = down_s1.at[pl.ds(piece_start((y + d) % 4), 48)]
+        return net.copy(d2 + d, part, down_r2.at[d], net.device(dy=d))
+
+    def down_4(k, source_z):
+        to_z = c + 2 * k
+        return pltpu.make_async_remote_copy(
+            src_ref=down_p,
+            dst_ref=fin_down.at[aligned(source_z, 160)],
+            send_sem=sent.at[d4 + k],
+            recv_sem=got.at[d4 + source_z],
+            device_id=(y * 4 + to_z // 2 * 2 + c, 2 * x + to_z % 2),
+            device_id_type=MESH,
+        )
+
+    down_local = pltpu.make_async_copy(down_p, fin_down.at[aligned(z, 160)], still.at[d4])
+
+    def down_5(source_z):
+        here = fin_down.at[aligned(source_z, 160)]
+        return net.copy(d5 + source_z, here, here, sibling)
+
+    e1, e3, e4 = (net.reserve(4) for _ in range(3))
+    out_go, out_total, out_sent = four_way(
+        net, net.reserve(4), out_z, z, lambda d: net.device(dz=d)
+    )
+
+    def out_1(d):
+        part = g_out.at[pl.ds(piece_start((y + d) % 4), 48)]
+        return net.copy(e1 + d, part, out_r1.at[d], net.device(dy=d))
+
+    def out_3(d):
+        return net.copy(e3 + d, out_t, fin_out.at[y], net.device(dy=d))
+
+    out_local = pltpu.make_async_copy(out_t, fin_out.at[y], still.at[e3])
+
+    def out_4(source_y):
+        return net.copy(e4 + source_y, fin_out.at[source_y], fin_out.at[source_y], sibling)
+
+    near, pass_on, swap, add, out_add = (net.reserve(4) for _ in range(5))
+
+    def near_copy(dx):
+        return net.copy(near + dx, branch, branch_all.at[aligned(me, rows)], net.device(dx))
+
+    def pass_copy(dx):
+        here = branch_all.at[aligned(2 * ((x - dx + 4) % 4) + c, rows)]
+        return net.copy(pass_on + dx, here, here, sibling)
+
+    def swap_copy(dx, to_x):
+        return net.copy(swap + dx, give.at[to_x], over.at[to_x], sibling)
+
+    def add_copy(dx, to_x):
+        return net.copy(add + dx, sums.at[to_x], arrived.at[dx], net.device(4 - dx))
+
+    def out_add_copy(dx):
+        to_x = (x - dx + 4) % 4
+        return net.copy(out_add + dx, out_sums.at[to_x], out_arrived.at[dx], net.device(4 - dx))
+
+    wait()
+    for dx in (1, 3, 2):
+        near_copy(dx).start()
+    up[0]()
+    down_mine.start()
+    for d in (2, 1, 3):
+        down_1(d).start()
+
+    @pl.loop(0, 4)
+    def _(i):
+        @pl.when(i < 3)
+        def _():
+            load_probs(i + 1).start()
+
+        load_probs(i).wait()
+        here = aligned(i, tile)
+        for h in range(2):
+            cols = slice(h * HD, (h + 1) * HD)
+            back = jnp.concatenate([grad_mixed[2 * i, :, cols], grad_mixed[2 * i + 1, :, cols]])
+            seen = jnp.concatenate([mixed[2 * i, :, cols], mixed[2 * i + 1, :, cols]])
+            low = prob_buf[i % 2, h]
+            row_total = jnp.sum(back.astype(F32) * seen.astype(F32), axis=-1, keepdims=True)
+            grad_probs = lax.dot_general(back, heads[4 + h], NT, preferred_element_type=F32)
+            grad_scores = (low.astype(F32) * (grad_probs - row_total)).astype(BF16)
+            sum_v[h] += lax.dot_general(low, back, TN, preferred_element_type=F32)
+            sum_k[h] += lax.dot_general(
+                grad_scores, heads[h, here, :], TN, preferred_element_type=F32
+            )
+            grad_q = jnp.dot(grad_scores, heads[2 + h], preferred_element_type=F32)
+            grads[here, cols] = (grad_q * HD**-0.5).astype(BF16)
+
+    for h in range(2):
+        grads[:, 160 + h * HD : 160 + (h + 1) * HD] = (sum_k[h] * HD**-0.5).astype(BF16)
+        grads[:, 320 + h * HD : 320 + (h + 1) * HD] = sum_v[h].astype(BF16)
+
+    @pl.loop(0, 4)
+    def _(k):
+        dx = order(k)
+        dx = jnp.where(k == 3, 0, dx)
+        to_x = (x - dx + 4) % 4
+        part = lax.dot_general(
+            grads[aligned(to_x, tile), :], w_qkv[...], NT, preferred_element_type=F32
+        )
+        low, high = part[:rows], part[rows:]
+        give[to_x] = jnp.where(c == 0, high, low).astype(BF16)
+        swap_copy(dx, to_x).start()
+        kept = jnp.where(c == 0, low, high)
+        swap_copy(dx, to_x).wait_recv()
+        kept = kept + over[to_x].astype(F32)
+
+        @pl.when(dx != 0)
+        def _():
+            sums[to_x] = kept.astype(BF16)
+            add_copy(dx, to_x).start()
+
+        @pl.when(dx == 0)
+        def _():
+            final_grad[...] = kept
+
+    for dx in (1, 3, 2):
+        out_add_copy(dx).start()
+    load_h1.wait()
+
+    @pl.loop(0, 2)
+    def _(i):
+        cols = pl.ds(pl.multiple_of(i * 640, 128), 640)
+        made = lax.dot_general(tall[:, cols], grads[...], TN, preferred_element_type=F32)
+        g_qkv[pl.ds(4 * i, 4)] = made.astype(BF16).reshape(4, 160, 480)
+
+    three[0]()
+    head_y[y] = jnp.zeros((8, 640), F32)
+    head_y[y, 0:1, :] = g_up_bias[...]
+    column_sums = jnp.sum(grads[...].astype(F32), axis=0, keepdims=True)
+    head_y[y, 1:2, :160] = column_sums[:, :160]
+    head_y[y, 2:3, :160] = column_sums[:, 320:]
+    head_y_go, head_y_total, head_y_sent = four_way(
+        net, net.reserve(4), head_y, y, lambda d: net.device(dy=d)
+    )
+    head_y_go()
+
+    own_branch.wait()
+    pass_copy(0).start()
+    for dx in (1, 3, 2):
+        near_copy(dx).wait_recv()
+        pass_copy(dx).start()
+
+    up[1]()
+    down_mine.wait()
+    total = down_r1[0].astype(F32)
+    for d in (1, 2, 3):
+        down_1(d).wait_recv()
+        total = total + down_r1[d].astype(F32)
+    down_s1[...] = total.astype(BF16)
+    for d in (2, 1, 3):
+        down_2(d).start()
+
+    for dx in range(4):
+        pass_copy(dx).wait_recv()
+        pass_copy(dx).wait_send()
+    load_branch = pltpu.make_async_copy(branch_all, tall, still.at[net.reserve(1)])
+    load_branch.start()
+    load_branch.wait()
+    seen = jnp.concatenate([mixed[block] for block in range(8)])
+    g_out[...] = lax.dot_general(seen, tall[...], TN, preferred_element_type=F32).astype(BF16)
+    for d in (2, 1, 3):
+        out_1(d).start()
+
+    up[2]()
+    total = down_s1[pl.ds(piece_start(y), 48), :].astype(F32)
+    for d in (1, 2, 3):
+        down_2(d).wait_recv()
+        total = total + down_r2[d].astype(F32)
+    down_l3[y] = total.astype(BF16)
+    d3_go()
+
+    grad_first = final_grad[...]
+    for dx in (1, 3, 2):
+        add_copy(dx, (x - dx + 4) % 4).wait_recv()
+        grad_first = grad_first + arrived[dx].astype(F32)
+    values = own[...].astype(F32)
+    center = values - jnp.mean(values, axis=-1, keepdims=True)
+    inverse = lax.rsqrt(jnp.mean(center * center, axis=-1, keepdims=True) + EPS)
+    normed = center * inverse
+    scaled = grad_first * vectors[4:5, :]
+    back = inverse * (
+        scaled
+        - jnp.mean(scaled, axis=-1, keepdims=True)
+        - normed * jnp.mean(scaled * normed, axis=-1, keepdims=True)
+    )
+    final_grad[...] = grad_middle[...] + back
+    grad_arrived, grad_left = net.cross(final_grad, input_grad)
+    gain = jnp.sum(grad_first * normed, axis=0, keepdims=True)
+    shift = jnp.sum(grad_first, axis=0, keepdims=True)
+    for block in range(8):
+        cols = slice(160 * block, 160 * block + 160)
+        here = vec_cut.at[block // 2, block % 2]
+        here[0:4, :] = g_vectors[:, cols]
+        here[4:5, :] = gain[:, cols]
+        here[5:6, :] = shift[:, cols]
+        here[6:8, :] = jnp.zeros((2, 160), F32)
+    v1 = net.reserve(8)
+
+    def vec_copy(dx, dc):
+        return net.copy(
+            v1 + 2 * dx + dc, vec_cut.at[(x + dx) % 4], vec_1.at[me], net.device(dx, dc)
+        )
+
+    others = [(dx, dc) for dx in (2, 1, 3, 0) for dc in (1, 0) if dx or dc]
+    for dx, dc in others:
+        vec_copy(dx, dc).start()
+    vec_1[me] = vec_cut[x]
+
+    total = g_out[pl.ds(piece_start(y), 48), :].astype(F32)
+    for d in (1, 2, 3):
+        out_1(d).wait_recv()
+        total = total + out_r1[d].astype(F32)
+    out_z[z] = total.astype(BF16)
+    out_go()
+    up[3]()
+    for d in (1, 2, 3):
+        net.copy(d3 + d, down_l3.at[y], down_l3.at[y], net.device(dy=d)).wait_recv()
+    for i in range(3):
+        down_p[48 * i : 48 * i + 48, :] = down_l3[i]
+    down_p[144:160, :] = down_l3[3, 32:48, :]
+    for k in range(2):
+
+        @pl.when(c + 2 * k != z)
+        def _():
+            down_4(k, z).start()
+
+    @pl.when(c == zl)
     def _():
-        sum_k[...] = jnp.zeros_like(sum_k)
-        sum_v[...] = jnp.zeros_like(sum_v)
-
-    here = pl.ds(pl.multiple_of(step * tile, tile), tile)
-    for h in range(2):
-        cols = slice(h * HD, (h + 1) * HD)
-        mine, back, low = queries[h], grad_mixed[:, cols], probs[h]
-        row_total = jnp.sum(
-            back.astype(F32) * mixed[:, cols].astype(F32), axis=-1, keepdims=True
-        )
-        grad_probs = lax.dot_general(back, values[h], NT, preferred_element_type=F32)
-        grad_scores = (low.astype(F32) * (grad_probs - row_total)).astype(BF16)
-        sum_v[h] += lax.dot_general(low, back, TN, preferred_element_type=F32)
-        sum_k[h] += lax.dot_general(grad_scores, mine, TN, preferred_element_type=F32)
-        grad_q = jnp.dot(grad_scores, keys[h], preferred_element_type=F32) * scale
-        grads[here, cols] = grad_q.astype(BF16)
-
-    @pl.when(step == pl.num_programs(0) - 1)
+        down_local.start()
+
+    three[1]()
+    head_z[z] = head_y_total()
+    head_z_go, head_z_total, head_z_sent = four_way(
+        net, net.reserve(4), head_z, z, lambda d: net.device(dz=d)
+    )
+    head_z_go()
+    for dx, dc in others:
+        vec_copy(dx, dc).wait_recv()
+    total = vec_1[0]
+    for block in range(1, 8):
+        total = total + vec_1[block]
+    vec_1s[...] = total
+    v2 = net.reserve(4)
+
+    def vec_z(d):
+        return net.copy(v2 + d, vec_1s.at[(z + d) % 2], vec_2.at[z], net.device(dz=d))
+
+    for d in (2, 1, 3):
+        vec_z(d).start()
+    vec_2[z] = vec_1s[zl]
+    out_t[...] = out_total().astype(BF16)
+
+    @pl.when(c == zl)
     def _():
-        for h in range(2):
-            grads[:, 160 + h * HD : 160 + (h + 1) * HD] = (sum_k[h] * scale).astype(BF16)
-            grads[:, 320 + h * HD : 320 + (h + 1) * HD] = sum_v[h].astype(BF16)
-
-
-def attend_back(heads, probs, mixed, grad_mixed, tile):
-    rows = heads.shape[1]
+        out_local.start()
+        for d in (2, 1, 3):
+            out_3(d).start()
+
+    up[4]()
+    up_share[0]()
+    three[2]()
+
+    total = result[...]
+    for dx in (1, 3, 2):
+        out_add_copy(dx).wait_recv()
+        total = total + out_arrived[dx].astype(F32)
+    final_rows[...] = total.astype(BF16)
+    output_arrived, output_left = net.cross(final_rows, output)
+
+    head_sib[0] = head_z_total()
+    head_copy = net.go(head_sib.at[0], head_sib.at[1], sibling)
+    for d in (1, 2, 3):
+        vec_z(d).wait_recv()
+    vec_3[y] = (vec_2[0] + vec_2[1]) + (vec_2[2] + vec_2[3])
+    vec_y_go, vec_y_total, vec_y_sent = four_way(
+        net, net.reserve(4), vec_3, y, lambda d: net.device(dy=d)
+    )
+    vec_y_go()
+
+    @pl.when(c == zl)
+    def _():
+        down_local.wait()
+        down_5(z).start()
+        for d in (1, 2, 3):
+            source_z = (z + d) % 4
+            down_4(0, source_z).wait_recv()
+            down_5(source_z).start()
+        out_local.wait()
+        out_4(y).start()
+        for d in (1, 2, 3):
+            out_3(d).wait_recv()
+            out_4((y + 4 - d) % 4).start()
+
+    three[3]()
+    three[4]()
+    for block in range(8):
+        cols = slice(160 * block, 160 * block + 160)
+        for k in range(3):
+            qkv_rows[k, :, cols] = qkv_landed[block, :, 160 * k : 160 * k + 160]
+    three_share[0]()
+    up_share[1]()
+    head_copy.wait_recv()
+    hb_out[...] = jnp.where(c == zl, head_sib[0], head_sib[1])
+    vec_out[...] = vec_y_total()
+    three_share[1]()
+
+    @pl.when(c == zl)
+    def _():
+        for i in range(4):
+            down_5(i).wait_send()
+            out_4(i).wait_send()
+        for d in (1, 2, 3):
+            out_3(d).wait_send()
+
+    @pl.when(c != zl)
+    def _():
+        for i in range(4):
+            down_5(i).wait_recv()
+            out_4(i).wait_recv()
+
+    for k in range(2):
+
+        @pl.when(c + 2 * k != z)
+        def _():
+            down_4(k, z).wait_send()
+
+    up_share[2]()
+    three_share[2]()
+    grad_arrived()
+    grad_left()
+    output_arrived()
+    output_left()
+    for done in (up[5], three[5], d3_sent, out_sent, head_y_sent, head_z_sent, vec_y_sent):
+        done()
+    for d in (1, 2, 3):
+        down_1(d).wait_send()
+        down_2(d).wait_send()
+        out_1(d).wait_send()
+        vec_z(d).wait_send()
+        near_copy(d).wait_send()
+        add_copy(d, (x - d + 4) % 4).wait_send()
+        out_add_copy(d).wait_send()
+    for d in range(4):
+        swap_copy(d, (x - d + 4) % 4).wait_send()
+    for dx, dc in others:
+        vec_copy(dx, dc).wait_send()
+    net.all_sent()
+
+
+def finish(
+    heads,
+    mixed,
+    grad_mixed,
+    w_qkv,
+    own,
+    smalls,
+    result,
+    grad_middle,
+    branch,
+    out_sums,
+    g_up_bias,
+    g_vectors,
+    probs,
+    h1,
+    g_up,
+    g_down,
+):
+    rows, width = own.shape
+
+    def shape(*dims, dtype=BF16):
+        return jax.ShapeDtypeStruct(dims, dtype)
+
+    def buffer(*dims, dtype=BF16):
+        return pltpu.VMEM(dims, dtype)
+
+    def column_buffers(columns):
+        return [
+            buffer(4, 8, 48, columns),
+            buffer(8, 48, columns),
+            buffer(4, 2, 48, columns),
+            buffer(2, 48, columns),
+            buffer(4, 48, columns),
+        ]
+
     return pl.pallas_call(
-        functools.partial(attend_back_kernel, HD**-0.5),
-        grid=(rows // tile,),
-        in_specs=[
-            pl.BlockSpec((2, tile, HD), lambda i: (0, i, 0)),
-            pl.BlockSpec((2, rows, HD), lambda i: (1, 0, 0)),
-            pl.BlockSpec((2, rows, HD), lambda i: (2, 0, 0)),
-            pl.BlockSpec((2, tile, rows), lambda i: (0, i, 0)),
-            pl.BlockSpec((tile, 160), lambda i: (i, 0)),
-            pl.BlockSpec((tile, 160), lambda i: (i, 0)),
+        finish_kernel,
+        in_specs=[VMEM] * 12 + [HBM] * 4,
+        out_specs=[VMEM] * 2 + [HBM] * 7,
+        out_shape=[
+            shape(8, 640, dtype=F32),
+            shape(8, 160, dtype=F32),
+            shape(rows, width),
+            shape(rows, width, dtype=F32),
+            shape(4, 48, 5120),
+            shape(4, 3, 48, width),
+            shape(640, width),
+            shape(4, 48, width),
+            shape(8 * rows, width),
         ],
-        out_specs=pl.BlockSpec((rows, 480), lambda i: (0, 0)),
-        out_shape=jax.ShapeDtypeStruct((rows, 480), BF16),
         scratch_shapes=[
-            pltpu.VMEM((2, rows, HD), F32),
-            pltpu.VMEM((2, rows, HD), F32),
-        ],
-        compiler_params=pltpu.CompilerParams(vmem_limit_bytes=48 << 20),
-        cost_estimate=pl.CostEstimate(
-            flops=16 * rows * rows * 256, bytes_accessed=16 << 20, transcendentals=0
+            buffer(8 * rows, width),
+            buffer(2, 2, 2 * rows, 8 * rows),
+            buffer(8 * rows, 480),
+            buffer(2, 8 * rows, HD, dtype=F32),
+            buffer(2, 8 * rows, HD, dtype=F32),
+            buffer(4, rows, width),
+            buffer(4, rows, width),
+            buffer(4, rows, width),
+            buffer(4, rows, width),
+            buffer(4, rows, width),
+            buffer(rows, width),
+            buffer(rows, width, dtype=F32),
+        ]
+        + column_buffers(640)
+        + [buffer(48, 5120), buffer(8, 160, 480)]
+        + column_buffers(480)
+        + [
+            buffer(8, 48, 480),
+            buffer(3, 48, width),
+            buffer(4, 160, width),
+            buffer(160, width),
+            buffer(4, 48, width),
+            buffer(4, 48, width),
+            buffer(160, width),
+            buffer(160, width),
+            buffer(4, 48, width),
+            buffer(4, 48, width),
+            buffer(48, width),
+            buffer(4, 8, 640, dtype=F32),
+            buffer(4, 8, 640, dtype=F32),
+            buffer(2, 8, 640, dtype=F32),
+            buffer(4, 2, 8, 160, dtype=F32),
+            buffer(8, 2, 8, 160, dtype=F32),
+            buffer(2, 8, 160, dtype=F32),
+            buffer(4, 8, 160, dtype=F32),
+            buffer(4, 8, 160, dtype=F32),
+            buffer(8, width, dtype=F32),
+        ]
+        + scratch_for(192),
+        compiler_params=pltpu.CompilerParams(
+            collective_id=2, has_side_effects=True, vmem_limit_bytes=62 << 20
         ),
-    )(heads, heads, heads, probs, mixed, grad_mixed)
-
-
-def dot(a, b):
-    return jnp.dot(a, b, preferred_element_type=F32)
-
-
-def dot_nt(a, b):
-    return lax.dot_general(a, b, NT, preferred_element_type=F32)
-
-
-def dot_tn(a, b):
-    return lax.dot_general(a, b, TN, preferred_element_type=F32)
-
-
-def rejoin_rows(part, y, c, zl):
-    pieces = part.astype(BF16).reshape((4, part.shape[0] // 4) + part.shape[1:])
-    total = pick(pieces, y).astype(F32)
-    for dy in (2, 1, 3):
-        total = total + along_y(pick(pieces, (y + dy) % 4), dy).astype(F32)
-    total = sum_four(total.astype(BF16), along_z).astype(BF16)
-    other = to_sibling(total)
-    total = jnp.where(c == zl, total, other)
-    blocks = [total] + [along_y(total, dy) for dy in (1, 2, 3)]
-    held = place(blocks, [(y - dy) % 4 for dy in range(4)])
-    return held.reshape((-1,) + held.shape[2:]).astype(F32)
-
-
-def rejoin_columns(part, y, c, x, zl):
-    depth = part.shape[0] // 32
-    pieces = part.astype(BF16).reshape(8, 4, depth, part.shape[1])
-    total = pick(pieces, y, 1).astype(F32)
-    for dy in (2, 1, 3):
-        total = total + along_y(pick(pieces, (y + dy) % 4, 1), dy).astype(F32)
-    total = sum_four(total.astype(BF16), along_z).astype(BF16)
-    near = [pick(total, 2 * x + zl)]
-    near += [along_x(pick(total, 2 * ((x + dx) % 4) + zl), dx) for dx in (1, 2, 3)]
-    near = jnp.stack(near)
-    far = to_sibling(near)
-    blocks, indices = [], []
-    for dx in range(4):
-        for dc, source in enumerate((near, far)):
-            blocks.append(source[dx])
-            indices.append(2 * ((x - dx) % 4) + (c ^ dc))
-    whole = place(blocks, indices)
-    blocks = [whole] + [along_y(whole, dy) for dy in (1, 2, 3)]
-    return place(blocks, [(y - dy) % 4 for dy in range(4)])
+    )(
+        heads,
+        mixed,
+        grad_mixed,
+        w_qkv,
+        own,
+        smalls,
+        result,
+        grad_middle,
+        branch,
+        out_sums,
+        g_up_bias,
+        g_vectors,
+        probs,
+        h1,
+        g_up,
+        g_down,
+    )
 
 
 def per_device(
@@ -827,13 +1496,13 @@
     )
 
     (
-        middle,
+        result,
         grad_middle,
         branch,
-        out_parts,
-        g_w_up,
-        g_w_down,
-        g_b_up,
+        out_sums,
+        g_up,
+        g_down,
+        g_up_bias,
         g_vectors,
         grad_mixed,
     ) = middle_part(
@@ -846,71 +1515,46 @@
         down_mine,
         top.reshape(8 * rows, width),
     )
-    g_b_up = g_b_up[0]
-
-    def relative(blocks):
-        blocks = blocks.reshape(8, rows, width)
-        return [
-            [pick(blocks, 2 * ((x - dx) % 4) + (c ^ dc)) for dc in range(2)] for dx in range(4)
-        ]
-
-    full = smalls[:, :8, :160].transpose(1, 0, 2).reshape(8, width).astype(F32)
-    bias_down, gain_one, shift_one = full[3], full[4], full[5]
-    mixed = mixed.reshape(8 * rows, 160)
-    grad_qkv = attend_back(heads, probs, mixed, grad_mixed.reshape(8 * rows, 160), 384)
-    result = scatter_group(relative(out_parts))
-    output = cross((middle + result + bias_down).astype(BF16))
-    branch_blocks = gather_group(branch)
-    branch_all = place(
-        [block for both in branch_blocks for block in both],
-        [2 * ((x - dx) % 4) + (c ^ dc) for dx in range(4) for dc in range(2)],
-    ).reshape(8 * rows, width)
-    g_w_out = dot_tn(mixed, branch_all)
-
-    grad_first = scatter_group(relative(dot_nt(grad_qkv, w_qkv).astype(BF16)))
-    g_w_qkv = dot_tn(h1.reshape(8 * rows, width), grad_qkv)
-    sums = jnp.sum(grad_qkv.astype(F32), axis=0)
-    normed_one, inverse_one, _ = norm_fwd(own.astype(F32), gain_one, shift_one)
-    grad_ln, g_gain_attn, g_shift_attn = norm_back(grad_first, normed_one, inverse_one, gain_one)
-    input_grad = cross(grad_middle + grad_ln)
-
-    grad_down = rejoin_rows(g_w_down, y, c, zl)
-    grad_out = rejoin_rows(g_w_out, y, c, zl)
-    grad_up = rejoin_columns(g_w_up, y, c, x, zl)
-    grad_up = grad_up.transpose(0, 2, 1, 3).reshape(160, 5120).astype(F32)
-    three = rejoin_columns(g_w_qkv, y, c, x, zl).reshape(4, 8, 40, 3, 160)
-    three = three.transpose(3, 0, 2, 1, 4).reshape(3, 160, width).astype(F32)
-
-    vectors = jnp.stack(
-        [g_vectors[0], g_vectors[1], g_gain_attn, g_shift_attn, g_vectors[2], g_vectors[3]]
-    )
-    vectors = vectors + to_sibling(vectors)
-    vectors = sum_four(vectors, along_x)
-    sliced = jnp.concatenate([sums[:160], sums[320:], g_b_up])
-    packed = jnp.concatenate([vectors.reshape(-1), sliced])
-    packed = sum_four(packed, along_y)
-    packed = sum_four(packed, along_z)
-    sliced = packed[6 * width :]
-    sliced = jnp.where(c == zl, sliced, to_sibling(sliced))
-    vectors = lax.dynamic_slice_in_dim(packed[: 6 * width].reshape(6, width), shard * 160, 160, 1)
+    hb_out, vec_out, output, input_grad, fin_up, fin_qkv, fin_down, fin_out, _ = finish(
+        heads,
+        mixed,
+        grad_mixed,
+        w_qkv,
+        own,
+        smalls,
+        result,
+        grad_middle,
+        branch,
+        out_sums,
+        g_up_bias,
+        g_vectors,
+        probs,
+        h1.reshape(8 * rows, width),
+        g_up.reshape(8, 160, 640),
+        g_down,
+    )
+
+    def whole(pieces):
+        return jnp.concatenate([pieces[0], pieces[1], pieces[2], pieces[3, 32:]]).astype(F32)
+
     return (
         output[None],
         input_grad[None],
-        three[0],
-        three[1],
-        three[2],
-        grad_out,
-        grad_up,
-        grad_down,
-        sliced[:160],
-        sliced[160:320],
-        vectors[0],
-        sliced[320:],
-        vectors[1],
-        vectors[2],
-        vectors[3],
-        vectors[4],
-        vectors[5],
+        whole(fin_qkv[:, 0]),
+        whole(fin_qkv[:, 1]),
+        whole(fin_qkv[:, 2]),
+        whole(fin_out),
+        whole(fin_up),
+        fin_down.astype(F32),
+        hb_out[1, :160],
+        hb_out[2, :160],
+        vec_out[0],
+        hb_out[0],
+        vec_out[1],
+        vec_out[4],
+        vec_out[5],
+        vec_out[2],
+        vec_out[3],
     )
 
 

time: 609 us -> 354 us (0.58); the launches traced: 598 us -> 352 us
  waiting for transfers between devices: 119 us -> 0 us
  starting transfers between devices: 116 us -> 0 us
  Pallas kernels: 215 us -> 328 us
  local copies, waits for them, and re-layouts: 110 us -> 16.3 us
  other arithmetic: 25.3 us -> 7.18 us
  matrix products: 10.4 us -> 0 us
    ppermute x80 -> x0, waiting for transfers between devices: 119 us -> none  [send(): return lax.ppermute(value, AXES, pairs(move))]
    ppermute x80 -> x0, starting transfers between devices: 116 us -> none  [send(): return lax.ppermute(value, AXES, pairs(move))]
    pallas_call x1, Pallas kernels: 15.2 us -> 128 us  [finish(): pl.pallas_call(finish_kernel, in_specs=[VMEM] * 12 + [HBM] * 4, out_specs...]
    dynamic_update_slice x37 -> x0, local copies, waits for them, and re-layouts: 35.1 us -> none  [place(): held = lax.dynamic_update_index_in_dim(held, block, index, 0)]
    slice x17 -> x2, local copies, waits for them, and re-layouts: 21.7 us -> 2.85 us  [the longest x1 1.51 us: per_device(): hb_out[2, :160]]
    squeeze x11 -> x8, local copies, waits for them, and re-layouts: 19 us -> 4.48 us  [the longest x3 2.66 us: whole(): pieces[0]]
    dot_general x3 -> x0, matrix products: 10.4 us -> none  [the longest x2 6.15 us: dot_tn(): return lax.dot_general(a, b, TN, preferred_element_type=F32)]
    convert_element_type x15 -> x5, other arithmetic: 17 us -> 7.18 us  [the longest x4 5.21 us: whole(): jnp.concatenate([pieces[0], pieces[1], pieces[2], pieces[3, 32:]])]
  transfers between devices with their start and end apart: 80 -> 0, of which waited for: 26 -> 0; matrix products, arithmetic and copies ran while one was open for 21% -> 0% of each run, Pallas kernels for 0% -> 0%
where the time goes in v3:
time: 354 us; the launch traced here: 352 us
  Pallas kernels  328 us (93%)
  local copies, waits for them, and re-layouts  16.3 us (5%)
  other arithmetic  7.18 us (2%)
    pallas_call x1, Pallas kernels, begin(): pl.pallas_call(begin_kernel, in_specs=[VMEM] * 5 + [HBM] * 4 + [VMEM], ou...  131 us
    pallas_call x1, Pallas kernels, finish(): pl.pallas_call(finish_kernel, in_specs=[VMEM] * 12 + [HBM] * 4, out_specs...  128 us
    pallas_call x1, Pallas kernels, middle_part(): pl.pallas_call(middle_kernel, in_specs=[VMEM] * 8, out_specs=[VMEM] * 9,...  68.7 us

profile of v3, /device:TPU:0, one launch (start us, length us, event | category | flops | bytes accessed | tf_op | source)
XLA Modules:
  0.0 352.4 jit_solution(3926940347101097266)
XLA Ops:
  1.3 0.7 stack.27
  2.0 0.7 stack.28
  2.6 0.7 stack.29
  3.3 0.7 stack.30
  3.9 0.7 stack.31
  4.6 0.7 stack.32
  5.3 0.7 stack.33
  5.9 0.7 stack.34
  6.6 0.7 reshape.124
  7.3 0.6 broadcast_in_dim.10.length
  7.9 0.0 copy-start.4
  7.9 0.6 copy-done.4
  8.5 131.1 %shard_map.305 = (bf16[8,192,1280]{2,1,0:T(8,128)(2,1)}, bf16[6,1536,80]{2,1,0:T(8,128)(2,1)}, bf16[2,1536,1536]{2,1,0:T(8,128)(2,1)}, bf16[8,192,160]{2,1,0:T(8...) custom-call(bf16[192,1280]{1,0:T(8,128)(2,1)} %bitcast.70, ...), custom_call_target="tpu_custom_call" | custom-call | tf_op jit(solution)/shard_map/pallas_call | solution.py:438
  139.7 68.7 %shard_map.306 = (f32[192,1280]{1,0:T(8,128)}, f32[192,1280]{1,0:T(8,128)}, bf16[192,1280]{1,0:T(8,128)(2,1)}, bf16[4,192,1280]{2,1,0:T(8,128)(2,1)}, bf16[1280,...) custom-call(bf16[8,192,160]{2,1,0:T(8,128)(2,1)} %get-tuple-element., ...), custom_call_target="tpu_custom_call" | custom-call | tf_op jit(solution)/shard_map/pallas_call | solution.py:663
  208.4 127.7 %shard_map.307 = (f32[8,640]{1,0:T(8,128)}, f32[8,160]{1,0:T(8,128)}, bf16[192,1280]{1,0:T(8,128)(2,1)}, f32[192,1280]{1,0:T(8,128)}, bf16[4,48,5120]{2,1,0:T(8,...) custom-call(bf16[6,1536,80]{2,1,0:T(8,128)(2,1)} %get-tuple-element., ...), custom_call_target="tpu_custom_call" | custom-call | tf_op jit(solution)/shard_map/pallas_call | solution.py:1374
  336.1 1.3 slice_reduce_fusion
  337.4 1.5 fusion
  339.0 0.8 slice_bitcast_fusion.22
  339.7 1.2 slice_bitcast_fusion.9
  340.9 0.9 slice_bitcast_fusion.6
  341.8 1.4 slice_bitcast_fusion.2
  343.3 0.0 copy-done
  343.3 0.1 slice_bitcast_fusion.12
  343.4 0.1 slice_bitcast_fusion.3
  343.5 0.9 maximum_convert_fusion.3
  344.4 0.9 maximum_convert_fusion.2
  345.4 1.3 maximum_convert_fusion.1
  346.7 2.1 maximum_convert_fusion
  348.7 0.0 copy-done.1
  348.7 2.0 convert_element_type.31
  350.7 0.8 copy.39
  351.5 0.9 copy.40
  (11 shorter events, 0.1 us)
Async XLA Ops:
  7.9 0.6 copy-start.4
  339.7 3.5 copy-start
  346.7 2.1 copy-start.1
  348.7 2.0 copy-start.3
  348.7 2.7 copy-start.2

commit v4 on v3

--- a/solution.py
+++ b/solution.py
@@ -1,5 +1,3 @@
-import functools
-
 import jax
 import jax.numpy as jnp
 from jax import lax
@@ -7,106 +5,12 @@
 from jax.experimental.pallas import tpu as pltpu
 from jax.sharding import PartitionSpec as P
 
-H = 16
 HD = 80
 EPS = 1e-05
-AXES = ("rep", "shard")
 F32 = jnp.float32
 BF16 = jnp.bfloat16
 NT = (((1,), (1,)), ((), ()))
 TN = (((0,), (0,)), ((), ()))
-
-
-def flat_index(y, zh, c, x, zl):
-    return ((y % 4) * 4 + (zh % 2) * 2 + c % 2) * 8 + (x % 4) * 2 + zl % 2
-
-
-def pairs(move):
-    found = []
-    for y in range(4):
-        for zh in range(2):
-            for c in range(2):
-                for x in range(4):
-                    for zl in range(2):
-                        here = flat_index(y, zh, c, x, zl)
-                        found.append((here, flat_index(*move(y, zh, c, x, zl))))
-    return found
-
-
-def send(value, move):
-    return lax.ppermute(value, AXES, pairs(move))
-
-
-def along_x(value, dx):
-    return send(value, lambda y, zh, c, x, zl: (y, zh, c, x + dx, zl))
-
-
-def along_y(value, dy):
-    return send(value, lambda y, zh, c, x, zl: (y + dy, zh, c, x, zl))
-
-
-def along_z(value, dz):
-    def move(y, zh, c, x, zl):
-        z = (2 * zh + zl + dz) % 4
-        return (y, z // 2, c, x, z % 2)
-
-    return send(value, move)
-
-
-def to_sibling(value):
-    return send(value, lambda y, zh, c, x, zl: (y, zh, c + 1, x, zl))
-
-
-def cross(value):
-    return send(value, lambda y, zh, c, x, zl: (y, zh, zl, x, c))
-
-
-def gather_group(own):
-    near = [own] + [along_x(own, dx) for dx in (1, 2, 3)]
-    return [[block, to_sibling(block)] for block in near]
-
-
-def scatter_group(parts):
-    total = None
-    for dx in (2, 1, 3, 0):
-        both = parts[dx][0].astype(F32) + to_sibling(parts[dx][1]).astype(F32)
-        if dx > 0:
-            both = along_x(both.astype(BF16), -dx).astype(F32)
-        total = both if total is None else total + both
-    return total
-
-
-def sum_four(value, along):
-    one, two, three = (along(value, step).astype(F32) for step in (1, 2, 3))
-    return (value.astype(F32) + two) + (one + three)
-
-
-def place(blocks, indices):
-    held = jnp.zeros((len(blocks),) + blocks[0].shape, blocks[0].dtype)
-    for block, index in zip(blocks, indices):
-        held = lax.dynamic_update_index_in_dim(held, block, index, 0)
-    return held
-
-
-def pick(array, index, axis=0):
-    return lax.dynamic_index_in_dim(array, index, axis, keepdims=False)
-
-
-def norm_fwd(values, gain, shift):
-    center = values - jnp.mean(values, axis=-1, keepdims=True)
-    inverse = lax.rsqrt(jnp.mean(center * center, axis=-1, keepdims=True) + EPS)
-    normed = center * inverse
-    return (normed, inverse, normed * gain + shift)
-
-
-def norm_back(grad_rows, normed, inverse, gain):
-    scaled = grad_rows * gain
-    grad_in = inverse * (
-        scaled
-        - jnp.mean(scaled, axis=-1, keepdims=True)
-        - normed * jnp.mean(scaled * normed, axis=-1, keepdims=True)
-    )
-    return (grad_in, jnp.sum(grad_rows * normed, axis=0), jnp.sum(grad_rows, axis=0))
 
 
 MESH = pl.DeviceIdType.MESH
@@ -217,6 +121,7 @@
     w_key,
     w_value,
     small,
+    up_bias,
     w_out,
     w_up,
     w_down,
@@ -229,12 +134,14 @@
     attended,
     w_qkv,
     smalls,
+    bias_up,
     own,
     clip,
     out_full,
     up_mine,
     down_mine,
     top,
+    out_own,
     gathered,
     cut,
     lens,
@@ -244,17 +151,19 @@
     still,
 ):
     net = Net(sent, got, still)
-    x, c, zl, me, shard = net.x, net.c, net.zl, net.me, net.shard
+    x, y, c, zh, zl, me, shard = net.x, net.y, net.c, net.zh, net.zl, net.me, net.shard
     rows, width = tokens.shape
     plane = [net.device(dx, dc) for dx in range(4) for dc in range(2) if dx or dc]
     across = [net.in_pair(dx, 1) for dx in range(4)]
-    everyone = plane + across + [(net.y * 4 + net.zh * 2 + 1 - c, 2 * x + 1 - zl)]
-    wait = net.greet(everyone)
+    rings = [net.device(dy=d) for d in (1, 2, 3)] + [net.device(dz=d) for d in (1, 2, 3)]
+    wait = net.greet(plane + across + rings + [(y * 4 + zh * 2 + 1 - c, 2 * x + 1 - zl)])
     for block in range(8):
         cols = slice(160 * block, 160 * block + 160)
-        cut[block, :, :160] = w_query[:, cols]
-        cut[block, :, 160:320] = w_key[:, cols]
-        cut[block, :, 320:] = w_value[:, cols]
+        for half in range(2):
+            part = slice(80 * half, 80 * half + 80)
+            cut[block, half, :, :160] = w_query[part, cols]
+            cut[block, half, :, 160:320] = w_key[part, cols]
+            cut[block, half, :, 320:] = w_value[part, cols]
     wait()
 
     token_arrived, token_left = net.cross(tokens, gathered.at[2 * x + zl])
@@ -263,6 +172,33 @@
     def token_send(k, source):
         dx = order(k)
         return net.copy(base + dx, source, gathered.at[me], net.device(dx))
+
+    cut_near, cut_ring, up_near, up_ring = (net.reserve(4) for _ in range(4))
+
+    def cut_copy(d):
+        source = cut.at[2 * ((x + d) % 4) + c, zh]
+        return net.copy(cut_near + d, source, w_qkv.at[x, zl, zh], net.device(d))
+
+    def cut_share(d):
+        here = w_qkv.at[:, zl, zh]
+        return net.copy(cut_ring + d, here, here, net.device(dz=d))
+
+    def up_part(index):
+        cols = pl.ds(pl.multiple_of(index * 640, 128), 640)
+        return w_up.at[aligned(zh, 80), cols]
+
+    def up_copy(d):
+        source = up_part(2 * ((x + d) % 4) + c)
+        return net.copy(up_near + d, source, up_mine.at[x, zl, zh], net.device(d))
+
+    def up_share(d):
+        here = up_mine.at[:, zl, zh]
+        return net.copy(up_ring + d, here, here, net.device(dz=d))
+
+    up_local = pltpu.make_async_copy(up_part(me), up_mine.at[x, zl, zh], still.at[up_near])
+
+    for d in (2, 1, 3):
+        cut_copy(d).start()
 
     @pl.when(c == zl)
     def _():
@@ -282,12 +218,9 @@
     for dx in (0, 1, 3, 2):
         for dz in range(2):
             if dx or dz:
-                device = net.in_pair(dx, dz)
-                arriving.append(net.go(small, smalls.at[shard], device))
-                target = 2 * ((x + dx) % 4) + c
-                arriving.append(net.go(cut.at[target], w_qkv.at[aligned(shard, 160)], device))
+                arriving.append(net.go(small, smalls.at[shard], net.in_pair(dx, dz)))
     smalls[shard] = small[...]
-    w_qkv[aligned(shard, 160)] = cut[me]
+    w_qkv[x, zl, zh] = cut[me, zh]
     token_arrived()
 
     @pl.when(c != zl)
@@ -297,18 +230,43 @@
 
     sibling = net.device(0, 1)
     own_over = net.go(gathered.at[me], gathered.at[me], sibling)
-    out_arrived, out_left = net.cross(w_out, out_full.at[2 * x + zl])
+    for d in (1, 3, 2):
+        cut_copy(d).wait_recv()
+    for d in (2, 1, 3):
+        cut_share(d).start()
+    up_local.start()
+    for d in (2, 1, 3):
+        up_copy(d).start()
+    bias_arrived, bias_left = net.cross(up_bias, bias_up)
     top_arrived, top_left = net.cross(cotangent, top.at[2 * x + zl])
-    down_arrived, down_left = net.cross(w_down, down_mine)
+    out_arrived, out_left = net.cross(w_out, out_own)
+
+    down_index, down_ring = net.reserve(1), net.reserve(4)
+    down_cross = net.copy(
+        down_index, w_down.at[aligned(y, 160)], down_mine.at[aligned(y, 160)], net.partner()
+    )
+    down_local = pltpu.make_async_copy(w_down, down_mine, still.at[down_index])
+
+    def down_share(d):
+        here = down_mine.at[aligned(y, 160)]
+        return net.copy(down_ring + d, here, here, net.device(dy=d))
+
+    @pl.when(c == zl)
+    def _():
+        down_local.start()
+
+    @pl.when(c != zl)
+    def _():
+        down_cross.start()
+
     own[...] = gathered[me]
-
     for copy in arriving:
         copy.wait_recv()
     for block in range(8):
-        vectors[:, 160 * block : 160 * block + 160] = smalls[block, :8, :160].astype(F32)
+        vectors[:, 160 * block : 160 * block + 160] = smalls[block, :8, :].astype(F32)
     gain, shift = vectors[4:5, :], vectors[5:6, :]
-    bias_q = smalls[me, 0:1, :160].astype(F32)
-    bias_v = smalls[me, 1:2, :160].astype(F32)
+    bias_q = smalls[me, 0:1, :].astype(F32)
+    bias_v = smalls[me, 1:2, :].astype(F32)
 
     def project(slot):
         values = gathered[slot].astype(F32)
@@ -316,7 +274,7 @@
         inverse = lax.rsqrt(jnp.mean(center * center, axis=-1, keepdims=True) + EPS)
         normed = (center * inverse * gain + shift).astype(BF16)
         h1[slot] = normed
-        made = jnp.dot(normed, w_qkv[...], preferred_element_type=F32)
+        made = jnp.dot(normed, w_qkv[...].reshape(width, 480), preferred_element_type=F32)
         here = aligned(slot, rows)
         for h in range(2):
             cols = slice(h * HD, (h + 1) * HD)
@@ -326,9 +284,65 @@
                 made[:, 320 + h * HD : 400 + h * HD] + bias_v[:, cols]
             ).astype(BF16)
 
+    top_near, top_over, out_near, out_ring, out_over = (net.reserve(4) for _ in range(5))
+
+    def top_copy(d):
+        return net.copy(top_near + d, top.at[me], top.at[me], net.device(d))
+
+    def top_pass(d):
+        here = top.at[2 * ((x - d + 4) % 4) + c]
+        return net.copy(top_over + d, here, here, sibling)
+
+    half = pl.ds(pl.multiple_of(y % 2 * 640, 128), 640)
+    out_piece = out_own.at[aligned(y // 2, 80), half]
+
+    def out_copy(d):
+        return net.copy(out_near + d, out_piece, out_full.at[x, c, y // 2, :, half], net.device(d))
+
+    def out_share(d):
+        here = out_full.at[:, c, y // 2, :, half]
+        return net.copy(out_ring + d, here, here, net.device(dy=d))
+
+    def out_pass(d):
+        from_y = (y - d + 4) % 4
+        cols = pl.ds(pl.multiple_of(from_y % 2 * 640, 128), 640)
+        here = out_full.at[:, c, from_y // 2, :, cols]
+        return net.copy(out_over + d, here, here, sibling)
+
+    out_local = pltpu.make_async_copy(
+        out_piece, out_full.at[x, c, y // 2, :, half], still.at[out_near]
+    )
+    out_arrived()
+    out_local.start()
+    for d in (2, 1, 3):
+        out_copy(d).start()
+    for d in (1, 3, 2):
+        cut_share(d).wait_recv()
+    up_local.wait()
+    for d in (1, 3, 2):
+        up_copy(d).wait_recv()
+    for d in (2, 1, 3):
+        up_share(d).start()
     project(me)
+    out_local.wait()
+    for d in (1, 3, 2):
+        out_copy(d).wait_recv()
+    for d in (2, 1, 3):
+        out_share(d).start()
+    out_pass(0).start()
     own_over.wait_recv()
     project(2 * x + 1 - c)
+
+    top_arrived()
+    for d in (2, 1, 3):
+        top_copy(d).start()
+
+    @pl.when(c != zl)
+    def _():
+        down_cross.wait_recv()
+        for d in (2, 1, 3):
+            down_share(d).start()
+
     over = net.reserve(4)
 
     def passed(dx, slot):
@@ -344,29 +358,7 @@
         passed(dx, 2 * from_x + c).wait_recv()
         project(2 * from_x + 1 - c)
 
-    later = []
-    top_arrived()
-    for dx in (1, 3, 2):
-        later.append((net.go(top.at[me], top.at[me], net.device(dx)), top, dx))
-    out_arrived()
-    for dx in (1, 3, 2):
-        later.append((net.go(out_full.at[me], out_full.at[me], net.device(dx)), out_full, dx))
-    last = [
-        net.go(top.at[me], top.at[me], sibling),
-        net.go(out_full.at[me], out_full.at[me], sibling),
-    ]
-    for dx in (0, 1, 3, 2):
-        for dz in range(2):
-            if dx or dz:
-                target = 2 * ((x + dx) % 4) + c
-                source = w_up.at[:, pl.ds(pl.multiple_of(target * 640, 128), 640)]
-                last.append(net.go(source, up_mine.at[shard], net.in_pair(dx, dz)))
-    mine_up = pltpu.make_async_copy(
-        w_up.at[:, pl.ds(pl.multiple_of(me * 640, 128), 640)],
-        up_mine.at[shard],
-        still.at[net.reserve(1)],
-    )
-    mine_up.start()
+    top_pass(0).start()
 
     lens_copy.wait_recv()
     clip[...] = lens[zl]
@@ -407,29 +399,44 @@
             mixed_send(dx, 0).start()
 
     attended[me] = mixed[me]
-    for copy, array, dx in later:
-        copy.wait_recv()
-        slot = 2 * ((x - dx + 4) % 4) + c
-        last.append(net.go(array.at[slot], array.at[slot], sibling))
-
+    for d in (1, 3, 2):
+        top_copy(d).wait_recv()
+        top_pass(d).start()
+    for d in (1, 3, 2):
+        out_share(d).wait_recv()
+        out_pass(d).start()
     for dx in range(4):
         for dc in range(2):
             if dx or dc:
                 mixed_send(dx, dc).wait()
-    for copy in last:
-        copy.wait_recv()
-    mine_up.wait()
-    down_arrived()
-    for left in (token_left, out_left, top_left, down_left):
+    for d in range(4):
+        top_pass(d).wait()
+        out_pass(d).wait()
+    for d in (1, 2, 3):
+        up_share(d).wait()
+        for copy in (cut_copy, cut_share, up_copy, top_copy, out_copy, out_share):
+            copy(d).wait_send()
+
+    @pl.when(c == zl)
+    def _():
+        down_local.wait()
+
+    @pl.when(c != zl)
+    def _():
+        down_cross.wait_send()
+        for d in (1, 2, 3):
+            down_share(d).wait()
+
+    bias_arrived()
+    for left in (token_left, out_left, top_left, bias_left):
         left()
     for k in range(3):
         token_send(k, gathered.at[me]).wait_send()
-        dx = order(k)
-        passed(dx, me).wait_send()
+        passed(order(k), me).wait_send()
     net.all_sent()
 
 
-def begin(tokens, w_query, w_key, w_value, small, w_out, w_up, w_down, cotangent, length):
+def begin(tokens, w_query, w_key, w_value, small, up_bias, w_out, w_up, w_down, cotangent, length):
     rows, width = tokens.shape
 
     def shape(*dims):
@@ -437,40 +444,43 @@
 
     return pl.pallas_call(
         begin_kernel,
-        in_specs=[VMEM] * 5 + [HBM] * 4 + [VMEM],
-        out_specs=[VMEM] * 9 + [HBM] * 4,
+        in_specs=[VMEM] * 11,
+        out_specs=[VMEM] * 10 + [HBM] * 4 + [VMEM],
         out_shape=[
             shape(8, rows, width),
             shape(6, 8 * rows, HD),
             shape(2, 8 * rows, 8 * rows),
             shape(8, rows, 160),
             shape(8, rows, 160),
-            shape(width, 480),
-            shape(8, 16, 640),
+            shape(4, 2, 2, 80, 480),
+            shape(8, 16, 160),
+            shape(16, 640),
             shape(rows, width),
             jax.ShapeDtypeStruct((8, 128), F32),
-            shape(8, 160, width),
-            shape(8, 160, 640),
+            shape(4, 2, 2, 80, width),
+            shape(4, 2, 2, 80, 640),
             shape(640, width),
             shape(8, rows, width),
+            shape(160, width),
         ],
         scratch_shapes=[
             pltpu.VMEM((8, rows, width), BF16),
-            pltpu.VMEM((8, 160, 480), BF16),
+            pltpu.VMEM((8, 2, 80, 480), BF16),
             pltpu.VMEM((2, 8, 128), F32),
             pltpu.VMEM((8, width), F32),
         ]
-        + scratch_for(80),
+        + scratch_for(96),
         compiler_params=pltpu.CompilerParams(
             collective_id=0, has_side_effects=True, vmem_limit_bytes=58 << 20
         ),
-    )(tokens, w_query, w_key, w_value, small, w_out, w_up, w_down, cotangent, length)
+    )(tokens, w_query, w_key, w_value, small, up_bias, w_out, w_up, w_down, cotangent, length)
 
 
 def middle_kernel(
     attended,
     own,
     smalls,
+    up_bias,
     clip,
     out_full,
     up_mine,
@@ -508,8 +518,8 @@
     rows, width = own.shape
     wait = net.greet([net.device(dx, dc) for dx in range(4) for dc in range(2) if dx or dc])
     for block in range(8):
-        vectors[:, 160 * block : 160 * block + 160] = smalls[block, :8, :160].astype(F32)
-    bias_up = smalls[me, 8:9, :].astype(F32)
+        vectors[:, 160 * block : 160 * block + 160] = smalls[block, :8, :].astype(F32)
+    bias_up = up_bias[0:1, :].astype(F32)
     mine = aligned(me, rows)
     for block in range(8):
         joined[:, 160 * block : 160 * block + 160] = attended[block]
@@ -651,7 +661,7 @@
     net.all_sent()
 
 
-def middle_part(attended, own, smalls, clip, out_full, up_mine, down_mine, top):
+def middle_part(attended, own, smalls, up_bias, clip, out_full, up_mine, down_mine, top):
     rows, width = own.shape
 
     def shape(*dims, dtype=BF16):
@@ -662,7 +672,7 @@
 
     return pl.pallas_call(
         middle_kernel,
-        in_specs=[VMEM] * 8,
+        in_specs=[VMEM] * 9,
         out_specs=[VMEM] * 9,
         out_shape=[
             shape(rows, width, dtype=F32),
@@ -695,7 +705,7 @@
         compiler_params=pltpu.CompilerParams(
             collective_id=1, has_side_effects=True, vmem_limit_bytes=60 << 20
         ),
-    )(attended, own, smalls, clip, out_full, up_mine, down_mine, top)
+    )(attended, own, smalls, up_bias, clip, out_full, up_mine, down_mine, top)
 
 
 def piece_start(index):
@@ -938,7 +948,7 @@
     )
     own_branch.start()
     for block in range(8):
-        vectors[:, 160 * block : 160 * block + 160] = smalls[block, :8, :160].astype(F32)
+        vectors[:, 160 * block : 160 * block + 160] = smalls[block, :8, :].astype(F32)
     sum_k[...] = jnp.zeros_like(sum_k)
     sum_v[...] = jnp.zeros_like(sum_v)
 
@@ -1078,6 +1088,15 @@
         grads[:, 160 + h * HD : 160 + (h + 1) * HD] = (sum_k[h] * HD**-0.5).astype(BF16)
         grads[:, 320 + h * HD : 320 + (h + 1) * HD] = sum_v[h].astype(BF16)
 
+    load_h1.wait()
+
+    @pl.loop(0, 2)
+    def _(i):
+        cols = pl.ds(pl.multiple_of(i * 640, 128), 640)
+        made = lax.dot_general(tall[:, cols], grads[...], TN, preferred_element_type=F32)
+        g_qkv[pl.ds(4 * i, 4)] = made.astype(BF16).reshape(4, 160, 480)
+
+    three[0]()
     @pl.loop(0, 4)
     def _(k):
         dx = order(k)
@@ -1102,27 +1121,6 @@
         def _():
             final_grad[...] = kept
 
-    for dx in (1, 3, 2):
-        out_add_copy(dx).start()
-    load_h1.wait()
-
-    @pl.loop(0, 2)
-    def _(i):
-        cols = pl.ds(pl.multiple_of(i * 640, 128), 640)
-        made = lax.dot_general(tall[:, cols], grads[...], TN, preferred_element_type=F32)
-        g_qkv[pl.ds(4 * i, 4)] = made.astype(BF16).reshape(4, 160, 480)
-
-    three[0]()
-    head_y[y] = jnp.zeros((8, 640), F32)
-    head_y[y, 0:1, :] = g_up_bias[...]
-    column_sums = jnp.sum(grads[...].astype(F32), axis=0, keepdims=True)
-    head_y[y, 1:2, :160] = column_sums[:, :160]
-    head_y[y, 2:3, :160] = column_sums[:, 320:]
-    head_y_go, head_y_total, head_y_sent = four_way(
-        net, net.reserve(4), head_y, y, lambda d: net.device(dy=d)
-    )
-    head_y_go()
-
     own_branch.wait()
     pass_copy(0).start()
     for dx in (1, 3, 2):
@@ -1150,6 +1148,17 @@
     for d in (2, 1, 3):
         out_1(d).start()
 
+    head_y[y] = jnp.zeros((8, 640), F32)
+    head_y[y, 0:1, :] = g_up_bias[...]
+    column_sums = jnp.sum(grads[...].astype(F32), axis=0, keepdims=True)
+    head_y[y, 1:2, :160] = column_sums[:, :160]
+    head_y[y, 2:3, :160] = column_sums[:, 320:]
+    head_y_go, head_y_total, head_y_sent = four_way(
+        net, net.reserve(4), head_y, y, lambda d: net.device(dy=d)
+    )
+    head_y_go()
+
+    three[1]()
     up[2]()
     total = down_s1[pl.ds(piece_start(y), 48), :].astype(F32)
     for d in (1, 2, 3):
@@ -1158,6 +1167,26 @@
     down_l3[y] = total.astype(BF16)
     d3_go()
 
+    three[2]()
+    up[3]()
+    for d in (1, 2, 3):
+        net.copy(d3 + d, down_l3.at[y], down_l3.at[y], net.device(dy=d)).wait_recv()
+    for i in range(3):
+        down_p[48 * i : 48 * i + 48, :] = down_l3[i]
+    down_p[144:160, :] = down_l3[3, 32:48, :]
+    for k in range(2):
+
+        @pl.when(c + 2 * k != z)
+        def _():
+            down_4(k, z).start()
+
+    @pl.when(c == zl)
+    def _():
+        down_local.start()
+
+    up[4]()
+    up_share[0]()
+    three[3]()
     grad_first = final_grad[...]
     for dx in (1, 3, 2):
         add_copy(dx, (x - dx + 4) % 4).wait_recv()
@@ -1195,29 +1224,20 @@
         vec_copy(dx, dc).start()
     vec_1[me] = vec_cut[x]
 
+    for dx in (1, 3, 2):
+        out_add_copy(dx).start()
+    three[4]()
+    for block in range(8):
+        cols = slice(160 * block, 160 * block + 160)
+        for k in range(3):
+            qkv_rows[k, :, cols] = qkv_landed[block, :, 160 * k : 160 * k + 160]
+    three_share[0]()
     total = g_out[pl.ds(piece_start(y), 48), :].astype(F32)
     for d in (1, 2, 3):
         out_1(d).wait_recv()
         total = total + out_r1[d].astype(F32)
     out_z[z] = total.astype(BF16)
     out_go()
-    up[3]()
-    for d in (1, 2, 3):
-        net.copy(d3 + d, down_l3.at[y], down_l3.at[y], net.device(dy=d)).wait_recv()
-    for i in range(3):
-        down_p[48 * i : 48 * i + 48, :] = down_l3[i]
-    down_p[144:160, :] = down_l3[3, 32:48, :]
-    for k in range(2):
-
-        @pl.when(c + 2 * k != z)
-        def _():
-            down_4(k, z).start()
-
-    @pl.when(c == zl)
-    def _():
-        down_local.start()
-
-    three[1]()
     head_z[z] = head_y_total()
     head_z_go, head_z_total, head_z_sent = four_way(
         net, net.reserve(4), head_z, z, lambda d: net.device(dz=d)
@@ -1244,17 +1264,6 @@
         out_local.start()
         for d in (2, 1, 3):
             out_3(d).start()
-
-    up[4]()
-    up_share[0]()
-    three[2]()
-
-    total = result[...]
-    for dx in (1, 3, 2):
-        out_add_copy(dx).wait_recv()
-        total = total + out_arrived[dx].astype(F32)
-    final_rows[...] = total.astype(BF16)
-    output_arrived, output_left = net.cross(final_rows, output)
 
     head_sib[0] = head_z_total()
     head_copy = net.go(head_sib.at[0], head_sib.at[1], sibling)
@@ -1280,18 +1289,18 @@
             out_3(d).wait_recv()
             out_4((y + 4 - d) % 4).start()
 
-    three[3]()
-    three[4]()
-    for block in range(8):
-        cols = slice(160 * block, 160 * block + 160)
-        for k in range(3):
-            qkv_rows[k, :, cols] = qkv_landed[block, :, 160 * k : 160 * k + 160]
-    three_share[0]()
+    total = result[...]
+    for dx in (1, 3, 2):
+        out_add_copy(dx).wait_recv()
+        total = total + out_arrived[dx].astype(F32)
+    final_rows[...] = total.astype(BF16)
+    output_arrived, output_left = net.cross(final_rows, output)
+
     up_share[1]()
+    three_share[1]()
     head_copy.wait_recv()
     hb_out[...] = jnp.where(c == zl, head_sib[0], head_sib[1])
     vec_out[...] = vec_y_total()
-    three_share[1]()
 
     @pl.when(c == zl)
     def _():
@@ -1449,6 +1458,62 @@
     )
 
 
+def widen_kernel(hb, vec, up, three, down, out, *results):
+    (o_up, o_q, o_k, o_v, o_down, o_out, *small, f_up, f_three, f_down, f_out, done) = results
+    copies = []
+
+    def push(source, target):
+        copy = pltpu.make_async_copy(source, target, done.at[len(copies)])
+        copy.start()
+        copies.append(copy)
+
+    for i in range(4):
+        here, there = slice(48 * i, min(48 * i + 48, 160)), slice(0, 48)
+        if i == 3:
+            there = slice(32, 48)
+        f_up[here, :] = up[i, there, :].astype(F32)
+        f_out[here, :] = out[i, there, :].astype(F32)
+        for k in range(3):
+            f_three[k, here, :] = three[i, k, there, :].astype(F32)
+    push(f_up, o_up)
+    for k, target in enumerate((o_q, o_k, o_v)):
+        push(f_three.at[k], target)
+    push(f_out, o_out)
+    f_down[...] = down[...].astype(F32)
+    push(f_down, o_down)
+    rows = (hb[1, :160], hb[2, :160], hb[0, :]) + tuple(vec[k, :] for k in range(6))
+    for target, row in zip(small, rows):
+        target[...] = row
+    for copy in copies:
+        copy.wait()
+
+
+def widen(hb, vec, up, three, down, out):
+    width = down.shape[1]
+
+    def shape(*dims):
+        return jax.ShapeDtypeStruct(dims, F32)
+
+    sizes = [160, 160, 640] + [160] * 6
+    return pl.pallas_call(
+        widen_kernel,
+        in_specs=[VMEM] * 6,
+        out_specs=[HBM] * 6 + [VMEM] * 9,
+        out_shape=[shape(160, 5120)]
+        + [shape(160, width)] * 3
+        + [shape(640, width), shape(160, width)]
+        + [shape(size) for size in sizes],
+        scratch_shapes=[
+            pltpu.VMEM((160, 5120), F32),
+            pltpu.VMEM((3, 160, width), F32),
+            pltpu.VMEM((640, width), F32),
+            pltpu.VMEM((160, width), F32),
+            pltpu.SemaphoreType.DMA((6,)),
+        ],
+        compiler_params=pltpu.CompilerParams(vmem_limit_bytes=48 << 20),
+    )(hb, vec, up, three, down, out)
+
+
 def per_device(
     tokens,
     lengths,
@@ -1469,13 +1534,14 @@
     shift_ffn,
     cotangent,
 ):
-    rep, shard = lax.axis_index("rep"), lax.axis_index("shard")
-    y, c, x, zl = rep // 4, rep % 2, shard // 2, shard % 2
     rows, width = tokens.shape[1:]
 
     eight = [b_query, b_value, b_out, b_down, gain_attn, shift_attn, gain_ffn, shift_ffn]
-    small = jnp.zeros((16, 640), BF16)
-    small = small.at[:8, :160].set(jnp.stack(eight)).at[8].set(b_up)
+    row = lax.broadcasted_iota(jnp.int32, (16, 160), 0)
+    small = jnp.zeros((16, 160), BF16)
+    for index, vector in enumerate(eight):
+        small = jnp.where(row == index, vector[None, :], small)
+    up_bias = jnp.broadcast_to(b_up[None, :], (16, 640))
     known = jnp.full((8, 128), lengths[0], F32)
     (
         h1,
@@ -1485,16 +1551,28 @@
         attended,
         w_qkv,
         smalls,
+        up_bias,
         own,
         clip,
         out_full,
         up_mine,
         down_mine,
         top,
+        _,
     ) = begin(
-        tokens[0], w_query, w_key, w_value, small, w_out, w_up, w_down, cotangent[0], known
-    )
-
+        tokens[0],
+        w_query,
+        w_key,
+        w_value,
+        small,
+        up_bias,
+        w_out,
+        w_up,
+        w_down,
+        cotangent[0],
+        known,
+    )
+    w_qkv = w_qkv.reshape(width, 480)
     (
         result,
         grad_middle,
@@ -1509,6 +1587,7 @@
         attended,
         own,
         smalls,
+        up_bias,
         clip,
         out_full.reshape(width, width),
         up_mine.reshape(width, 640),
@@ -1534,27 +1613,28 @@
         g_down,
     )
 
-    def whole(pieces):
-        return jnp.concatenate([pieces[0], pieces[1], pieces[2], pieces[3, 32:]]).astype(F32)
-
+    g_up, g_q, g_k, g_v, g_down, g_out, *small = widen(
+        hb_out, vec_out, fin_up, fin_qkv, fin_down, fin_out
+    )
+    b_q, b_v, b_u, b_o, b_d, gain_two, shift_two, gain_one, shift_one = small
     return (
         output[None],
         input_grad[None],
-        whole(fin_qkv[:, 0]),
-        whole(fin_qkv[:, 1]),
-        whole(fin_qkv[:, 2]),
-        whole(fin_out),
-        whole(fin_up),
-        fin_down.astype(F32),
-        hb_out[1, :160],
-        hb_out[2, :160],
-        vec_out[0],
-        hb_out[0],
-        vec_out[1],
-        vec_out[4],
-        vec_out[5],
-        vec_out[2],
-        vec_out[3],
+        g_q,
+        g_k,
+        g_v,
+        g_out,
+        g_up,
+        g_down,
+        b_q,
+        b_v,
+        b_o,
+        b_u,
+        b_d,
+        gain_one,
+        shift_one,
+        gain_two,
+        shift_two,
     )
 
 

time: 354 us -> 295 us (0.83)
  Pallas kernels: 328 us -> 280 us
  local copies, waits for them, and re-layouts: 16.3 us -> 10.4 us
  other arithmetic: 7.18 us -> 1.48 us
    pallas_call x2 -> x3, Pallas kernels: 200 us -> 161 us  [the longest x1 87.8 us: begin(): pl.pallas_call(begin_kernel, in_specs=[VMEM] * 11, out_specs=[VMEM] * 10...]
    pallas_call x1, Pallas kernels: 128 us -> 119 us  [finish(): pl.pallas_call(finish_kernel, in_specs=[VMEM] * 12 + [HBM] * 4, out_specs...]
    convert_element_type x5 -> x0, other arithmetic: 7.18 us -> none  [the longest x4 5.21 us: whole(): jnp.concatenate([pieces[0], pieces[1], pieces[2], pieces[3, 32:]])]
    unnamed x12 -> x18, local copies, waits for them, and re-layouts: 2.34 us -> 8.53 us
    another operation x10 -> x0, local copies, waits for them, and re-layouts: 5.98 us -> none  [the longest x9 5.29 us: per_device(): small = small.at[:8, :160].set(jnp.stack(eight)).at[8].set(b_up)]
    squeeze x8 -> x0, local copies, waits for them, and re-layouts: 4.48 us -> none  [the longest x3 2.66 us: whole(): pieces[0]]
where the time goes in v4:
time: 295 us; the launch traced here: 293 us
  Pallas kernels  280 us (95%)
  local copies, waits for them, and re-layouts  10.4 us (4%)
    pallas_call x1, Pallas kernels, finish(): pl.pallas_call(finish_kernel, in_specs=[VMEM] * 12 + [HBM] * 4, out_specs...  119 us
    pallas_call x1, Pallas kernels, begin(): pl.pallas_call(begin_kernel, in_specs=[VMEM] * 11, out_specs=[VMEM] * 10...  87.8 us
    pallas_call x1, Pallas kernels, middle_part(): pl.pallas_call(middle_kernel, in_specs=[VMEM] * 9, out_specs=[VMEM] * 9,...  68.4 us
    unnamed x18, local copies, waits for them, and re-layouts  8.53 us

profile of v4, /device:TPU:0, one launch (start us, length us, event | category | flops | bytes accessed | tf_op | source)
XLA Modules:
  0.0 293.4 jit_solution(16340124359726745716)
XLA Ops:
  1.3 0.6 broadcast_in_dim.79.length
  1.9 1.5 select_select_fusion.small
  3.4 1.3 broadcast_in_dim.78.up_bias
  4.7 87.8 %shard_map.305 = (bf16[8,192,1280]{2,1,0:T(8,128)(2,1)}, bf16[6,1536,80]{2,1,0:T(8,128)(2,1)}, bf16[2,1536,1536]{2,1,0:T(8,128)(2,1)}, bf16[8,192,160]{2,1,0:T(8...) custom-call(bf16[192,1280]{1,0:T(8,128)(2,1)} %bitcast.18, ...), custom_call_target="tpu_custom_call" | custom-call | tf_op jit(solution)/shard_map/pallas_call | solution.py:445
  92.5 68.4 %shard_map.306 = (f32[192,1280]{1,0:T(8,128)}, f32[192,1280]{1,0:T(8,128)}, bf16[192,1280]{1,0:T(8,128)(2,1)}, bf16[4,192,1280]{2,1,0:T(8,128)(2,1)}, bf16[1280,...) custom-call(bf16[8,192,160]{2,1,0:T(8,128)(2,1)} %get-tuple-element., ...), custom_call_target="tpu_custom_call" | custom-call | tf_op jit(solution)/shard_map/pallas_call | solution.py:673
  160.9 119.3 %shard_map.307 = (f32[8,640]{1,0:T(8,128)}, f32[8,160]{1,0:T(8,128)}, bf16[192,1280]{1,0:T(8,128)(2,1)}, f32[192,1280]{1,0:T(8,128)}, bf16[4,48,5120]{2,1,0:T(8,...) custom-call(bf16[6,1536,80]{2,1,0:T(8,128)(2,1)} %get-tuple-element., ...), custom_call_target="tpu_custom_call" | custom-call | tf_op jit(solution)/shard_map/pallas_call | solution.py:1383
  280.2 0.0 copy-start
  280.2 1.5 copy-done
  281.7 0.0 copy-start.1
  281.7 1.4 copy-done.1
  283.2 0.0 copy-start.2
  283.2 1.4 copy-done.2
  284.6 0.0 copy-start.3
  284.6 1.0 copy-done.3
  285.6 0.0 copy-start.4
  285.6 0.7 copy-done.4
  286.3 0.0 copy-start.5
  286.3 0.7 copy-done.5
  287.0 0.0 copy-start.7
  287.0 0.0 copy-start.6
  287.0 4.7 %shard_map.308 = (f32[160,5120]{1,0:T(8,128)}, f32[160,1280]{1,0:T(8,128)}, f32[160,1280]{1,0:T(8,128)}, f32[160,1280]{1,0:T(8,128)}, f32[640,1280]{1,0:T(8,128)...) custom-call(f32[8,640]{1,0:T(8,128)S(1)} %copy-done.4, ...), custom_call_target="tpu_custom_call" | custom-call | tf_op jit(solution)/shard_map/pallas_call | solution.py:1498
  291.7 0.0 copy-done.7
  291.7 0.8 copy.38
  292.5 0.0 copy-done.6
  292.5 0.9 copy.39
  (4 shorter events, 0.0 us)
Async XLA Ops:
  280.2 1.5 copy-start
  281.7 1.4 copy-start.1
  283.2 1.4 copy-start.2
  284.6 1.0 copy-start.3
  285.6 0.7 copy-start.4
  286.3 0.7 copy-start.5
  287.0 4.7 %copy-start.7 = (bf16[192,1280]{1,0:T(8,128)(2,1)S(1)}, bf16[192,1280]{1,0:T(8,128)(2,1)}, u32[]{:S(2)}) copy-start(bf16[192,1280]{1,0:T(8,128)(2,1)} %get-tuple-element.86) | copy-start | bytes 1474564
  287.0 5.5 %copy-start.6 = (f32[192,1280]{1,0:T(8,128)S(1)}, f32[192,1280]{1,0:T(8,128)}, u32[]{:S(2)}) copy-start(f32[192,1280]{1,0:T(8,128)} %get-tuple-element.87) | copy-start | bytes 2949124

commit v5 on v4

--- a/solution.py
+++ b/solution.py
@@ -142,6 +142,9 @@
     down_mine,
     top,
     out_own,
+    normed_rows,
+    head_rows,
+    prob_buf,
     gathered,
     cut,
     lens,
@@ -161,9 +164,11 @@
         cols = slice(160 * block, 160 * block + 160)
         for half in range(2):
             part = slice(80 * half, 80 * half + 80)
-            cut[block, half, :, :160] = w_query[part, cols]
-            cut[block, half, :, 160:320] = w_key[part, cols]
-            cut[block, half, :, 320:] = w_value[part, cols]
+            for k, weight in enumerate((w_query, w_key, w_value)):
+                piece = weight[part, cols]
+                for h in range(2):
+                    first = 240 * h + 80 * k
+                    cut[block, half, :, first : first + 80] = piece[:, 80 * h : 80 * h + 80]
     wait()
 
     token_arrived, token_left = net.cross(tokens, gathered.at[2 * x + zl])
@@ -202,7 +207,7 @@
 
     @pl.when(c == zl)
     def _():
-        for k in range(3):
+        for k in range(2):
             token_send(k, tokens).start()
 
     @pl.when(c == 0)
@@ -225,7 +230,7 @@
 
     @pl.when(c != zl)
     def _():
-        for k in range(3):
+        for k in range(2):
             token_send(k, gathered.at[me]).start()
 
     sibling = net.device(0, 1)
@@ -273,16 +278,15 @@
         center = values - jnp.mean(values, axis=-1, keepdims=True)
         inverse = lax.rsqrt(jnp.mean(center * center, axis=-1, keepdims=True) + EPS)
         normed = (center * inverse * gain + shift).astype(BF16)
-        h1[slot] = normed
+        normed_rows[slot] = normed
         made = jnp.dot(normed, w_qkv[...].reshape(width, 480), preferred_element_type=F32)
         here = aligned(slot, rows)
         for h in range(2):
             cols = slice(h * HD, (h + 1) * HD)
-            heads[h, here, :] = (made[:, cols] + bias_q[:, cols]).astype(BF16)
-            heads[2 + h, here, :] = made[:, 160 + h * HD : 240 + h * HD].astype(BF16)
-            heads[4 + h, here, :] = (
-                made[:, 320 + h * HD : 400 + h * HD] + bias_v[:, cols]
-            ).astype(BF16)
+            q, k, v = (made[:, 240 * h + 80 * j : 240 * h + 80 * j + 80] for j in range(3))
+            head_rows[h, here, :] = (q + bias_q[:, cols]).astype(BF16)
+            head_rows[2 + h, here, :] = k.astype(BF16)
+            head_rows[4 + h, here, :] = (v + bias_v[:, cols]).astype(BF16)
 
     top_near, top_over, out_near, out_ring, out_over = (net.reserve(4) for _ in range(5))
 
@@ -318,11 +322,6 @@
         out_copy(d).start()
     for d in (1, 3, 2):
         cut_share(d).wait_recv()
-    up_local.wait()
-    for d in (1, 3, 2):
-        up_copy(d).wait_recv()
-    for d in (2, 1, 3):
-        up_share(d).start()
     project(me)
     out_local.wait()
     for d in (1, 3, 2):
@@ -332,7 +331,6 @@
     out_pass(0).start()
     own_over.wait_recv()
     project(2 * x + 1 - c)
-
     top_arrived()
     for d in (2, 1, 3):
         top_copy(d).start()
@@ -343,7 +341,12 @@
         for d in (2, 1, 3):
             down_share(d).start()
 
-    over = net.reserve(4)
+    over, halves = net.reserve(4), net.reserve(2)
+
+    def token_half(i):
+        slot = 2 * ((x + 3 + 2 * i) % 4) + c
+        here = gathered.at[slot, pl.ds(i * rows // 2, rows // 2), :]
+        return net.copy(halves + i, here, here, net.device(1 + 2 * i))
 
     def passed(dx, slot):
         return net.copy(over + dx, gathered.at[slot], gathered.at[slot], sibling)
@@ -352,33 +355,62 @@
     def _(k):
         dx = order(k)
         from_x = (x - dx + 4) % 4
-        token_send(k, gathered.at[me]).wait_recv()
+
+        @pl.when(k == 0)
+        def _():
+            for i in range(2):
+                token_send(i, gathered.at[me]).wait_recv()
+                token_half(i).start()
+
+        @pl.when(k == 2)
+        def _():
+            for i in range(2):
+                token_half(i).wait_recv()
+
         passed(dx, 2 * from_x + c).start()
         project(2 * from_x + c)
         passed(dx, 2 * from_x + c).wait_recv()
         project(2 * from_x + 1 - c)
 
+    up_local.wait()
+    for d in (1, 3, 2):
+        up_copy(d).wait_recv()
+    for d in (2, 1, 3):
+        up_share(d).start()
     top_pass(0).start()
 
+    keep_h1 = pltpu.make_async_copy(normed_rows, h1, still.at[net.reserve(1)])
+    keep_h1.start()
+    keep_heads = pltpu.make_async_copy(head_rows, heads, still.at[net.reserve(1)])
+    keep_heads.start()
     lens_copy.wait_recv()
     clip[...] = lens[zl]
     clip_length = clip[0:1, 0:1]
     position = lax.broadcasted_iota(jnp.int32, (1, 8 * rows), 1).astype(F32)
     mask = jnp.where(position < clip_length, 0.0, -1e30)
 
-    def attend_rows(to_x):
+    def attend_rows(to_x, slot):
         here = aligned(to_x, 2 * rows)
         for h in range(2):
             cols = slice(h * HD, (h + 1) * HD)
-            scores = lax.dot_general(heads[h, here, :], heads[2 + h], NT, preferred_element_type=F32)
+            scores = lax.dot_general(
+                head_rows[h, here, :], head_rows[2 + h], NT, preferred_element_type=F32
+            )
             scores = scores * HD**-0.5 + mask
             risen = jnp.exp(scores - jnp.max(scores, axis=-1, keepdims=True))
             share = 1.0 / jnp.sum(risen, axis=-1, keepdims=True)
             low = (risen * share).astype(BF16)
-            probs[h, here, :] = low
-            made = jnp.dot(low, heads[4 + h], preferred_element_type=F32).astype(BF16)
+            prob_buf[slot, h] = low
+            made = jnp.dot(low, head_rows[4 + h], preferred_element_type=F32).astype(BF16)
             mixed[2 * to_x, :, cols] = made[:rows]
             mixed[2 * to_x + 1, :, cols] = made[rows:]
+
+    prob_index = net.reserve(2)
+
+    def keep_probs(to_x, slot):
+        return pltpu.make_async_copy(
+            prob_buf.at[slot], probs.at[:, aligned(to_x, 2 * rows), :], still.at[prob_index + slot]
+        )
 
     mixed_base = net.reserve(8)
 
@@ -391,7 +423,14 @@
     @pl.loop(1, 5)
     def _(step):
         dx = step % 4
-        attend_rows((x + dx) % 4)
+        to_x = (x + dx) % 4
+
+        @pl.when(step > 2)
+        def _():
+            keep_probs(to_x, step % 2).wait()
+
+        attend_rows(to_x, step % 2)
+        keep_probs(to_x, step % 2).start()
         mixed_send(dx, 1).start()
 
         @pl.when(dx != 0)
@@ -427,11 +466,17 @@
         for d in (1, 2, 3):
             down_share(d).wait()
 
+    keep_h1.wait()
+    keep_heads.wait()
+    for slot in range(2):
+        keep_probs(slot, slot).wait()
     bias_arrived()
     for left in (token_left, out_left, top_left, bias_left):
         left()
+    for k in range(2):
+        token_send(k, gathered.at[me]).wait_send()
+        token_half(k).wait_send()
     for k in range(3):
-        token_send(k, gathered.at[me]).wait_send()
         passed(order(k), me).wait_send()
     net.all_sent()
 
@@ -445,7 +490,7 @@
     return pl.pallas_call(
         begin_kernel,
         in_specs=[VMEM] * 11,
-        out_specs=[VMEM] * 10 + [HBM] * 4 + [VMEM],
+        out_specs=[HBM] * 3 + [VMEM] * 7 + [HBM] * 4 + [VMEM],
         out_shape=[
             shape(8, rows, width),
             shape(6, 8 * rows, HD),
@@ -464,6 +509,9 @@
             shape(160, width),
         ],
         scratch_shapes=[
+            pltpu.VMEM((8, rows, width), BF16),
+            pltpu.VMEM((6, 8 * rows, HD), BF16),
+            pltpu.VMEM((2, 2, 2 * rows, 8 * rows), BF16),
             pltpu.VMEM((8, rows, width), BF16),
             pltpu.VMEM((8, 2, 80, 480), BF16),
             pltpu.VMEM((2, 8, 128), F32),
@@ -555,7 +603,14 @@
     def add_copy(dx, to_x):
         return net.copy(add + dx, sums.at[to_x], arrived.at[dx], net.device(4 - dx))
 
-    for dx in (1, 3, 2):
+    halves = net.reserve(2)
+
+    def half_copy(i):
+        slot = 2 * ((x + 3 + 2 * i) % 4) + c
+        here = second.at[aligned(2 * slot + i, rows // 2)]
+        return net.copy(halves + i, here, here, net.device(1 + 2 * i))
+
+    for dx in (1, 3):
         near_copy(dx).start()
 
     @pl.loop(0, 4)
@@ -563,9 +618,16 @@
         dx = k ^ (k >> 1)
         to_x = (x - dx + 4) % 4
 
-        @pl.when(dx != 0)
+        @pl.when(k == 1)
         def _():
-            near_copy(dx).wait_recv()
+            for i in range(2):
+                near_copy(1 + 2 * i).wait_recv()
+                half_copy(i).start()
+
+        @pl.when(k == 3)
+        def _():
+            for i in range(2):
+                half_copy(i).wait_recv()
 
         pass_copy(dx, 2 * to_x + c).start()
         here = aligned(to_x, 2 * rows)
@@ -656,8 +718,10 @@
         swap_copy(dx, to_x).wait_send()
         out_copy(dx, to_x).wait_send()
         if dx:
-            near_copy(dx).wait_send()
             add_copy(dx, to_x).wait_send()
+    for i in range(2):
+        near_copy(1 + 2 * i).wait_send()
+        half_copy(i).wait_send()
     net.all_sent()
 
 
@@ -855,9 +919,9 @@
     result,
     grad_middle,
     branch,
-    out_sums,
     g_up_bias,
     g_vectors,
+    out_sums,
     probs,
     h1,
     g_up,
@@ -883,20 +947,29 @@
     out_arrived,
     final_rows,
     final_grad,
+    low_grad,
     up_r1,
     up_s1,
     up_r2,
     up_s2,
     up_planes,
     up_landed,
-    g_qkv,
-    qkv_r1,
-    qkv_s1,
-    qkv_r2,
-    qkv_s2,
-    qkv_planes,
-    qkv_landed,
+    g_head_0,
+    r1_head_0,
+    s1_head_0,
+    r2_head_0,
+    s2_head_0,
+    planes_head_0,
+    landed_head_0,
+    g_head_1,
+    r1_head_1,
+    s1_head_1,
+    r2_head_1,
+    s2_head_1,
+    planes_head_1,
+    landed_head_1,
     qkv_rows,
+    w_heads,
     down_r1,
     down_s1,
     down_r2,
@@ -934,10 +1007,10 @@
     tile = 2 * rows
     slots = net.reserve(2)
 
-    def load_probs(i):
-        slot = i % 2
+    def load_probs(j):
+        slot = j % 2
         return pltpu.make_async_copy(
-            probs.at[:, aligned(i, tile), :], prob_buf.at[slot], still.at[slots + slot]
+            probs.at[j // 4, aligned(j % 4, tile), :], prob_buf.at[slot], still.at[slots + slot]
         )
 
     load_probs(0).start()
@@ -949,8 +1022,8 @@
     own_branch.start()
     for block in range(8):
         vectors[:, 160 * block : 160 * block + 160] = smalls[block, :8, :].astype(F32)
-    sum_k[...] = jnp.zeros_like(sum_k)
-    sum_v[...] = jnp.zeros_like(sum_v)
+    for h in range(2):
+        w_heads[h] = w_qkv[:, 240 * h : 240 * h + 240]
 
     up = column_flow(
         net,
@@ -963,17 +1036,11 @@
         up_landed,
         lambda ref, hb: ref.at[:, pl.ds(pl.multiple_of(hb * 640, 128), 640)],
     )
-    three = column_flow(
-        net,
-        g_qkv,
-        qkv_r1,
-        qkv_s1,
-        qkv_r2,
-        qkv_s2,
-        qkv_planes,
-        qkv_landed,
-        lambda ref, hb: ref.at[hb],
-    )
+    head_buffers = (
+        (g_head_0, r1_head_0, s1_head_0, r2_head_0, s2_head_0, planes_head_0, landed_head_0),
+        (g_head_1, r1_head_1, s1_head_1, r2_head_1, s2_head_1, planes_head_1, landed_head_1),
+    )
+    flows = [column_flow(net, *held, lambda ref, hb: ref.at[hb]) for held in head_buffers]
     up_share = share_over_y(
         net,
         up_landed,
@@ -1061,54 +1128,68 @@
     for d in (2, 1, 3):
         down_1(d).start()
 
-    @pl.loop(0, 4)
-    def _(i):
-        @pl.when(i < 3)
-        def _():
-            load_probs(i + 1).start()
-
-        load_probs(i).wait()
-        here = aligned(i, tile)
-        for h in range(2):
-            cols = slice(h * HD, (h + 1) * HD)
+    for h in range(2):
+        cols = slice(h * HD, (h + 1) * HD)
+        sum_k[...] = jnp.zeros_like(sum_k)
+        sum_v[...] = jnp.zeros_like(sum_v)
+
+        @pl.loop(0, 4)
+        def _(i, h=h, cols=cols):
+            j = 4 * h + i
+
+            @pl.when(j < 7)
+            def _():
+                load_probs(j + 1).start()
+
+            load_probs(j).wait()
+            here = aligned(i, tile)
             back = jnp.concatenate([grad_mixed[2 * i, :, cols], grad_mixed[2 * i + 1, :, cols]])
             seen = jnp.concatenate([mixed[2 * i, :, cols], mixed[2 * i + 1, :, cols]])
-            low = prob_buf[i % 2, h]
+            low = prob_buf[j % 2]
             row_total = jnp.sum(back.astype(F32) * seen.astype(F32), axis=-1, keepdims=True)
             grad_probs = lax.dot_general(back, heads[4 + h], NT, preferred_element_type=F32)
             grad_scores = (low.astype(F32) * (grad_probs - row_total)).astype(BF16)
-            sum_v[h] += lax.dot_general(low, back, TN, preferred_element_type=F32)
-            sum_k[h] += lax.dot_general(
+            sum_v[...] += lax.dot_general(low, back, TN, preferred_element_type=F32)
+            sum_k[...] += lax.dot_general(
                 grad_scores, heads[h, here, :], TN, preferred_element_type=F32
             )
             grad_q = jnp.dot(grad_scores, heads[2 + h], preferred_element_type=F32)
-            grads[here, cols] = (grad_q * HD**-0.5).astype(BF16)
-
-    for h in range(2):
-        grads[:, 160 + h * HD : 160 + (h + 1) * HD] = (sum_k[h] * HD**-0.5).astype(BF16)
-        grads[:, 320 + h * HD : 320 + (h + 1) * HD] = sum_v[h].astype(BF16)
-
-    load_h1.wait()
-
-    @pl.loop(0, 2)
-    def _(i):
-        cols = pl.ds(pl.multiple_of(i * 640, 128), 640)
-        made = lax.dot_general(tall[:, cols], grads[...], TN, preferred_element_type=F32)
-        g_qkv[pl.ds(4 * i, 4)] = made.astype(BF16).reshape(4, 160, 480)
-
-    three[0]()
+            grads[h, here, :80] = (grad_q * HD**-0.5).astype(BF16)
+
+        grads[h, :, 80:160] = (sum_k[...] * HD**-0.5).astype(BF16)
+        grads[h, :, 160:] = sum_v[...].astype(BF16)
+        if h == 0:
+            load_h1.wait()
+
+        @pl.loop(0, 2)
+        def _(i, h=h):
+            cols = pl.ds(pl.multiple_of(i * 640, 128), 640)
+            made = lax.dot_general(tall[:, cols], grads[h], TN, preferred_element_type=F32)
+            head_buffers[h][0][pl.ds(4 * i, 4)] = made.astype(BF16).reshape(4, 160, 240)
+
+        flows[h][0]()
+
+    def back_rows(block):
+        made = [
+            lax.dot_general(
+                grads[h, aligned(block, rows), :], w_heads[h], NT, preferred_element_type=F32
+            )
+            for h in range(2)
+        ]
+        return made[0] + made[1]
+
     @pl.loop(0, 4)
     def _(k):
-        dx = order(k)
-        dx = jnp.where(k == 3, 0, dx)
+        dx = jnp.where(k == 3, 0, order(k))
         to_x = (x - dx + 4) % 4
-        part = lax.dot_general(
-            grads[aligned(to_x, tile), :], w_qkv[...], NT, preferred_element_type=F32
-        )
-        low, high = part[:rows], part[rows:]
-        give[to_x] = jnp.where(c == 0, high, low).astype(BF16)
+        give[to_x] = back_rows(2 * to_x + 1 - c).astype(BF16)
         swap_copy(dx, to_x).start()
-        kept = jnp.where(c == 0, low, high)
+
+    @pl.loop(0, 4)
+    def _(k):
+        dx = jnp.where(k == 3, 0, order(k))
+        to_x = (x - dx + 4) % 4
+        kept = back_rows(2 * to_x + c)
         swap_copy(dx, to_x).wait_recv()
         kept = kept + over[to_x].astype(F32)
 
@@ -1150,15 +1231,18 @@
 
     head_y[y] = jnp.zeros((8, 640), F32)
     head_y[y, 0:1, :] = g_up_bias[...]
-    column_sums = jnp.sum(grads[...].astype(F32), axis=0, keepdims=True)
-    head_y[y, 1:2, :160] = column_sums[:, :160]
-    head_y[y, 2:3, :160] = column_sums[:, 320:]
+    for h in range(2):
+        cols = slice(h * HD, (h + 1) * HD)
+        column_sums = jnp.sum(grads[h].astype(F32), axis=0, keepdims=True)
+        head_y[y, 1:2, cols] = column_sums[:, :80]
+        head_y[y, 2:3, cols] = column_sums[:, 160:]
     head_y_go, head_y_total, head_y_sent = four_way(
         net, net.reserve(4), head_y, y, lambda d: net.device(dy=d)
     )
     head_y_go()
 
-    three[1]()
+    for flow in flows:
+        flow[1]()
     up[2]()
     total = down_s1[pl.ds(piece_start(y), 48), :].astype(F32)
     for d in (1, 2, 3):
@@ -1167,7 +1251,8 @@
     down_l3[y] = total.astype(BF16)
     d3_go()
 
-    three[2]()
+    for flow in flows:
+        flow[2]()
     up[3]()
     for d in (1, 2, 3):
         net.copy(d3 + d, down_l3.at[y], down_l3.at[y], net.device(dy=d)).wait_recv()
@@ -1186,7 +1271,8 @@
 
     up[4]()
     up_share[0]()
-    three[3]()
+    for flow in flows:
+        flow[3]()
     grad_first = final_grad[...]
     for dx in (1, 3, 2):
         add_copy(dx, (x - dx + 4) % 4).wait_recv()
@@ -1201,8 +1287,8 @@
         - jnp.mean(scaled, axis=-1, keepdims=True)
         - normed * jnp.mean(scaled * normed, axis=-1, keepdims=True)
     )
-    final_grad[...] = grad_middle[...] + back
-    grad_arrived, grad_left = net.cross(final_grad, input_grad)
+    low_grad[...] = (grad_middle[...] + back).astype(BF16)
+    grad_arrived, grad_left = net.cross(low_grad, input_grad)
     gain = jnp.sum(grad_first * normed, axis=0, keepdims=True)
     shift = jnp.sum(grad_first, axis=0, keepdims=True)
     for block in range(8):
@@ -1226,11 +1312,14 @@
 
     for dx in (1, 3, 2):
         out_add_copy(dx).start()
-    three[4]()
+    for flow in flows:
+        flow[4]()
     for block in range(8):
         cols = slice(160 * block, 160 * block + 160)
         for k in range(3):
-            qkv_rows[k, :, cols] = qkv_landed[block, :, 160 * k : 160 * k + 160]
+            qkv_rows[k, :, cols] = jnp.concatenate(
+                [held[6][block, :, 80 * k : 80 * k + 80] for held in head_buffers], axis=1
+            )
     three_share[0]()
     total = g_out[pl.ds(piece_start(y), 48), :].astype(F32)
     for d in (1, 2, 3):
@@ -1328,7 +1417,7 @@
     grad_left()
     output_arrived()
     output_left()
-    for done in (up[5], three[5], d3_sent, out_sent, head_y_sent, head_z_sent, vec_y_sent):
+    for done in (up[5], flows[0][5], flows[1][5], d3_sent, out_sent, head_y_sent, head_z_sent, vec_y_sent):
         done()
     for d in (1, 2, 3):
         down_1(d).wait_send()
@@ -1382,13 +1471,13 @@
 
     return pl.pallas_call(
         finish_kernel,
-        in_specs=[VMEM] * 12 + [HBM] * 4,
+        in_specs=[VMEM] * 11 + [HBM] * 5,
         out_specs=[VMEM] * 2 + [HBM] * 7,
         out_shape=[
             shape(8, 640, dtype=F32),
             shape(8, 160, dtype=F32),
             shape(rows, width),
-            shape(rows, width, dtype=F32),
+            shape(rows, width),
             shape(4, 48, 5120),
             shape(4, 3, 48, width),
             shape(640, width),
@@ -1397,10 +1486,10 @@
         ],
         scratch_shapes=[
             buffer(8 * rows, width),
-            buffer(2, 2, 2 * rows, 8 * rows),
-            buffer(8 * rows, 480),
-            buffer(2, 8 * rows, HD, dtype=F32),
-            buffer(2, 8 * rows, HD, dtype=F32),
+            buffer(2, 2 * rows, 8 * rows),
+            buffer(2, 8 * rows, 240),
+            buffer(8 * rows, HD, dtype=F32),
+            buffer(8 * rows, HD, dtype=F32),
             buffer(4, rows, width),
             buffer(4, rows, width),
             buffer(4, rows, width),
@@ -1408,13 +1497,14 @@
             buffer(4, rows, width),
             buffer(rows, width),
             buffer(rows, width, dtype=F32),
+            buffer(rows, width),
         ]
         + column_buffers(640)
-        + [buffer(48, 5120), buffer(8, 160, 480)]
-        + column_buffers(480)
+        + [buffer(48, 5120)]
+        + ([buffer(8, 160, 240)] + column_buffers(240) + [buffer(8, 48, 240)]) * 2
         + [
-            buffer(8, 48, 480),
             buffer(3, 48, width),
+            buffer(2, width, 240),
             buffer(4, 160, width),
             buffer(160, width),
             buffer(4, 48, width),
@@ -1448,9 +1538,9 @@
         result,
         grad_middle,
         branch,
-        out_sums,
         g_up_bias,
         g_vectors,
+        out_sums,
         probs,
         h1,
         g_up,
@@ -1458,60 +1548,81 @@
     )
 
 
-def widen_kernel(hb, vec, up, three, down, out, *results):
-    (o_up, o_q, o_k, o_v, o_down, o_out, *small, f_up, f_three, f_down, f_out, done) = results
-    copies = []
+def widen_kernel(hb, vec, up, three, down, out, rows, grad, *results):
+    o_up, o_q, o_k, o_v, o_down, o_out, o_rows, o_grad = results[:8]
+    small, scratch = results[8:17], results[17:]
+    b_up, b_three, b_down, b_out, b_rows, b_grad, f_up, f_three, f_down, f_out, f_grad, came, done = scratch
+    loads, copies = [], []
+    sources = ((up, b_up), (three, b_three), (down, b_down), (out, b_out), (grad, b_grad), (rows, b_rows))
+    for source, target in sources:
+        loads.append(pltpu.make_async_copy(source, target, came.at[len(loads)]))
+        loads[-1].start()
 
     def push(source, target):
         copy = pltpu.make_async_copy(source, target, done.at[len(copies)])
         copy.start()
         copies.append(copy)
 
-    for i in range(4):
-        here, there = slice(48 * i, min(48 * i + 48, 160)), slice(0, 48)
-        if i == 3:
-            there = slice(32, 48)
-        f_up[here, :] = up[i, there, :].astype(F32)
-        f_out[here, :] = out[i, there, :].astype(F32)
-        for k in range(3):
-            f_three[k, here, :] = three[i, k, there, :].astype(F32)
+    pieces = ((slice(0, 48), 0, slice(0, 48)), (slice(48, 96), 1, slice(0, 48)))
+    pieces += ((slice(96, 144), 2, slice(0, 48)), (slice(144, 160), 3, slice(32, 48)))
+    loads[0].wait()
+    for here, i, there in pieces:
+        f_up[here, :] = b_up[i, there, :].astype(F32)
     push(f_up, o_up)
+    loads[1].wait()
     for k, target in enumerate((o_q, o_k, o_v)):
+        for here, i, there in pieces:
+            f_three[k, here, :] = b_three[i, k, there, :].astype(F32)
         push(f_three.at[k], target)
+    loads[2].wait()
+    f_down[...] = b_down[...].astype(F32)
+    push(f_down, o_down)
+    loads[3].wait()
+    for here, i, there in pieces:
+        f_out[here, :] = b_out[i, there, :].astype(F32)
     push(f_out, o_out)
-    f_down[...] = down[...].astype(F32)
-    push(f_down, o_down)
-    rows = (hb[1, :160], hb[2, :160], hb[0, :]) + tuple(vec[k, :] for k in range(6))
-    for target, row in zip(small, rows):
+    loads[4].wait()
+    f_grad[...] = b_grad[...].astype(F32)
+    push(f_grad, o_grad)
+    loads[5].wait()
+    push(b_rows, o_rows)
+    for target, row in zip(small, (hb[1, :160], hb[2, :160], hb[0, :])):
         target[...] = row
+    for k in range(6):
+        small[3 + k][...] = vec[k, :]
     for copy in copies:
         copy.wait()
 
 
-def widen(hb, vec, up, three, down, out):
+def widen(hb, vec, up, three, down, out, rows, grad):
     width = down.shape[1]
 
     def shape(*dims):
         return jax.ShapeDtypeStruct(dims, F32)
 
     sizes = [160, 160, 640] + [160] * 6
+    arrays = (up, three, down, out, rows, grad)
     return pl.pallas_call(
         widen_kernel,
-        in_specs=[VMEM] * 6,
-        out_specs=[HBM] * 6 + [VMEM] * 9,
+        in_specs=[VMEM] * 2 + [HBM] * 6,
+        out_specs=[HBM] * 8 + [VMEM] * 9,
         out_shape=[shape(160, 5120)]
         + [shape(160, width)] * 3
         + [shape(640, width), shape(160, width)]
+        + [jax.ShapeDtypeStruct(rows.shape, BF16), shape(*grad.shape)]
         + [shape(size) for size in sizes],
-        scratch_shapes=[
+        scratch_shapes=[pltpu.VMEM(array.shape, BF16) for array in arrays]
+        + [
             pltpu.VMEM((160, 5120), F32),
             pltpu.VMEM((3, 160, width), F32),
             pltpu.VMEM((640, width), F32),
             pltpu.VMEM((160, width), F32),
+            pltpu.VMEM(grad.shape, F32),
             pltpu.SemaphoreType.DMA((6,)),
+            pltpu.SemaphoreType.DMA((8,)),
         ],
-        compiler_params=pltpu.CompilerParams(vmem_limit_bytes=48 << 20),
-    )(hb, vec, up, three, down, out)
+        compiler_params=pltpu.CompilerParams(vmem_limit_bytes=60 << 20),
+    )(hb, vec, up, three, down, out, rows, grad)
 
 
 def per_device(
@@ -1613,8 +1724,8 @@
         g_down,
     )
 
-    g_up, g_q, g_k, g_v, g_down, g_out, *small = widen(
-        hb_out, vec_out, fin_up, fin_qkv, fin_down, fin_out
+    g_up, g_q, g_k, g_v, g_down, g_out, output, input_grad, *small = widen(
+        hb_out, vec_out, fin_up, fin_qkv, fin_down, fin_out, output, input_grad
     )
     b_q, b_v, b_u, b_o, b_d, gain_two, shift_two, gain_one, shift_one = small
     return (

time: 295 us -> 281 us (0.953); the launches traced: 293 us -> 276 us
  Pallas kernels: 280 us -> 271 us
  local copies, waits for them, and re-layouts: 10.4 us -> 1.89 us
    pallas_call x3, Pallas kernels: 212 us -> 202 us  [the longest x1 102 us: finish(): pl.pallas_call(finish_kernel, in_specs=[VMEM] * 11 + [HBM] * 5, out_specs...]
    unnamed x18 -> x0, local copies, waits for them, and re-layouts: 8.53 us -> none
where the time goes in v5:
time: 281 us; the launch traced here: 276 us
  Pallas kernels  271 us (96%)
    pallas_call x1, Pallas kernels, finish(): pl.pallas_call(finish_kernel, in_specs=[VMEM] * 11 + [HBM] * 5, out_specs...  102 us
    pallas_call x1, Pallas kernels, begin(): pl.pallas_call(begin_kernel, in_specs=[VMEM] * 11, out_specs=[HBM] * 3 +...  92.4 us
    pallas_call x1, Pallas kernels, middle_part(): pl.pallas_call(middle_kernel, in_specs=[VMEM] * 9, out_specs=[VMEM] * 9,...  68.8 us
    pallas_call x1, Pallas kernels, widen(): pl.pallas_call(widen_kernel, in_specs=[VMEM] * 2 + [HBM] * 6, out_specs=[...  7.4 us

profile of v5, /device:TPU:0, one launch (start us, length us, event | category | flops | bytes accessed | tf_op | source)
XLA Modules:
  0.0 275.8 jit_solution(12974955857518785423)
XLA Ops:
  1.3 0.6 broadcast_in_dim.79.length
  1.9 1.5 select_select_fusion.small
  3.4 1.3 broadcast_in_dim.78.up_bias
  4.7 92.4 %shard_map.305 = (bf16[8,192,1280]{2,1,0:T(8,128)(2,1)}, bf16[6,1536,80]{2,1,0:T(8,128)(2,1)}, bf16[2,1536,1536]{2,1,0:T(8,128)(2,1)}, bf16[8,192,160]{2,1,0:T(8...) custom-call(bf16[192,1280]{1,0:T(8,128)(2,1)} %bitcast.17, ...), custom_call_target="tpu_custom_call" | custom-call | tf_op jit(solution)/shard_map/pallas_call | solution.py:490
  97.1 68.8 %shard_map.306 = (f32[192,1280]{1,0:T(8,128)}, f32[192,1280]{1,0:T(8,128)}, bf16[192,1280]{1,0:T(8,128)(2,1)}, bf16[4,192,1280]{2,1,0:T(8,128)(2,1)}, bf16[1280,...) custom-call(bf16[8,192,160]{2,1,0:T(8,128)(2,1)} %get-tuple-element., ...), custom_call_target="tpu_custom_call" | custom-call | tf_op jit(solution)/shard_map/pallas_call | solution.py:737
  165.9 102.2 %shard_map.307 = (f32[8,640]{1,0:T(8,128)}, f32[8,160]{1,0:T(8,128)}, bf16[192,1280]{1,0:T(8,128)(2,1)}, bf16[192,1280]{1,0:T(8,128)(2,1)}, bf16[4,48,5120]{2,1,...) custom-call(bf16[6,1536,80]{2,1,0:T(8,128)(2,1)} %get-tuple-element., ...), custom_call_target="tpu_custom_call" | custom-call | tf_op jit(solution)/shard_map/pallas_call | solution.py:1472
  268.2 7.4 %shard_map.308 = (f32[160,5120]{1,0:T(8,128)}, f32[160,1280]{1,0:T(8,128)}, f32[160,1280]{1,0:T(8,128)}, f32[160,1280]{1,0:T(8,128)}, f32[640,1280]{1,0:T(8,128)...) custom-call(f32[8,640]{1,0:T(8,128)} %get-tuple-element.88.hb, ...), custom_call_target="tpu_custom_call" | custom-call | tf_op jit(solution)/shard_map/pallas_call | solution.py:1605
  (4 shorter events, 0.0 us)

commit v6 on v5

--- a/solution.py
+++ b/solution.py
@@ -188,6 +188,13 @@
         here = w_qkv.at[:, zl, zh]
         return net.copy(cut_ring + d, here, here, net.device(dz=d))
 
+    cut_half = net.reserve(2)
+
+    def cut_on(i):
+        from_z = (2 * zh + zl + 3 + 2 * i) % 4
+        here = w_qkv.at[pl.ds(2 * i, 2), from_z % 2, from_z // 2]
+        return net.copy(cut_half + i, here, here, net.device(dz=1 + 2 * i))
+
     def up_part(index):
         cols = pl.ds(pl.multiple_of(index * 640, 128), 640)
         return w_up.at[aligned(zh, 80), cols]
@@ -237,33 +244,11 @@
     own_over = net.go(gathered.at[me], gathered.at[me], sibling)
     for d in (1, 3, 2):
         cut_copy(d).wait_recv()
-    for d in (2, 1, 3):
+    for d in (1, 3):
         cut_share(d).start()
     up_local.start()
     for d in (2, 1, 3):
         up_copy(d).start()
-    bias_arrived, bias_left = net.cross(up_bias, bias_up)
-    top_arrived, top_left = net.cross(cotangent, top.at[2 * x + zl])
-    out_arrived, out_left = net.cross(w_out, out_own)
-
-    down_index, down_ring = net.reserve(1), net.reserve(4)
-    down_cross = net.copy(
-        down_index, w_down.at[aligned(y, 160)], down_mine.at[aligned(y, 160)], net.partner()
-    )
-    down_local = pltpu.make_async_copy(w_down, down_mine, still.at[down_index])
-
-    def down_share(d):
-        here = down_mine.at[aligned(y, 160)]
-        return net.copy(down_ring + d, here, here, net.device(dy=d))
-
-    @pl.when(c == zl)
-    def _():
-        down_local.start()
-
-    @pl.when(c != zl)
-    def _():
-        down_cross.start()
-
     own[...] = gathered[me]
     for copy in arriving:
         copy.wait_recv()
@@ -288,10 +273,42 @@
             head_rows[2 + h, here, :] = k.astype(BF16)
             head_rows[4 + h, here, :] = (v + bias_v[:, cols]).astype(BF16)
 
+    for i in range(2):
+        cut_share(1 + 2 * i).wait_recv()
+        cut_on(i).start()
+    bias_arrived, bias_left = net.cross(up_bias, bias_up)
+    top_arrived, top_left = net.cross(cotangent, top.at[2 * x + zl])
+    out_arrived, out_left = net.cross(w_out, out_own)
+
+    down_index, down_ring = net.reserve(1), net.reserve(4)
+    down_cross = net.copy(
+        down_index, w_down.at[aligned(y, 160)], down_mine.at[aligned(y, 160)], net.partner()
+    )
+    down_local = pltpu.make_async_copy(w_down, down_mine, still.at[down_index])
+
+    def down_share(d):
+        here = down_mine.at[aligned(y, 160)]
+        return net.copy(down_ring + d, here, here, net.device(dy=d))
+
+    @pl.when(c == zl)
+    def _():
+        down_local.start()
+
+    @pl.when(c != zl)
+    def _():
+        down_cross.start()
+
     top_near, top_over, out_near, out_ring, out_over = (net.reserve(4) for _ in range(5))
 
     def top_copy(d):
         return net.copy(top_near + d, top.at[me], top.at[me], net.device(d))
+
+    top_halves = net.reserve(2)
+
+    def top_half(i):
+        slot = 2 * ((x + 3 + 2 * i) % 4) + c
+        here = top.at[slot, pl.ds(i * rows // 2, rows // 2), :]
+        return net.copy(top_halves + i, here, here, net.device(1 + 2 * i))
 
     def top_pass(d):
         here = top.at[2 * ((x - d + 4) % 4) + c]
@@ -316,62 +333,65 @@
     out_local = pltpu.make_async_copy(
         out_piece, out_full.at[x, c, y // 2, :, half], still.at[out_near]
     )
+    for i in range(2):
+        cut_on(i).wait_recv()
+    project(me)
+    own_over.wait_recv()
+    project(2 * x + 1 - c)
     out_arrived()
     out_local.start()
     for d in (2, 1, 3):
         out_copy(d).start()
-    for d in (1, 3, 2):
-        cut_share(d).wait_recv()
-    project(me)
+
+    @pl.when(c != zl)
+    def _():
+        down_cross.wait_recv()
+        for d in (2, 1, 3):
+            down_share(d).start()
+
+    over, halves = net.reserve(4), net.reserve(2)
+
+    def token_half(i):
+        slot = 2 * ((x + 3 + 2 * i) % 4) + c
+        here = gathered.at[slot, pl.ds(i * rows // 2, rows // 2), :]
+        return net.copy(halves + i, here, here, net.device(1 + 2 * i))
+
+    def passed(dx, slot):
+        return net.copy(over + dx, gathered.at[slot], gathered.at[slot], sibling)
+
+    @pl.loop(0, 3)
+    def _(k):
+        dx = order(k)
+        from_x = (x - dx + 4) % 4
+
+        @pl.when(k == 0)
+        def _():
+            for i in range(2):
+                token_send(i, gathered.at[me]).wait_recv()
+                token_half(i).start()
+
+        @pl.when(k == 1)
+        def _():
+            top_arrived()
+            for i in range(2):
+                top_copy(1 + 2 * i).start()
+
+        @pl.when(k == 2)
+        def _():
+            for i in range(2):
+                token_half(i).wait_recv()
+
+        passed(dx, 2 * from_x + c).start()
+        project(2 * from_x + c)
+        passed(dx, 2 * from_x + c).wait_recv()
+        project(2 * from_x + 1 - c)
+
     out_local.wait()
     for d in (1, 3, 2):
         out_copy(d).wait_recv()
     for d in (2, 1, 3):
         out_share(d).start()
     out_pass(0).start()
-    own_over.wait_recv()
-    project(2 * x + 1 - c)
-    top_arrived()
-    for d in (2, 1, 3):
-        top_copy(d).start()
-
-    @pl.when(c != zl)
-    def _():
-        down_cross.wait_recv()
-        for d in (2, 1, 3):
-            down_share(d).start()
-
-    over, halves = net.reserve(4), net.reserve(2)
-
-    def token_half(i):
-        slot = 2 * ((x + 3 + 2 * i) % 4) + c
-        here = gathered.at[slot, pl.ds(i * rows // 2, rows // 2), :]
-        return net.copy(halves + i, here, here, net.device(1 + 2 * i))
-
-    def passed(dx, slot):
-        return net.copy(over + dx, gathered.at[slot], gathered.at[slot], sibling)
-
-    @pl.loop(0, 3)
-    def _(k):
-        dx = order(k)
-        from_x = (x - dx + 4) % 4
-
-        @pl.when(k == 0)
-        def _():
-            for i in range(2):
-                token_send(i, gathered.at[me]).wait_recv()
-                token_half(i).start()
-
-        @pl.when(k == 2)
-        def _():
-            for i in range(2):
-                token_half(i).wait_recv()
-
-        passed(dx, 2 * from_x + c).start()
-        project(2 * from_x + c)
-        passed(dx, 2 * from_x + c).wait_recv()
-        project(2 * from_x + 1 - c)
-
     up_local.wait()
     for d in (1, 3, 2):
         up_copy(d).wait_recv()
@@ -425,6 +445,13 @@
         dx = step % 4
         to_x = (x + dx) % 4
 
+        @pl.when(step == 2)
+        def _():
+            for i in range(2):
+                top_copy(1 + 2 * i).wait_recv()
+                top_half(i).start()
+                top_pass(1 + 2 * i).start()
+
         @pl.when(step > 2)
         def _():
             keep_probs(to_x, step % 2).wait()
@@ -438,9 +465,9 @@
             mixed_send(dx, 0).start()
 
     attended[me] = mixed[me]
-    for d in (1, 3, 2):
-        top_copy(d).wait_recv()
-        top_pass(d).start()
+    for i in range(2):
+        top_half(i).wait_recv()
+    top_pass(2).start()
     for d in (1, 3, 2):
         out_share(d).wait_recv()
         out_pass(d).start()
@@ -453,8 +480,13 @@
         out_pass(d).wait()
     for d in (1, 2, 3):
         up_share(d).wait()
-        for copy in (cut_copy, cut_share, up_copy, top_copy, out_copy, out_share):
+        for copy in (cut_copy, up_copy, out_copy, out_share):
             copy(d).wait_send()
+    for i in range(2):
+        for copy in (cut_share, top_copy):
+            copy(1 + 2 * i).wait_send()
+        cut_on(i).wait_send()
+        top_half(i).wait_send()
 
     @pl.when(c == zl)
     def _():
@@ -776,18 +808,78 @@
     return pl.multiple_of(48 * index - 32 * (index // 3), 16)
 
 
-def column_flow(net, source, r1, s1, r2, s2, planes, landed, place_of):
+def beside(p, way):
+    return p + 1 - 2 * (p % 2) if way == 0 else 3 - p
+
+
+def halving(net, piece, r1, t1, r3):
+    x = net.x
+    b1, b2 = net.reserve(4), net.reserve(2)
+    both = [(half, slot) for slot in (1, 0) for half in range(2)]
+
+    def copy_1(half, slot):
+        near = beside(x, half)
+        wanted = near if slot == 0 else beside(near, 1 - half)
+        return net.copy(
+            b1 + 2 * half + slot, piece(half, wanted), r1.at[half, slot], net.device(near - x + 4)
+        )
+
+    def copy_2(half):
+        device = net.device(beside(x, 1 - half) - x + 4)
+        return net.copy(b2 + half, t1.at[half], r3.at[half], device)
+
+    def first():
+        for half, slot in both:
+            copy_1(half, slot).start()
+
+    def halfway(kept):
+        for half in range(2):
+            copy_1(half, 1).wait_recv()
+            t1[half] = (kept(half).astype(F32) + r1[half, 1].astype(F32)).astype(BF16)
+            copy_2(half).start()
+
+    def total(half):
+        copy_1(half, 0).wait_recv()
+        copy_2(half).wait_recv()
+        return r1[half, 0].astype(F32) + r3[half].astype(F32)
+
+    def sent():
+        for half, slot in both:
+            copy_1(half, slot).wait_send()
+        for half in range(2):
+            copy_2(half).wait_send()
+
+    return first, halfway, total, sent
+
+
+def column_flow(net, source, m1, r1, t1, r3, s1, r2, s2, planes, landed, place_of):
     y, z, x, c = net.y, 2 * net.zh + net.zl, net.x, net.c
     b1, b2, b3, b4, b5 = (net.reserve(4) for _ in range(5))
+    b6 = net.reserve(2)
     sibling = net.device(0, 1)
 
-    def copy_1(d):
-        rows = pl.ds(piece_start((y + d) % 4), 48)
-        return net.copy(b1 + d, source.at[:, rows, :], r1.at[d], net.device(dy=d))
-
-    mine = pltpu.make_async_copy(
-        source.at[:, pl.ds(piece_start(y), 48), :], r1.at[0], net.still.at[b1]
-    )
+    def piece(half, p):
+        return source.at[pl.ds(4 * half, 4), pl.ds(piece_start(p), 48), :]
+
+    def copy_1(half, slot):
+        near = beside(y, half)
+        wanted = near if slot == 0 else beside(near, 1 - half)
+        return net.copy(
+            b1 + 2 * half + slot,
+            piece(half, wanted),
+            r1.at[half, slot],
+            net.device(dy=near - y + 4),
+        )
+
+    def load(half, slot):
+        wanted = y if slot == 0 else beside(y, 1 - half)
+        return pltpu.make_async_copy(
+            piece(half, wanted), m1.at[half, slot], net.still.at[b1 + 2 * half + slot]
+        )
+
+    def copy_6(half):
+        device = net.device(dy=beside(y, 1 - half) - y + 4)
+        return net.copy(b6 + half, t1.at[half], r3.at[half], device)
 
     def copy_2(d):
         part = s1.at[pl.ds(2 * ((z + d) % 4), 2)]
@@ -804,19 +896,27 @@
         here = place_of(landed, 2 * ((x - d + 4) % 4) + c)
         return net.copy(b5 + d, here, here, sibling)
 
+    both = [(half, slot) for half in range(2) for slot in range(2)]
+
     def first():
-        mine.start()
-        for d in (2, 1, 3):
-            copy_1(d).start()
+        for half, slot in both:
+            copy_1(half, slot).start()
+        for half, slot in both:
+            load(half, slot).start()
+
+    def halfway():
+        for half, slot in both:
+            load(half, slot).wait()
+            copy_1(half, slot).wait_recv()
+        for half in range(2):
+            t1[half] = (m1[half, 1].astype(F32) + r1[half, 1].astype(F32)).astype(BF16)
+            copy_6(half).start()
 
     def second():
-        mine.wait()
-        for d in (1, 2, 3):
-            copy_1(d).wait_recv()
-        total = r1[0].astype(F32)
-        for d in (1, 2, 3):
-            total = total + r1[d].astype(F32)
-        s1[...] = total.astype(BF16)
+        for half in range(2):
+            copy_6(half).wait_recv()
+            total = m1[half, 0].astype(F32) + r1[half, 0].astype(F32) + r3[half].astype(F32)
+            s1[pl.ds(4 * half, 4)] = total.astype(BF16)
         for d in (2, 1, 3):
             copy_2(d).start()
 
@@ -849,10 +949,14 @@
         for d in range(4):
             copy_5(d).wait_send()
         for d in (1, 2, 3):
-            for copy in (copy_1, copy_2, copy_3, copy_4):
+            for copy in (copy_2, copy_3, copy_4):
                 copy(d).wait_send()
-
-    return first, second, third, fourth, fifth, sent
+        for half in range(2):
+            copy_6(half).wait_send()
+        for half, slot in both:
+            copy_1(half, slot).wait_send()
+
+    return first, halfway, second, third, fourth, fifth, sent
 
 
 def share_over_y(net, whole, final, half_of):
@@ -943,26 +1047,40 @@
     give,
     over,
     sums,
-    arrived,
-    out_arrived,
+    back_r1,
+    back_t1,
+    back_r3,
+    out_r1_x,
+    out_t1_x,
+    out_r3_x,
+    out_kept,
     final_rows,
     final_grad,
     low_grad,
+    up_m1,
     up_r1,
+    up_t1,
+    up_r3,
     up_s1,
     up_r2,
     up_s2,
     up_planes,
     up_landed,
     g_head_0,
+    m1_head_0,
     r1_head_0,
+    t1_head_0,
+    r3_head_0,
     s1_head_0,
     r2_head_0,
     s2_head_0,
     planes_head_0,
     landed_head_0,
     g_head_1,
+    m1_head_1,
     r1_head_1,
+    t1_head_1,
+    r3_head_1,
     s1_head_1,
     r2_head_1,
     s2_head_1,
@@ -1028,7 +1146,10 @@
     up = column_flow(
         net,
         g_up,
+        up_m1,
         up_r1,
+        up_t1,
+        up_r3,
         up_s1,
         up_r2,
         up_s2,
@@ -1037,8 +1158,30 @@
         lambda ref, hb: ref.at[:, pl.ds(pl.multiple_of(hb * 640, 128), 640)],
     )
     head_buffers = (
-        (g_head_0, r1_head_0, s1_head_0, r2_head_0, s2_head_0, planes_head_0, landed_head_0),
-        (g_head_1, r1_head_1, s1_head_1, r2_head_1, s2_head_1, planes_head_1, landed_head_1),
+        (
+            g_head_0,
+            m1_head_0,
+            r1_head_0,
+            t1_head_0,
+            r3_head_0,
+            s1_head_0,
+            r2_head_0,
+            s2_head_0,
+            planes_head_0,
+            landed_head_0,
+        ),
+        (
+            g_head_1,
+            m1_head_1,
+            r1_head_1,
+            t1_head_1,
+            r3_head_1,
+            s1_head_1,
+            r2_head_1,
+            s2_head_1,
+            planes_head_1,
+            landed_head_1,
+        ),
     )
     flows = [column_flow(net, *held, lambda ref, hb: ref.at[hb]) for held in head_buffers]
     up_share = share_over_y(
@@ -1101,7 +1244,8 @@
     def out_4(source_y):
         return net.copy(e4 + source_y, fin_out.at[source_y], fin_out.at[source_y], sibling)
 
-    near, pass_on, swap, add, out_add = (net.reserve(4) for _ in range(5))
+    near, pass_on, swap = (net.reserve(4) for _ in range(3))
+    branch_halves = net.reserve(2)
 
     def near_copy(dx):
         return net.copy(near + dx, branch, branch_all.at[aligned(me, rows)], net.device(dx))
@@ -1113,15 +1257,35 @@
     def swap_copy(dx, to_x):
         return net.copy(swap + dx, give.at[to_x], over.at[to_x], sibling)
 
-    def add_copy(dx, to_x):
-        return net.copy(add + dx, sums.at[to_x], arrived.at[dx], net.device(4 - dx))
-
-    def out_add_copy(dx):
-        to_x = (x - dx + 4) % 4
-        return net.copy(out_add + dx, out_sums.at[to_x], out_arrived.at[dx], net.device(4 - dx))
+    half_rows = rows // 2
+
+    def branch_half(i):
+        here = branch_all.at[aligned(2 * (2 * ((x + 3 + 2 * i) % 4) + c) + i, half_rows)]
+        return net.copy(branch_halves + i, here, here, net.device(1 + 2 * i))
+
+    def in_half(half):
+        return pl.ds(half_rows * half, half_rows)
+
+    back_sum = halving(
+        net, lambda half, p: sums.at[p, in_half(half)], back_r1, back_t1, back_r3
+    )
+    out_sum = halving(
+        net, lambda half, p: out_sums.at[p, in_half(half)], out_r1_x, out_t1_x, out_r3_x
+    )
+    out_load = [
+        pltpu.make_async_copy(
+            out_sums.at[beside(x, 1 - half), in_half(half)],
+            out_kept.at[half],
+            still.at[net.reserve(1)],
+        )
+        for half in range(2)
+    ]
+    for load in out_load:
+        load.start()
 
     wait()
-    for dx in (1, 3, 2):
+    out_sum[0]()
+    for dx in (1, 3):
         near_copy(dx).start()
     up[0]()
     down_mine.start()
@@ -1167,7 +1331,18 @@
             made = lax.dot_general(tall[:, cols], grads[h], TN, preferred_element_type=F32)
             head_buffers[h][0][pl.ds(4 * i, 4)] = made.astype(BF16).reshape(4, 160, 240)
 
+        if h == 0:
+            up[1]()
+            for load in out_load:
+                load.wait()
+            out_sum[1](lambda half: out_kept[half])
         flows[h][0]()
+        if h == 1:
+            flows[0][1]()
+            for i in range(2):
+                near_copy(1 + 2 * i).wait_recv()
+                branch_half(i).start()
+            up[2]()
 
     def back_rows(block):
         made = [
@@ -1185,6 +1360,9 @@
         give[to_x] = back_rows(2 * to_x + 1 - c).astype(BF16)
         swap_copy(dx, to_x).start()
 
+    flows[1][1]()
+    up[3]()
+
     @pl.loop(0, 4)
     def _(k):
         dx = jnp.where(k == 3, 0, order(k))
@@ -1196,19 +1374,21 @@
         @pl.when(dx != 0)
         def _():
             sums[to_x] = kept.astype(BF16)
-            add_copy(dx, to_x).start()
 
         @pl.when(dx == 0)
         def _():
             final_grad[...] = kept
 
+    back_sum[0]()
+    flows[0][2]()
     own_branch.wait()
     pass_copy(0).start()
-    for dx in (1, 3, 2):
-        near_copy(dx).wait_recv()
+    for dx in (1, 3):
         pass_copy(dx).start()
-
-    up[1]()
+    for i in range(2):
+        branch_half(i).wait_recv()
+    pass_copy(2).start()
+
     down_mine.wait()
     total = down_r1[0].astype(F32)
     for d in (1, 2, 3):
@@ -1241,9 +1421,9 @@
     )
     head_y_go()
 
-    for flow in flows:
-        flow[1]()
-    up[2]()
+    flows[1][2]()
+    up[4]()
+    back_sum[1](lambda half: sums[beside(x, 1 - half), in_half(half), :])
     total = down_s1[pl.ds(piece_start(y), 48), :].astype(F32)
     for d in (1, 2, 3):
         down_2(d).wait_recv()
@@ -1252,8 +1432,7 @@
     d3_go()
 
     for flow in flows:
-        flow[2]()
-    up[3]()
+        flow[3]()
     for d in (1, 2, 3):
         net.copy(d3 + d, down_l3.at[y], down_l3.at[y], net.device(dy=d)).wait_recv()
     for i in range(3):
@@ -1269,14 +1448,15 @@
     def _():
         down_local.start()
 
-    up[4]()
+    up[5]()
     up_share[0]()
     for flow in flows:
-        flow[3]()
-    grad_first = final_grad[...]
-    for dx in (1, 3, 2):
-        add_copy(dx, (x - dx + 4) % 4).wait_recv()
-        grad_first = grad_first + arrived[dx].astype(F32)
+        flow[4]()
+    total = result[...] + jnp.concatenate([out_sum[2](half) for half in range(2)])
+    final_rows[...] = total.astype(BF16)
+    output_arrived, output_left = net.cross(final_rows, output)
+
+    grad_first = final_grad[...] + jnp.concatenate([back_sum[2](half) for half in range(2)])
     values = own[...].astype(F32)
     center = values - jnp.mean(values, axis=-1, keepdims=True)
     inverse = lax.rsqrt(jnp.mean(center * center, axis=-1, keepdims=True) + EPS)
@@ -1310,15 +1490,13 @@
         vec_copy(dx, dc).start()
     vec_1[me] = vec_cut[x]
 
-    for dx in (1, 3, 2):
-        out_add_copy(dx).start()
     for flow in flows:
-        flow[4]()
+        flow[5]()
     for block in range(8):
         cols = slice(160 * block, 160 * block + 160)
         for k in range(3):
             qkv_rows[k, :, cols] = jnp.concatenate(
-                [held[6][block, :, 80 * k : 80 * k + 80] for held in head_buffers], axis=1
+                [held[9][block, :, 80 * k : 80 * k + 80] for held in head_buffers], axis=1
             )
     three_share[0]()
     total = g_out[pl.ds(piece_start(y), 48), :].astype(F32)
@@ -1378,12 +1556,6 @@
             out_3(d).wait_recv()
             out_4((y + 4 - d) % 4).start()
 
-    total = result[...]
-    for dx in (1, 3, 2):
-        out_add_copy(dx).wait_recv()
-        total = total + out_arrived[dx].astype(F32)
-    final_rows[...] = total.astype(BF16)
-    output_arrived, output_left = net.cross(final_rows, output)
 
     up_share[1]()
     three_share[1]()
@@ -1417,18 +1589,20 @@
     grad_left()
     output_arrived()
     output_left()
-    for done in (up[5], flows[0][5], flows[1][5], d3_sent, out_sent, head_y_sent, head_z_sent, vec_y_sent):
+    for done in (up[6], flows[0][6], flows[1][6], d3_sent, out_sent, head_y_sent, head_z_sent, vec_y_sent):
         done()
     for d in (1, 2, 3):
         down_1(d).wait_send()
         down_2(d).wait_send()
         out_1(d).wait_send()
         vec_z(d).wait_send()
-        near_copy(d).wait_send()
-        add_copy(d, (x - d + 4) % 4).wait_send()
-        out_add_copy(d).wait_send()
     for d in range(4):
         swap_copy(d, (x - d + 4) % 4).wait_send()
+    for i in range(2):
+        near_copy(1 + 2 * i).wait_send()
+        branch_half(i).wait_send()
+    back_sum[3]()
+    out_sum[3]()
     for dx, dc in others:
         vec_copy(dx, dc).wait_send()
     net.all_sent()
@@ -1462,7 +1636,10 @@
 
     def column_buffers(columns):
         return [
-            buffer(4, 8, 48, columns),
+            buffer(2, 2, 4, 48, columns),
+            buffer(2, 2, 4, 48, columns),
+            buffer(2, 4, 48, columns),
+            buffer(2, 4, 48, columns),
             buffer(8, 48, columns),
             buffer(4, 2, 48, columns),
             buffer(2, 48, columns),
@@ -1493,8 +1670,13 @@
             buffer(4, rows, width),
             buffer(4, rows, width),
             buffer(4, rows, width),
-            buffer(4, rows, width),
-            buffer(4, rows, width),
+            buffer(2, 2, rows // 2, width),
+            buffer(2, rows // 2, width),
+            buffer(2, rows // 2, width),
+            buffer(2, 2, rows // 2, width),
+            buffer(2, rows // 2, width),
+            buffer(2, rows // 2, width),
+            buffer(2, rows // 2, width),
             buffer(rows, width),
             buffer(rows, width, dtype=F32),
             buffer(rows, width),

time: 281 us -> 270 us (0.961); the launches traced: 276 us -> 268 us
  Pallas kernels: 271 us -> 263 us
    pallas_call x1, Pallas kernels: 92.4 us -> 81.4 us  [begin(): pl.pallas_call(begin_kernel, in_specs=[VMEM] * 11, out_specs=[HBM] * 3 +...]
    pallas_call x1, Pallas kernels: 102 us -> 106 us  [finish(): pl.pallas_call(finish_kernel, in_specs=[VMEM] * 11 + [HBM] * 5, out_specs...]
where the time goes in v6:
time: 270 us; the launch traced here: 268 us
  Pallas kernels  263 us (97%)
    pallas_call x1, Pallas kernels, finish(): pl.pallas_call(finish_kernel, in_specs=[VMEM] * 11 + [HBM] * 5, out_specs...  106 us
    pallas_call x1, Pallas kernels, begin(): pl.pallas_call(begin_kernel, in_specs=[VMEM] * 11, out_specs=[HBM] * 3 +...  81.4 us
    pallas_call x1, Pallas kernels, middle_part(): pl.pallas_call(middle_kernel, in_specs=[VMEM] * 9, out_specs=[VMEM] * 9,...  68.8 us
    pallas_call x1, Pallas kernels, widen(): pl.pallas_call(widen_kernel, in_specs=[VMEM] * 2 + [HBM] * 6, out_specs=[...  7.4 us

profile of v6, /device:TPU:0, one launch (start us, length us, event | category | flops | bytes accessed | tf_op | source)
XLA Modules:
  0.0 268.1 jit_solution(16434611788939234319)
XLA Ops:
  1.3 0.6 broadcast_in_dim.79.length
  1.9 1.5 select_select_fusion.small
  3.4 1.3 broadcast_in_dim.78.up_bias
  4.7 81.4 %shard_map.305 = (bf16[8,192,1280]{2,1,0:T(8,128)(2,1)}, bf16[6,1536,80]{2,1,0:T(8,128)(2,1)}, bf16[2,1536,1536]{2,1,0:T(8,128)(2,1)}, bf16[8,192,160]{2,1,0:T(8...) custom-call(bf16[192,1280]{1,0:T(8,128)(2,1)} %bitcast.17, ...), custom_call_target="tpu_custom_call" | custom-call | tf_op jit(solution)/shard_map/pallas_call | solution.py:522
  86.1 68.8 %shard_map.306 = (f32[192,1280]{1,0:T(8,128)}, f32[192,1280]{1,0:T(8,128)}, bf16[192,1280]{1,0:T(8,128)(2,1)}, bf16[4,192,1280]{2,1,0:T(8,128)(2,1)}, bf16[1280,...) custom-call(bf16[8,192,160]{2,1,0:T(8,128)(2,1)} %get-tuple-element., ...), custom_call_target="tpu_custom_call" | custom-call | tf_op jit(solution)/shard_map/pallas_call | solution.py:769
  154.9 105.6 %shard_map.307 = (f32[8,640]{1,0:T(8,128)}, f32[8,160]{1,0:T(8,128)}, bf16[192,1280]{1,0:T(8,128)(2,1)}, bf16[192,1280]{1,0:T(8,128)(2,1)}, bf16[4,48,5120]{2,1,...) custom-call(bf16[6,1536,80]{2,1,0:T(8,128)(2,1)} %get-tuple-element., ...), custom_call_target="tpu_custom_call" | custom-call | tf_op jit(solution)/shard_map/pallas_call | solution.py:1649
  260.5 7.4 %shard_map.308 = (f32[160,5120]{1,0:T(8,128)}, f32[160,1280]{1,0:T(8,128)}, f32[160,1280]{1,0:T(8,128)}, f32[160,1280]{1,0:T(8,128)}, f32[640,1280]{1,0:T(8,128)...) custom-call(f32[8,640]{1,0:T(8,128)} %get-tuple-element.88.hb, ...), custom_call_target="tpu_custom_call" | custom-call | tf_op jit(solution)/shard_map/pallas_call | solution.py:1787
  (4 shorter events, 0.0 us)

commit v7 on v6

--- a/solution.py
+++ b/solution.py
@@ -1353,6 +1353,18 @@
         ]
         return made[0] + made[1]
 
+    head_y[y] = jnp.zeros((8, 640), F32)
+    head_y[y, 0:1, :] = g_up_bias[...]
+    for h in range(2):
+        cols = slice(h * HD, (h + 1) * HD)
+        column_sums = jnp.sum(grads[h].astype(F32), axis=0, keepdims=True)
+        head_y[y, 1:2, cols] = column_sums[:, :80]
+        head_y[y, 2:3, cols] = column_sums[:, 160:]
+    head_y_go, head_y_total, head_y_sent = four_way(
+        net, net.reserve(4), head_y, y, lambda d: net.device(dy=d)
+    )
+    head_y_go()
+
     @pl.loop(0, 4)
     def _(k):
         dx = jnp.where(k == 3, 0, order(k))
@@ -1362,6 +1374,15 @@
 
     flows[1][1]()
     up[3]()
+    down_mine.wait()
+    total = down_r1[0].astype(F32)
+    for d in (1, 2, 3):
+        down_1(d).wait_recv()
+        total = total + down_r1[d].astype(F32)
+    down_s1[...] = total.astype(BF16)
+    for d in (2, 1, 3):
+        down_2(d).start()
+
 
     @pl.loop(0, 4)
     def _(k):
@@ -1389,14 +1410,19 @@
         branch_half(i).wait_recv()
     pass_copy(2).start()
 
-    down_mine.wait()
-    total = down_r1[0].astype(F32)
+    head_z[z] = head_y_total()
+    head_z_go, head_z_total, head_z_sent = four_way(
+        net, net.reserve(4), head_z, z, lambda d: net.device(dz=d)
+    )
+    head_z_go()
+    flows[1][2]()
+    up[4]()
+    total = down_s1[pl.ds(piece_start(y), 48), :].astype(F32)
     for d in (1, 2, 3):
-        down_1(d).wait_recv()
-        total = total + down_r1[d].astype(F32)
-    down_s1[...] = total.astype(BF16)
-    for d in (2, 1, 3):
-        down_2(d).start()
+        down_2(d).wait_recv()
+        total = total + down_r2[d].astype(F32)
+    down_l3[y] = total.astype(BF16)
+    d3_go()
 
     for dx in range(4):
         pass_copy(dx).wait_recv()
@@ -1409,30 +1435,10 @@
     for d in (2, 1, 3):
         out_1(d).start()
 
-    head_y[y] = jnp.zeros((8, 640), F32)
-    head_y[y, 0:1, :] = g_up_bias[...]
-    for h in range(2):
-        cols = slice(h * HD, (h + 1) * HD)
-        column_sums = jnp.sum(grads[h].astype(F32), axis=0, keepdims=True)
-        head_y[y, 1:2, cols] = column_sums[:, :80]
-        head_y[y, 2:3, cols] = column_sums[:, 160:]
-    head_y_go, head_y_total, head_y_sent = four_way(
-        net, net.reserve(4), head_y, y, lambda d: net.device(dy=d)
-    )
-    head_y_go()
-
-    flows[1][2]()
-    up[4]()
     back_sum[1](lambda half: sums[beside(x, 1 - half), in_half(half), :])
-    total = down_s1[pl.ds(piece_start(y), 48), :].astype(F32)
-    for d in (1, 2, 3):
-        down_2(d).wait_recv()
-        total = total + down_r2[d].astype(F32)
-    down_l3[y] = total.astype(BF16)
-    d3_go()
-
     for flow in flows:
         flow[3]()
+    up[5]()
     for d in (1, 2, 3):
         net.copy(d3 + d, down_l3.at[y], down_l3.at[y], net.device(dy=d)).wait_recv()
     for i in range(3):
@@ -1448,14 +1454,21 @@
     def _():
         down_local.start()
 
-    up[5]()
-    up_share[0]()
+    total = g_out[pl.ds(piece_start(y), 48), :].astype(F32)
+    for d in (1, 2, 3):
+        out_1(d).wait_recv()
+        total = total + out_r1[d].astype(F32)
+    out_z[z] = total.astype(BF16)
+    out_go()
     for flow in flows:
         flow[4]()
+    up_share[0]()
     total = result[...] + jnp.concatenate([out_sum[2](half) for half in range(2)])
     final_rows[...] = total.astype(BF16)
     output_arrived, output_left = net.cross(final_rows, output)
 
+    head_sib[0] = head_z_total()
+    head_copy = net.go(head_sib.at[0], head_sib.at[1], sibling)
     grad_first = final_grad[...] + jnp.concatenate([back_sum[2](half) for half in range(2)])
     values = own[...].astype(F32)
     center = values - jnp.mean(values, axis=-1, keepdims=True)
@@ -1499,17 +1512,14 @@
                 [held[9][block, :, 80 * k : 80 * k + 80] for held in head_buffers], axis=1
             )
     three_share[0]()
-    total = g_out[pl.ds(piece_start(y), 48), :].astype(F32)
-    for d in (1, 2, 3):
-        out_1(d).wait_recv()
-        total = total + out_r1[d].astype(F32)
-    out_z[z] = total.astype(BF16)
-    out_go()
-    head_z[z] = head_y_total()
-    head_z_go, head_z_total, head_z_sent = four_way(
-        net, net.reserve(4), head_z, z, lambda d: net.device(dz=d)
-    )
-    head_z_go()
+    out_t[...] = out_total().astype(BF16)
+
+    @pl.when(c == zl)
+    def _():
+        out_local.start()
+        for d in (2, 1, 3):
+            out_3(d).start()
+
     for dx, dc in others:
         vec_copy(dx, dc).wait_recv()
     total = vec_1[0]
@@ -1524,24 +1534,6 @@
     for d in (2, 1, 3):
         vec_z(d).start()
     vec_2[z] = vec_1s[zl]
-    out_t[...] = out_total().astype(BF16)
-
-    @pl.when(c == zl)
-    def _():
-        out_local.start()
-        for d in (2, 1, 3):
-            out_3(d).start()
-
-    head_sib[0] = head_z_total()
-    head_copy = net.go(head_sib.at[0], head_sib.at[1], sibling)
-    for d in (1, 2, 3):
-        vec_z(d).wait_recv()
-    vec_3[y] = (vec_2[0] + vec_2[1]) + (vec_2[2] + vec_2[3])
-    vec_y_go, vec_y_total, vec_y_sent = four_way(
-        net, net.reserve(4), vec_3, y, lambda d: net.device(dy=d)
-    )
-    vec_y_go()
-
     @pl.when(c == zl)
     def _():
         down_local.wait()
@@ -1550,6 +1542,17 @@
             source_z = (z + d) % 4
             down_4(0, source_z).wait_recv()
             down_5(source_z).start()
+
+    for d in (1, 2, 3):
+        vec_z(d).wait_recv()
+    vec_3[y] = (vec_2[0] + vec_2[1]) + (vec_2[2] + vec_2[3])
+    vec_y_go, vec_y_total, vec_y_sent = four_way(
+        net, net.reserve(4), vec_3, y, lambda d: net.device(dy=d)
+    )
+    vec_y_go()
+
+    @pl.when(c == zl)
+    def _():
         out_local.wait()
         out_4(y).start()
         for d in (1, 2, 3):

time: 270 us -> 260 us (0.963)
  Pallas kernels: 263 us -> 254 us
    pallas_call x1, Pallas kernels: 106 us -> 96.1 us  [finish(): pl.pallas_call(finish_kernel, in_specs=[VMEM] * 11 + [HBM] * 5, out_specs...]
where the time goes in v7:
time: 260 us; the launch traced here: 259 us
  Pallas kernels  254 us (98%)
    pallas_call x1, Pallas kernels, finish(): pl.pallas_call(finish_kernel, in_specs=[VMEM] * 11 + [HBM] * 5, out_specs...  96.1 us
    pallas_call x1, Pallas kernels, begin(): pl.pallas_call(begin_kernel, in_specs=[VMEM] * 11, out_specs=[HBM] * 3 +...  81.4 us
    pallas_call x1, Pallas kernels, middle_part(): pl.pallas_call(middle_kernel, in_specs=[VMEM] * 9, out_specs=[VMEM] * 9,...  68.8 us
    pallas_call x1, Pallas kernels, widen(): pl.pallas_call(widen_kernel, in_specs=[VMEM] * 2 + [HBM] * 6, out_specs=[...  7.4 us

profile of v7, /device:TPU:0, one launch (start us, length us, event | category | flops | bytes accessed | tf_op | source)
XLA Modules:
  0.0 258.6 jit_solution(14280612538701055151)
XLA Ops:
  1.3 0.6 broadcast_in_dim.79.length
  1.9 1.5 select_select_fusion.small
  3.4 1.3 broadcast_in_dim.78.up_bias
  4.7 81.4 %shard_map.305 = (bf16[8,192,1280]{2,1,0:T(8,128)(2,1)}, bf16[6,1536,80]{2,1,0:T(8,128)(2,1)}, bf16[2,1536,1536]{2,1,0:T(8,128)(2,1)}, bf16[8,192,160]{2,1,0:T(8...) custom-call(bf16[192,1280]{1,0:T(8,128)(2,1)} %bitcast.17, ...), custom_call_target="tpu_custom_call" | custom-call | tf_op jit(solution)/shard_map/pallas_call | solution.py:522
  86.1 68.8 %shard_map.306 = (f32[192,1280]{1,0:T(8,128)}, f32[192,1280]{1,0:T(8,128)}, bf16[192,1280]{1,0:T(8,128)(2,1)}, bf16[4,192,1280]{2,1,0:T(8,128)(2,1)}, bf16[1280,...) custom-call(bf16[8,192,160]{2,1,0:T(8,128)(2,1)} %get-tuple-element., ...), custom_call_target="tpu_custom_call" | custom-call | tf_op jit(solution)/shard_map/pallas_call | solution.py:769
  154.9 96.1 %shard_map.307 = (f32[8,640]{1,0:T(8,128)}, f32[8,160]{1,0:T(8,128)}, bf16[192,1280]{1,0:T(8,128)(2,1)}, bf16[192,1280]{1,0:T(8,128)(2,1)}, bf16[4,48,5120]{2,1,...) custom-call(bf16[6,1536,80]{2,1,0:T(8,128)(2,1)} %get-tuple-element., ...), custom_call_target="tpu_custom_call" | custom-call | tf_op jit(solution)/shard_map/pallas_call | solution.py:1652
  251.1 7.4 %shard_map.308 = (f32[160,5120]{1,0:T(8,128)}, f32[160,1280]{1,0:T(8,128)}, f32[160,1280]{1,0:T(8,128)}, f32[160,1280]{1,0:T(8,128)}, f32[640,1280]{1,0:T(8,128)...) custom-call(f32[8,640]{1,0:T(8,128)} %get-tuple-element.88.hb, ...), custom_call_target="tpu_custom_call" | custom-call | tf_op jit(solution)/shard_map/pallas_call | solution.py:1790
  (4 shorter events, 0.0 us)

commit v8 on v7

--- a/solution.py
+++ b/solution.py
@@ -380,23 +380,23 @@
         def _():
             for i in range(2):
                 token_half(i).wait_recv()
+            out_local.wait()
+            for d in (1, 3, 2):
+                out_copy(d).wait_recv()
+            for d in (2, 1, 3):
+                out_share(d).start()
+            out_pass(0).start()
+            up_local.wait()
+            for d in (1, 3, 2):
+                up_copy(d).wait_recv()
+            for d in (2, 1, 3):
+                up_share(d).start()
 
         passed(dx, 2 * from_x + c).start()
         project(2 * from_x + c)
         passed(dx, 2 * from_x + c).wait_recv()
         project(2 * from_x + 1 - c)
 
-    out_local.wait()
-    for d in (1, 3, 2):
-        out_copy(d).wait_recv()
-    for d in (2, 1, 3):
-        out_share(d).start()
-    out_pass(0).start()
-    up_local.wait()
-    for d in (1, 3, 2):
-        up_copy(d).wait_recv()
-    for d in (2, 1, 3):
-        up_share(d).start()
     top_pass(0).start()
 
     keep_h1 = pltpu.make_async_copy(normed_rows, h1, still.at[net.reserve(1)])

time: 260 us -> 260 us (level)
  no operation moved by 1% of the time
where the time goes in v8:
time: 260 us; the launch traced here: 259 us
  Pallas kernels  254 us (98%)
    pallas_call x1, Pallas kernels, finish(): pl.pallas_call(finish_kernel, in_specs=[VMEM] * 11 + [HBM] * 5, out_specs...  96.1 us
    pallas_call x1, Pallas kernels, begin(): pl.pallas_call(begin_kernel, in_specs=[VMEM] * 11, out_specs=[HBM] * 3 +...  81.4 us
    pallas_call x1, Pallas kernels, middle_part(): pl.pallas_call(middle_kernel, in_specs=[VMEM] * 9, out_specs=[VMEM] * 9,...  68.8 us
    pallas_call x1, Pallas kernels, widen(): pl.pallas_call(widen_kernel, in_specs=[VMEM] * 2 + [HBM] * 6, out_specs=[...  7.4 us

profile of v8, /device:TPU:0, one launch (start us, length us, event | category | flops | bytes accessed | tf_op | source)
XLA Modules:
  0.0 258.6 jit_solution(3231798692994796220)
XLA Ops:
  1.3 0.6 broadcast_in_dim.79.length
  1.9 1.5 select_select_fusion.small
  3.4 1.3 broadcast_in_dim.78.up_bias
  4.7 81.4 %shard_map.305 = (bf16[8,192,1280]{2,1,0:T(8,128)(2,1)}, bf16[6,1536,80]{2,1,0:T(8,128)(2,1)}, bf16[2,1536,1536]{2,1,0:T(8,128)(2,1)}, bf16[8,192,160]{2,1,0:T(8...) custom-call(bf16[192,1280]{1,0:T(8,128)(2,1)} %bitcast.17, ...), custom_call_target="tpu_custom_call" | custom-call | tf_op jit(solution)/shard_map/pallas_call | solution.py:522
  86.1 68.8 %shard_map.306 = (f32[192,1280]{1,0:T(8,128)}, f32[192,1280]{1,0:T(8,128)}, bf16[192,1280]{1,0:T(8,128)(2,1)}, bf16[4,192,1280]{2,1,0:T(8,128)(2,1)}, bf16[1280,...) custom-call(bf16[8,192,160]{2,1,0:T(8,128)(2,1)} %get-tuple-element., ...), custom_call_target="tpu_custom_call" | custom-call | tf_op jit(solution)/shard_map/pallas_call | solution.py:769
  154.9 96.1 %shard_map.307 = (f32[8,640]{1,0:T(8,128)}, f32[8,160]{1,0:T(8,128)}, bf16[192,1280]{1,0:T(8,128)(2,1)}, bf16[192,1280]{1,0:T(8,128)(2,1)}, bf16[4,48,5120]{2,1,...) custom-call(bf16[6,1536,80]{2,1,0:T(8,128)(2,1)} %get-tuple-element., ...), custom_call_target="tpu_custom_call" | custom-call | tf_op jit(solution)/shard_map/pallas_call | solution.py:1652
  251.1 7.4 %shard_map.308 = (f32[160,5120]{1,0:T(8,128)}, f32[160,1280]{1,0:T(8,128)}, f32[160,1280]{1,0:T(8,128)}, f32[160,1280]{1,0:T(8,128)}, f32[640,1280]{1,0:T(8,128)...) custom-call(f32[8,640]{1,0:T(8,128)} %get-tuple-element.88.hb, ...), custom_call_target="tpu_custom_call" | custom-call | tf_op jit(solution)/shard_map/pallas_call | solution.py:1790
  (4 shorter events, 0.0 us)
